TPU v7x, 128 devices: a whole 4x4x4 slice. The times are simulated.
128 devices in a mesh: star: 8 (over y, core), tm: 16 (over x, z).
Axes of the slice: x: 4, y: 4, z: 4, core: 2. Of those that a mesh axis runs over, the one named last changes fastest.
Arguments:
- flux: float32 [16384, 8192], P('star', 'tm'), may hold values from -6 to 6
- valid: int32 [16384, 8192], P('star', 'tm'), may hold values 0 or 1
- quality: int32 [16384, 8192], P('star', 'tm'), may hold values from 0 to 3
- basis: float32 [16, 8192], P(None, 'tm'), may hold values from -0.0625 to 0.0625
- neighbours: int32 [16384, 64], P('star'), may hold values from 0 to 16383
- prior_prec: float32 [16], replicated, may hold values from 0.3 to 3
- decay: float32 [16, 8192], P(None, 'tm'), may hold values from 0.3 to 1, as said below
- load_u: float32 [16, 8192], P(None, 'tm'), may hold values from -1.5 to 1.5
- feed_w: float32 [16, 8192], P(None, 'tm'), may hold values from -0.0625 to 0.0625
- inv_diag: float32 [8192], P('tm'), may hold values from 0.25 to 1.75
Outputs:
- map_coeffs: float32 [16384, 16], P('star')
- whitened: float32 [16384, 8192], P('star', 'tm')
Inputs may be any that keep to these rules, and one draw needn't show every extreme that they name: `decay`: each factor is positive and at most 1.
All inputs are finite; a program needn't handle non-finite values. No bound on the sum of `valid` on one device may be relied on, other than what follows from the above.
Results may differ from a plain program's by a relative error of at most 0.00011.
Values sent between devices are 32-bit elements; how exact they have to be, the bound alone decides.
No kernel may reach another device: no remote copies, remote signals or barrier semaphores. Data moves between devices by JAX's collectives and lax.ppermute only.
A program may use at most 256 MiB of HBM per device.

v0:
```python
import jax
import jax.numpy as jnp
from jax import lax
from jax.sharding import PartitionSpec as P

BASIS_VECTORS = 16
NOISE_TERMS = 16


HIGHEST = lax.Precision.HIGHEST


def carried_in(part, axis, combine, identity):
    place = lax.axis_index(axis)
    gathered = jax.tree.map(lambda a: lax.all_gather(a, axis), part)
    state = jax.tree.map(lambda a, e: jnp.zeros_like(a) + jnp.asarray(e, a.dtype), part, identity)

    def one(step, state):
        return combine(
            state, jax.tree.map(lambda a: lax.dynamic_index_in_dim(a, step, 0, False), gathered)
        )

    return lax.fori_loop(0, place, one, state)


def spd_solve(matrix, vector):
    order = matrix.shape[0]
    factor = [[None] * order for index in range(order)]
    for column in range(order):
        pivot = matrix[column, column]
        for inner in range(column):
            pivot = pivot - factor[column][inner] * factor[column][inner]
        root_value = jnp.sqrt(pivot)
        factor[column][column] = root_value
        for row_index in range(column + 1, order):
            entry = matrix[row_index, column]
            for inner in range(column):
                entry = entry - factor[row_index][inner] * factor[column][inner]
            factor[row_index][column] = entry / root_value
    forward = []
    for row_index in range(order):
        entry = vector[row_index]
        for inner in range(row_index):
            entry = entry - factor[row_index][inner] * forward[inner]
        forward.append(entry / factor[row_index][row_index])
    backward = [None] * order
    for row_index in range(order - 1, -1, -1):
        entry = forward[row_index]
        for inner in range(row_index + 1, order):
            entry = entry - factor[inner][row_index] * backward[inner]
        backward[row_index] = entry / factor[row_index][row_index]
    return jnp.stack(backward, axis=0)


def solve_rows(gram_sums, right_sums, ridge):
    matrices = gram_sums.reshape(BASIS_VECTORS, BASIS_VECTORS, gram_sums.shape[1])
    ridge_block = ridge[:, None] * jnp.eye(BASIS_VECTORS, dtype=jnp.float32)
    return spd_solve(matrices + ridge_block[:, :, None], right_sums)


def neighbour_mean(coeff_table, listed):
    return jnp.mean(jnp.take(coeff_table, listed, axis=1), axis=2)


def combine(earlier, later):
    return (earlier[0] * later[0], earlier[1] * later[0][None, :] + later[1])


def per_device(
    flux, valid, quality, basis, neighbours, prior_prec, decay, load_u, feed_w, inv_diag
):
    valid_f = valid.astype(jnp.float32)
    weight = valid_f / (1.0 + quality.astype(jnp.float32))
    cadence_times = flux.shape[1]
    paired_rows = (basis[:, None, :] * basis[None, :, :]).reshape(
        BASIS_VECTORS * BASIS_VECTORS, cadence_times
    )
    gram_part = lax.dot_general(paired_rows, weight, (((1,), (1,)), ((), ())), precision=HIGHEST)
    right_part = lax.dot_general(basis, weight * flux, (((1,), (1,)), ((), ())), precision=HIGHEST)
    ridge_lsq = jnp.full((BASIS_VECTORS,), 0.1, jnp.float32)
    gram_sums, right_sums = lax.psum((gram_part, right_part), "tm")
    fitted = solve_rows(gram_sums, right_sums, ridge_lsq)
    coeff_table = lax.all_gather(fitted, "star", axis=1, tiled=True)
    prior_mean = neighbour_mean(coeff_table, neighbours)
    map_rows = solve_rows(gram_sums, right_sums + prior_prec[:, None] * prior_mean, prior_prec)
    trend = lax.dot_general(map_rows, basis, (((0,), (0,)), ((), ())), precision=HIGHEST)
    residual = valid_f * (flux - trend)
    log_decay = jnp.log(decay)
    cadence_position = jnp.arange(cadence_times)
    upper_ones = (cadence_position[:, None] <= cadence_position[None, :]).astype(jnp.float32)
    through = jnp.dot(log_decay, upper_ones, precision=HIGHEST)
    before = through - log_decay
    group_log = through[:, -1]
    strictly_lower = (cadence_position[:, None] > cadence_position[None, :])[None, :, :]
    exponent = jnp.where(strictly_lower, before[:, :, None] - through[:, None, :], 0.0)
    kernel_terms = jnp.where(strictly_lower, jnp.exp(exponent), 0.0)
    kernel_sum = jnp.einsum("jt,jtu,ju->tu", load_u, kernel_terms, feed_w, precision=HIGHEST)
    local_part = lax.dot_general(residual, kernel_sum, (((1,), (1,)), ((), ())), precision=HIGHEST)
    carry_feed = jnp.exp(group_log[:, None] - through) * feed_w
    carry_local = lax.dot_general(residual, carry_feed, (((1,), (1,)), ((), ())), precision=HIGHEST)
    group_decay = jnp.exp(group_log)
    identity = (jnp.ones((NOISE_TERMS,), jnp.float32), jnp.zeros(carry_local.shape, jnp.float32))
    ignored, state_in = carried_in((group_decay, carry_local), "tm", combine, identity)
    entry_load = load_u * jnp.exp(before)
    incoming = jnp.dot(state_in, entry_load, precision=HIGHEST)
    whitened = (residual - local_part - incoming) * inv_diag[None, :]
    return (map_rows.T, whitened)


def solution(mesh):
    in_specs = (
        P("star", "tm"),
        P("star", "tm"),
        P("star", "tm"),
        P(None, "tm"),
        P("star", None),
        P(),
        P(None, "tm"),
        P(None, "tm"),
        P(None, "tm"),
        P("tm"),
    )
    out_specs = (P("star", None), P("star", "tm"))
    return jax.shard_map(
        per_device, mesh=mesh, in_specs=in_specs, out_specs=out_specs, check_vma=False
    )
```

profile of v0, /device:TPU:0, one launch (start us, length us, event | category | flops | bytes accessed | tf_op | source)
XLA Modules:
  0.0 753.4 jit_solution(13524107405663141630)
XLA Ops:
  8.2 8.1 %fusion.759 = f32[256,2048]{1,0:T(8,128)} fusion(f32[256,512]{1,0:T(8,128)S(1)} %bitcast.3366, s32[2048,512]{1,0:T(8,128)} %param.14, s32[2048,512]{1,0:T(8,128)} %param.13), kind=kOutput, calls=%fused_computation.1677 | convolution fusion | flops 3225419776 | bytes 11010048 | tf_op jit(solution)/shard_map/dot_general | solution.py:78
  16.3 5.2 fusion.5
  26.3 88.8 %all-reduce.4.cloned.1.call-done = (f32[16,16,2048]{2,1,0:T(8,128)}, f32[16,2048]{1,0:T(8,128)}) async-done(((f32[16,16,2048]{2,1,0:T(8,128)}, f32[16,2048]{1,0:T(8,128)}), (f32[16,16,2048]{2,1,0:T(8,128)}, f32[16,2048]{1,0:T(8,128)})) %all-reduce.4.cloned.1.call-update) | async-done | bytes 2228240 | tf_op jit(solution)/shard_map/psum | solution.py:81
  115.1 2.0 broadcast_add_fusion.1
  134.6 3.9 subtract_divide_fusion.156
  153.5 11.1 %all-gather.5.cloned.1.call-done = f32[16,16384]{1,0:T(8,128)} async-done(((f32[16,2048]{1,0:T(8,128)}), f32[16,16384]{1,0:T(8,128)}) %all-gather.5.cloned.1.call-update) | async-done | bytes 1048592 | tf_op jit(solution)/shard_map/all_gather | solution.py:83
  164.6 6.1 copy.21
  170.7 436.7 %gather_fusion = f32[131072,16]{1,0:T(8,128)} fusion(f32[16,16384]{0,1:T(8,128)} %copy.21, s32[131072]{0:T(1024)S(1)} %broadcast_clamp_fusion), kind=kCustom, calls=%fused_computation | custom fusion | bytes 17301504 | tf_op jit(solution)/shard_map/jit(_take)/gather | solution.py:62
  607.4 25.0 %select_reduce_fusion = f32[2048,16]{1,0:T(8,128)S(1)} fusion(pred[2048,64]{1,0:T(8,128)(4,1)} %copy.19, f32[131072,16]{1,0:T(8,128)} %gather_fusion), kind=kLoop, calls=%fused_computation.5 | loop fusion | flops 4161536 | bytes 8650752 | tf_op jit(solution)/shard_map/reduce_sum | solution.py:62
  634.0 3.0 subtract_divide_fusion.36
  637.0 2.0 subtract_divide_fusion.38
  641.6 2.0 subtract_divide_fusion.26
  643.6 1.9 subtract_divide_fusion.24
  645.5 4.8 subtract_divide_fusion.12
  652.1 2.3 subtract_divide_fusion
  655.4 6.5 subtract_multiply_fusion.1
  662.0 2.0 copy-done
  664.0 4.3 fusion.13
  669.8 40.6 %all-reduce = f32[256]{0:T(256)S(1)} all-reduce(f32[256]{0:T(256)S(1)} %dynamic-update-slice), channel_id=2, replica_groups=mesh['star'=8,'tm'=16] {'tm'}, use_global_device_ids=true, to_apply=%add | all-reduce | flops 256 | bytes 2048
  710.7 4.0 multiply_bitcast_fusion
  714.7 16.3 %fusion.1 = f32[512,1,512]{2,1,0:T(1,128)S(1)} fusion(f32[16,512,1]{0,2,1:T(1,128)S(1)} %copy.25, f32[16,512,512]{1,2,0:T(8,128)S(1)} %multiply_bitcast_fusion), kind=kOutput, calls=%fused_computation.6 | convolution fusion | flops 50331648 | bytes 17858560 | tf_op jit(solution)/shard_map/jt,jtu,ju->tu/dot_general | solution.py:97
  731.1 2.8 copy.28
  734.2 3.5 fusion.10
  737.7 8.7 %subtract_multiply_fusion = f32[2048,512]{1,0:T(8,128)} fusion(f32[2048,512]{1,0:T(8,128)S(1)} %fusion.10, f32[2048,512]{1,0:T(8,128)S(1)} %copy-done.1, f32[512]{0:T(512)S(1)} %copy-done.102, f32[512,1,512]{2,1,0:T(1,128)S(1)} %fusion.1), kind=kOutput, calls=%fused_computation.9 | convolution fusion | flops 6445596672 | bytes 13633536 | tf_op jit(solution)/shard_map/dot_general | solution.py:98
  (296 shorter events, 45.2 us)
Async XLA Ops:
  7.2 107.9 %all-reduce.4.cloned.1.call-start = ((), (), s32[]{:S(2)}) async-start(), calls=%async_computation.2 | async-start | bytes 4456448 | tf_op jit(solution)/shard_map/psum | solution.py:81
  21.5 143.1 %all-gather.5.cloned.1.call-start = ((), (), s32[]{:S(2)}) async-start(), calls=%async_computation | async-start | bytes 1179648 | tf_op jit(solution)/shard_map/all_gather | solution.py:83
  132.4 10.4 %copy-start.68 = (f32[1,2048]{1,0:T(1,128)}, f32[1,2048]{1,0:T(1,128)S(1)}, u32[]{:S(2)}) copy-start(f32[1,2048]{1,0:T(1,128)S(1)} %get-tuple-element.93) | copy-start | bytes 24580
  141.8 589.3 %all-gather.7.cloned.1.call-start = ((), (), s32[]{:S(2)}) async-start(), calls=%async_computation.1 | async-start | bytes 2228224 | tf_op jit(solution)/shard_map/all_gather | solution.py:15
  145.6 25.1 %copy-start.51 = (f32[1,2048]{1,0:T(1,128)}, f32[1,2048]{1,0:T(1,128)S(1)}, u32[]{:S(2)}) copy-start(f32[1,2048]{1,0:T(1,128)S(1)} %get-tuple-element.166) | copy-start | bytes 24580
  146.8 23.9 %copy-start.61 = (f32[1,2048]{1,0:T(1,128)}, f32[1,2048]{1,0:T(1,128)S(1)}, u32[]{:S(2)}) copy-start(f32[1,2048]{1,0:T(1,128)S(1)} %get-tuple-element.186) | copy-start | bytes 24580
  146.8 23.9 %copy-start.63 = (f32[1,2048]{1,0:T(1,128)}, f32[1,2048]{1,0:T(1,128)S(1)}, u32[]{:S(2)}) copy-start(f32[1,2048]{1,0:T(1,128)S(1)} %get-tuple-element.187) | copy-start | bytes 24580
  148.1 22.6 %copy-start.7 = (f32[1,2048]{1,0:T(1,128)}, f32[1,2048]{1,0:T(1,128)S(1)}, u32[]{:S(2)}) copy-start(f32[1,2048]{1,0:T(1,128)S(1)} %get-tuple-element.210) | copy-start | bytes 24580
  148.1 22.6 %copy-start.9 = (f32[1,2048]{1,0:T(1,128)}, f32[1,2048]{1,0:T(1,128)S(1)}, u32[]{:S(2)}) copy-start(f32[1,2048]{1,0:T(1,128)S(1)} %get-tuple-element.227) | copy-start | bytes 24580
  633.1 12.4 %copy-start.8 = (f32[1,2048]{1,0:T(1,128)S(1)}, f32[1,2048]{1,0:T(1,128)}, u32[]{:S(2)}) copy-start(f32[1,2048]{1,0:T(1,128)} %copy-done.7) | copy-start | bytes 24580
  633.1 12.4 %copy-start.10 = (f32[1,2048]{1,0:T(1,128)S(1)}, f32[1,2048]{1,0:T(1,128)}, u32[]{:S(2)}) copy-start(f32[1,2048]{1,0:T(1,128)} %copy-done.9) | copy-start | bytes 24580
  641.2 9.2 %copy-start.52 = (f32[1,2048]{1,0:T(1,128)S(1)}, f32[1,2048]{1,0:T(1,128)}, u32[]{:S(2)}) copy-start(f32[1,2048]{1,0:T(1,128)} %copy-done.51) | copy-start | bytes 24580
  641.2 9.2 %copy-start.62 = (f32[1,2048]{1,0:T(1,128)S(1)}, f32[1,2048]{1,0:T(1,128)}, u32[]{:S(2)}) copy-start(f32[1,2048]{1,0:T(1,128)} %copy-done.61) | copy-start | bytes 24580
  641.5 10.6 %copy-start.58 = (f32[1,2048]{1,0:T(1,128)S(1)}, f32[1,2048]{1,0:T(1,128)}, u32[]{:S(2)}) copy-start(f32[1,2048]{1,0:T(1,128)} %copy-done.57) | copy-start | bytes 24580
  641.5 10.6 %copy-start.60 = (f32[1,2048]{1,0:T(1,128)S(1)}, f32[1,2048]{1,0:T(1,128)}, u32[]{:S(2)}) copy-start(f32[1,2048]{1,0:T(1,128)} %copy-done.59) | copy-start | bytes 24580
  641.5 10.6 %copy-start.64 = (f32[1,2048]{1,0:T(1,128)S(1)}, f32[1,2048]{1,0:T(1,128)}, u32[]{:S(2)}) copy-start(f32[1,2048]{1,0:T(1,128)} %copy-done.63) | copy-start | bytes 24580
  641.5 10.6 %copy-start.66 = (f32[1,2048]{1,0:T(1,128)S(1)}, f32[1,2048]{1,0:T(1,128)}, u32[]{:S(2)}) copy-start(f32[1,2048]{1,0:T(1,128)} %copy-done.65) | copy-start | bytes 24580
  641.5 10.6 %copy-start.69 = (f32[1,2048]{1,0:T(1,128)S(1)}, f32[1,2048]{1,0:T(1,128)}, u32[]{:S(2)}) copy-start(f32[1,2048]{1,0:T(1,128)} %copy-done.68) | copy-start | bytes 24580
  641.5 10.6 %copy-start.71 = (f32[1,2048]{1,0:T(1,128)S(1)}, f32[1,2048]{1,0:T(1,128)}, u32[]{:S(2)}) copy-start(f32[1,2048]{1,0:T(1,128)} %copy-done.70) | copy-start | bytes 24580
  641.5 10.6 %copy-start.73 = (f32[1,2048]{1,0:T(1,128)S(1)}, f32[1,2048]{1,0:T(1,128)}, u32[]{:S(2)}) copy-start(f32[1,2048]{1,0:T(1,128)} %get-tuple-element.209) | copy-start | bytes 24580
  641.6 13.8 %copy-start.50 = (f32[16,512]{1,0:T(8,128)S(1)}, f32[16,512]{1,0:T(8,128)}, u32[]{:S(2)}) copy-start(f32[16,512]{1,0:T(8,128)} %param.15) | copy-start | bytes 98308
  643.6 10.8 %copy-start.101 = (f32[2048]{0:T(1024)}, f32[2048]{0:T(1024)S(1)}, u32[]{:S(2)}) copy-start(f32[2048]{0:T(1024)S(1)} %get-tuple-element.1184) | copy-start | bytes 24580
  662.0 48.5 %copy-start.67 = (f32[16,512]{1,0:T(8,128)S(1)}, f32[16,512]{1,0:T(8,128)}, u32[]{:S(2)}) copy-start(f32[16,512]{1,0:T(8,128)} %param.19) | copy-start | bytes 98308
  662.0 48.7 %copy-start.56 = (f32[16,512]{1,0:T(8,128)S(1)}, f32[16,512]{1,0:T(8,128)}, u32[]{:S(2)}) copy-start(f32[16,512]{1,0:T(8,128)} %get-tuple-element.1188) | copy-start | bytes 98308
  (88 other events, 608.6 us)
Sparse Core Ops, SparseCore 0:
  21.6 93.4 all-reduce.3
  142.0 22.6 all-gather.4
  668.5 45.2 all-gather.6
where the time goes:
time: 761 us; the launch traced here: 753 us
  local copies, waits for them, and re-layouts  462 us (61%)
  waiting for transfers between devices  100 us (13%)
  other arithmetic  80.8 us (11%)
  matrix products  53.5 us (7%)
  blocking collectives  40.6 us (5%)
  between operations  16.6 us (2%)
    gather x1, local copies, waits for them, and re-layouts, neighbour_mean(): return jnp.mean(jnp.take(coeff_table, listed, axis=1), axis=2)  437 us
    psum x1, waiting for transfers between devices, per_device(): gram_sums, right_sums = lax.psum((gram_part, right_part), 'tm')  88.8 us
    unnamed x1, blocking collectives  40.6 us
    reduce_sum x1, other arithmetic, neighbour_mean(): return jnp.mean(jnp.take(coeff_table, listed, axis=1), axis=2)  25 us
    div x12, other arithmetic, spd_solve(): backward[row_index] = entry / factor[row_index][row_index]  19.9 us
    dot_general x1, matrix products, per_device(): jnp.einsum('jt,jtu,ju->tu', load_u, kernel_terms, feed_w, precision=HIGHEST)  16.3 us
  transfers between devices with their start and end apart: 3, of which 2 were waited for; matrix products, arithmetic and copies ran while one was open for 5% of the time, Pallas kernels for 0%

commit v1 on v0

v1 whole, which is shorter than its diff:
```python
import jax
import jax.numpy as jnp
import numpy as np
from jax import lax
from jax.experimental import pallas as pl
from jax.experimental.pallas import tpu as pltpu
from jax.sharding import Mesh, PartitionSpec as P

BASIS_VECTORS = 16
NOISE_TERMS = 16
NEIGH = 64
DIAGONALS = 9
PAIRS = 136
OWN = 128
CUT = 128
STEP = 256
CHUNKS = STEP // OWN
GRAM_ROWS = PAIRS + 16
CROSS_ROWS = 16 + BASIS_VECTORS * NOISE_TERMS
WHITEN_STEP = 512
WHITEN_CHUNKS = WHITEN_STEP // OWN

F32 = jnp.float32
BF16 = jnp.bfloat16
MIB = 1 << 20


def split3(x):
    high = x.astype(BF16)
    rest = x - high.astype(F32)
    mid = rest.astype(BF16)
    low = (rest - mid.astype(F32)).astype(BF16)
    return high, mid, low


def left_stack(x):
    high, mid, low = split3(x)
    return jnp.concatenate([high, high, mid, high, mid, low], axis=0)


def right_stack(x):
    high, mid, low = split3(x)
    return jnp.concatenate([high, mid, high, low, mid, high], axis=0)


def dot_nt(a, b):
    return lax.dot_general(a, b, (((1,), (1,)), ((), ())), preferred_element_type=F32)


def dot_tn(a, b):
    return lax.dot_general(a, b, (((0,), (0,)), ((), ())), preferred_element_type=F32)


def dot_nn(a, b):
    return lax.dot_general(a, b, (((1,), (0,)), ((), ())), preferred_element_type=F32)


def masked_sums(x, mask):
    rows = x.shape[0]
    stacked = jnp.concatenate(split3(x), axis=0)
    sums = dot_nn(stacked, mask.astype(F32).astype(BF16))
    return sums[0:rows] + (sums[rows : 2 * rows] + sums[2 * rows : 3 * rows])


def narrow_dots(table_ref, start, x, pieces):
    parts = split3(x)[:pieces]
    sums = [
        dot_nt(table_ref[start : start + 16 * (3 - place), :], part)
        for place, part in enumerate(parts)
    ]
    total = sums[0][32:48]
    for place in range(1, pieces):
        total = total + sums[place][16 * (2 - place) : 16 * (3 - place)]
    mid = sums[0][16:32] + sums[1][0:16]
    return sums[0][0:16] + (mid + total)


def gram_kernel(flux_ref, valid_ref, quality_ref, basis_ref, out_ref, marked_ref, table_ref):
    wide = DIAGONALS * BASIS_VECTORS
    rights = 3 * wide

    @pl.when(pl.program_id(0) == 0)
    def _():
        basis = basis_ref[...]
        scaled = basis * (1.0 / 12.0)
        products = []
        for diagonal in range(DIAGONALS):
            turned = basis
            if diagonal:
                turned = jnp.concatenate([basis[diagonal:], basis[:diagonal]], axis=0)
            products.append(scaled * turned)
        for place, piece in enumerate(split3(jnp.concatenate(products, axis=0))):
            table_ref[place * wide : (place + 1) * wide, :] = piece
        for place, piece in enumerate(split3(scaled)):
            table_ref[rights + place * 16 : rights + place * 16 + 16, :] = piece

    flux = flux_ref[...]
    quality = quality_ref[...]
    usable = valid_ref[...] != 0
    marked_ref[...] = jnp.where(usable, flux, jnp.nan)
    twelfths = jnp.where(
        quality == 0, 12.0, jnp.where(quality == 1, 6.0, jnp.where(quality == 2, 4.0, 3.0))
    )
    weight = jnp.where(usable, twelfths, 0.0)
    grams = dot_nt(table_ref[0:rights, :], weight.astype(BF16))
    gram = grams[0:PAIRS] + (grams[wide : wide + PAIRS] + grams[2 * wide : 2 * wide + PAIRS])
    right = narrow_dots(table_ref, rights, weight * flux, 3)
    for chunk in range(CHUNKS):
        lanes = slice(chunk * OWN, (chunk + 1) * OWN)
        out_ref[chunk, 0:PAIRS, :] = gram[:, lanes]
        out_ref[chunk, PAIRS:GRAM_ROWS, :] = right[:, lanes]


def cross_kernel(marked_ref, basis_ref, decay_ref, feed_ref, out_ref, decayed_ref, table_ref):
    cross = BASIS_VECTORS * NOISE_TERMS
    feeds = 2 * cross

    @pl.when(pl.program_id(0) == 0)
    def _():
        log_decay = jnp.log(decay_ref[...])
        count = log_decay.shape[1]
        rows = lax.broadcasted_iota(jnp.int32, (count, count), 0)
        columns = lax.broadcasted_iota(jnp.int32, (count, count), 1)
        suffix = masked_sums(log_decay, rows > columns)
        feed = jnp.exp(suffix) * feed_ref[...]
        whole = jnp.exp(suffix[:, 0:1] + log_decay[:, 0:1])
        decayed_ref[...] = jnp.broadcast_to(whole, (NOISE_TERMS, OWN))
        for k in range(BASIS_VECTORS):
            product = basis_ref[k : k + 1, :] * feed
            for place, piece in enumerate(split3(product)[:2]):
                first = place * cross + k * 16
                table_ref[first : first + 16, :] = piece
        for place, piece in enumerate(split3(feed)):
            table_ref[feeds + place * 16 : feeds + place * 16 + 16, :] = piece

    marked = marked_ref[...]
    usable = marked == marked
    sums = dot_nt(table_ref[0:feeds, :], jnp.where(usable, 1.0, 0.0).astype(BF16))
    crossed = sums[0:cross] + sums[cross : 2 * cross]
    plain = narrow_dots(table_ref, feeds, jnp.where(usable, marked, 0.0), 2)
    for chunk in range(CHUNKS):
        lanes = slice(chunk * OWN, (chunk + 1) * OWN)
        out_ref[chunk, 0:16, :] = plain[:, lanes]
        out_ref[chunk, 16:CROSS_ROWS, :] = crossed[:, lanes]


def count_kernel(code_ref, low_ref, out_ref):
    entries = 8 * NEIGH
    row_code = lax.broadcasted_iota(jnp.int32, (128 * 8, entries), 0)
    low_code = lax.broadcasted_iota(jnp.int32, (128, entries), 0)

    def one_half(group):
        code = code_ref[pl.ds(group, 1), :]
        low = low_ref[pl.ds(group, 1), :]
        highs = jnp.where(row_code == code, 1.0, 0.0).astype(BF16)
        lows = jnp.where(low_code == low, 1.0, 0.0).astype(BF16)
        return dot_nt(highs, lows).reshape(128, 8, 128)

    def one(step, ignored):
        both = jnp.concatenate([one_half(2 * step), one_half(2 * step + 1)], axis=1)
        out_ref[:, pl.ds(pl.multiple_of(step * 16, 16), 16), :] = both.astype(BF16)
        return ignored

    lax.fori_loop(0, OWN // 16, one, 0)


def noise_kernel(
    decay_ref, load_ref, feed_ref, basis_ref, high_ref, low_ref, entry_ref, stack_ref
):
    log_decay = jnp.log(decay_ref[...])
    load = load_ref[...]
    feed = feed_ref[...]
    count = log_decay.shape[1]
    rows = lax.broadcasted_iota(jnp.int32, (count, count), 0)
    columns = lax.broadcasted_iota(jnp.int32, (count, count), 1)
    together = (rows // CUT) == (columns // CUT)
    before = masked_sums(log_decay, together & (rows < columns))
    tail = masked_sums(log_decay, together & (rows > columns))
    through = before + log_decay
    cuts = count // CUT
    totals = [through[:, (cut + 1) * CUT - 1 : (cut + 1) * CUT] for cut in range(cuts)]
    lower = lax.broadcasted_iota(jnp.int32, (CUT, CUT), 0) < lax.broadcasted_iota(
        jnp.int32, (CUT, CUT), 1
    )
    high_ref[...] = jnp.zeros_like(high_ref)
    low_ref[...] = jnp.zeros_like(low_ref)

    def keep(u, t, block):
        high = block.astype(BF16)
        span = (slice(u * CUT, (u + 1) * CUT), slice(t * CUT, (t + 1) * CUT))
        high_ref[span] = high
        low_ref[span] = (block - high.astype(F32)).astype(BF16)

    passed = jnp.zeros((NOISE_TERMS, 1), F32)
    entries = []
    for t in range(cuts):
        lanes = slice(t * CUT, (t + 1) * CUT)
        middle = through[:, t * CUT + CUT // 2 - 1 : t * CUT + CUT // 2]
        near_left = feed[:, lanes] * jnp.exp(middle - through[:, lanes])
        near_right = load[:, lanes] * jnp.exp(before[:, lanes] - middle)
        near = dot_tn(left_stack(near_left), right_stack(near_right))
        keep(t, t, jnp.where(lower, near, 0.0))
        far_right = right_stack(load[:, lanes] * jnp.exp(before[:, lanes]))
        between = jnp.zeros((NOISE_TERMS, 1), F32)
        for u in range(t - 1, -1, -1):
            span = slice(u * CUT, (u + 1) * CUT)
            far_left = left_stack(feed[:, span] * jnp.exp(tail[:, span] + between))
            keep(u, t, dot_tn(far_left, far_right))
            between = between + totals[u]
        entries.append(load[:, lanes] * jnp.exp(before[:, lanes] + passed))
        passed = passed + totals[t]
    entry_ref[...] = right_stack(jnp.concatenate(entries, axis=1))
    stack_ref[...] = right_stack(basis_ref[...])


def row_of_pair(i, j):
    apart = (j - i) % BASIS_VECTORS
    if apart < 8 or (apart == 8 and i < 8):
        return apart * BASIS_VECTORS + i
    return ((i - j) % BASIS_VECTORS) * BASIS_VECTORS + j


def eliminate(columns, vector):
    order = BASIS_VECTORS
    columns = list(columns)
    rows = lax.broadcasted_iota(jnp.int32, columns[0].shape, 0)
    scaled, pivots = [], []
    for k in range(order):
        inverse = 1.0 / columns[k][k : k + 1, :]
        factor = jnp.where(rows > k, columns[k] * inverse, 0.0)
        for j in range(k + 1, order):
            columns[j] = columns[j] - factor * columns[j][k : k + 1, :]
        scaled.append(factor)
        pivots.append(inverse)
        if vector is not None:
            vector = vector - factor * vector[k : k + 1, :]
    return scaled, pivots, vector, columns


def back_substitute(vector, uppers, pivots):
    rows = lax.broadcasted_iota(jnp.int32, vector.shape, 0)
    solved = jnp.zeros_like(vector)
    for k in range(BASIS_VECTORS - 1, -1, -1):
        value = vector[k : k + 1, :] * pivots[k]
        vector = vector - uppers[k] * value
        solved = jnp.where(rows == k, value, solved)
    return solved


def solve_kernel(parts_ref, prec_ref, fitted_ref, factor_ref, upper_ref, pivot_ref, right_ref, sums_ref, matrix_ref):
    total = parts_ref[0]
    for part in range(1, parts_ref.shape[0]):
        total = total + parts_ref[part]
    sums_ref[...] = total
    right = total[PAIRS : PAIRS + 16]
    right_ref[...] = right
    order = BASIS_VECTORS
    for j in range(order):
        for i in range(order):
            row = row_of_pair(i, j)
            matrix_ref[j * order + i : j * order + i + 1, :] = sums_ref[row : row + 1, :]
    rows = lax.broadcasted_iota(jnp.int32, right.shape, 0)
    plain = [matrix_ref[j * order : (j + 1) * order, :] for j in range(order)]
    prec = prec_ref[...]
    ridged = [jnp.where(rows == j, plain[j] + 0.1, plain[j]) for j in range(order)]
    ignored, pivots, reduced, uppers = eliminate(ridged, right)
    fitted = back_substitute(reduced, uppers, pivots)
    for peer in range(fitted_ref.shape[0]):
        fitted_ref[peer] = fitted
    weighted = [jnp.where(rows == j, plain[j] + prec, plain[j]) for j in range(order)]
    factors, pivots, ignored, uppers = eliminate(weighted, None)
    for k in range(order):
        factor_ref[k] = factors[k]
        upper_ref[k] = uppers[k]
        pivot_ref[k : k + 1, :] = pivots[k]


def map_kernel(
    fitted_ref, counts_ref, prec_ref, factor_ref, upper_ref, pivot_ref, right_ref, out_ref
):
    prior = jnp.zeros((48, OWN), F32)
    for place in range(0, fitted_ref.shape[0], 2):
        wide = jnp.concatenate([fitted_ref[place], fitted_ref[place + 1]], axis=1)
        listed = jnp.concatenate([counts_ref[place], counts_ref[place + 1]], axis=1)
        prior = prior + dot_nt(jnp.concatenate(split3(wide), axis=0), listed)
    prior_mean = (prior[0:16] + (prior[16:32] + prior[32:48])) * (1.0 / NEIGH)
    vector = right_ref[...] + prec_ref[...] * prior_mean
    for k in range(BASIS_VECTORS):
        vector = vector - factor_ref[k] * vector[k : k + 1, :]
    uppers = [upper_ref[k] for k in range(BASIS_VECTORS)]
    pivots = [pivot_ref[k : k + 1, :] for k in range(BASIS_VECTORS)]
    coeffs = back_substitute(vector, uppers, pivots)
    for peer in range(out_ref.shape[0]):
        out_ref[peer] = coeffs


def carry_kernel(rows_ref, crossed_ref, decayed_ref, out_ref):
    for owner in range(rows_ref.shape[0]):
        coeffs = rows_ref[owner]
        carry = crossed_ref[owner, 0:16, :]
        for k in range(BASIS_VECTORS):
            first = 16 + 16 * k
            carry = carry - coeffs[k : k + 1, :] * crossed_ref[owner, first : first + 16, :]
        out_ref[owner, 0:16, :] = carry
        out_ref[owner, 16:32, :] = decayed_ref[...]


def state_kernel(carry_ref, out_ref):
    state = jnp.zeros((NOISE_TERMS, OWN), F32)
    for block in range(carry_ref.shape[0]):
        out_ref[block] = state
        state = state * carry_ref[block, 16:32, :] + carry_ref[block, 0:16, :]


def local_kernel(marked_ref, rows_ref, stack_ref, high_ref, low_ref, coeffs_ref, out_ref):
    coeffs = jnp.concatenate([rows_ref[chunk] for chunk in range(WHITEN_CHUNKS)], axis=1)
    coeffs_ref[...] = coeffs
    trend = dot_tn(left_stack(coeffs), stack_ref[...])
    marked = marked_ref[...]
    residual = jnp.where(marked == marked, marked - trend, 0.0)
    high = residual.astype(BF16)
    low = (residual - high.astype(F32)).astype(BF16)
    count = residual.shape[1]
    for first in range(0, count, 256):
        lanes = slice(first, first + 256)
        upto = slice(0, first + 256)
        local = dot_nn(low[:, upto], high_ref[upto, lanes]) + dot_nn(high[:, upto], low_ref[upto, lanes])
        local = local + dot_nn(high[:, upto], high_ref[upto, lanes])
        out_ref[:, lanes] = residual[:, lanes] - local


def finish_kernel(local_ref, states_ref, entry_ref, scale_ref, out_ref):
    states = jnp.concatenate([states_ref[chunk] for chunk in range(WHITEN_CHUNKS)], axis=1)
    incoming = dot_tn(left_stack(states), entry_ref[...])
    out_ref[...] = (local_ref[...] - incoming) * scale_ref[...]


def vmem():
    return pl.BlockSpec(memory_space=pltpu.VMEM)


def params(mib):
    return pltpu.CompilerParams(vmem_limit_bytes=mib * MIB)


def cost(flops, bytes_accessed):
    return pl.CostEstimate(flops=flops, bytes_accessed=bytes_accessed, transcendentals=0)


def per_device(
    flux, valid, quality, basis, neighbours, prior_prec, decay, load_u, feed_w, inv_diag
):
    stars, cadences = flux.shape
    blocks = stars // OWN
    steps = stars // STEP
    place = lax.axis_index("tm")
    prec = jnp.broadcast_to(prior_prec[:, None], (BASIS_VECTORS, OWN))

    listed = lax.dynamic_slice_in_dim(neighbours, place * OWN, OWN, 0).reshape(blocks, -1)
    code = (listed >> 7) * 8 + lax.broadcasted_iota(jnp.int32, listed.shape, 1) // NEIGH

    wide_spec = pl.BlockSpec((STEP, cadences), lambda i: (i, 0))
    table_spec = pl.BlockSpec((16, cadences), lambda i: (0, 0))
    parts, marked = pl.pallas_call(
        gram_kernel,
        grid=(steps,),
        in_specs=[wide_spec, wide_spec, wide_spec, table_spec],
        out_specs=[pl.BlockSpec((CHUNKS, GRAM_ROWS, OWN), lambda i: (i, 0, 0)), wide_spec],
        out_shape=[
            jax.ShapeDtypeStruct((blocks, GRAM_ROWS, OWN), F32),
            jax.ShapeDtypeStruct((stars, cadences), F32),
        ],
        scratch_shapes=[pltpu.VMEM((480, cadences), BF16)],
        compiler_params=params(56),
        cost_estimate=cost(2 * stars * cadences * 600, 18 * MIB),
        name="gram",
    )(flux, valid, quality, basis)

    crossed, decayed = pl.pallas_call(
        cross_kernel,
        grid=(steps,),
        in_specs=[wide_spec, table_spec, table_spec, table_spec],
        out_specs=[
            pl.BlockSpec((CHUNKS, CROSS_ROWS, OWN), lambda i: (i, 0, 0)),
            pl.BlockSpec((NOISE_TERMS, OWN), lambda i: (0, 0)),
        ],
        out_shape=[
            jax.ShapeDtypeStruct((blocks, CROSS_ROWS, OWN), F32),
            jax.ShapeDtypeStruct((NOISE_TERMS, OWN), F32),
        ],
        scratch_shapes=[pltpu.VMEM((560, cadences), BF16)],
        compiler_params=params(56),
        cost_estimate=cost(2 * stars * cadences * 800, 8 * MIB),
        name="cross",
    )(marked, basis, decay, feed_w)
    parts = lax.all_to_all(parts, "tm", 0, 0, tiled=True)
    parts, crossed, decayed = lax.optimization_barrier((parts, crossed, decayed))

    square = jax.ShapeDtypeStruct((16, 16, OWN), F32)
    flat = jax.ShapeDtypeStruct((16, OWN), F32)
    everyone = ("y", "c", "tm")
    copies = jax.ShapeDtypeStruct((lax.axis_size(everyone), 16, OWN), F32)
    fitted, factor, upper, pivot, right = pl.pallas_call(
        solve_kernel,
        in_specs=[vmem()] * 2,
        out_specs=[vmem()] * 5,
        out_shape=[copies, square, square, flat, flat],
        scratch_shapes=[pltpu.VMEM((GRAM_ROWS, OWN), F32), pltpu.VMEM((256, OWN), F32)],
        compiler_params=params(16),
        cost_estimate=cost(1 << 20, 2 * MIB),
        name="solve",
    )(parts, prec)

    fitted, later_code, later_low, later_decay, later_basis = lax.optimization_barrier(
        (fitted, code, listed & 127, decay, basis)
    )
    fitted = lax.all_to_all(fitted, everyone, 0, 0, tiled=True)
    counts = pl.pallas_call(
        count_kernel,
        in_specs=[vmem(), vmem()],
        out_specs=vmem(),
        out_shape=jax.ShapeDtypeStruct((128, OWN, 128), BF16),
        compiler_params=params(16),
        cost_estimate=cost(4 << 30, 4 * MIB),
        name="count",
    )(later_code, later_low)
    high, low, entry, stack = pl.pallas_call(
        noise_kernel,
        in_specs=[vmem()] * 4,
        out_specs=[vmem()] * 4,
        out_shape=[
            jax.ShapeDtypeStruct((cadences, cadences), BF16),
            jax.ShapeDtypeStruct((cadences, cadences), BF16),
            jax.ShapeDtypeStruct((96, cadences), BF16),
            jax.ShapeDtypeStruct((96, cadences), BF16),
        ],
        compiler_params=params(16),
        cost_estimate=cost(2 << 30, 2 * MIB),
        name="noise",
    )(later_decay, load_u, feed_w, later_basis)
    fitted, counts, high, low, entry, stack = lax.optimization_barrier(
        (fitted, counts, high, low, entry, stack)
    )

    rows = pl.pallas_call(
        map_kernel,
        in_specs=[vmem()] * 7,
        out_specs=vmem(),
        out_shape=jax.ShapeDtypeStruct((blocks, 16, OWN), F32),
        compiler_params=params(16),
        cost_estimate=cost(1 << 28, 6 * MIB),
        name="map",
    )(fitted, counts, prec, factor, upper, pivot, right)
    rows = lax.all_to_all(rows, "tm", 0, 0, tiled=True)

    carries = pl.pallas_call(
        carry_kernel,
        in_specs=[vmem()] * 3,
        out_specs=vmem(),
        out_shape=jax.ShapeDtypeStruct((blocks, 32, OWN), F32),
        compiler_params=params(16),
        cost_estimate=cost(1 << 24, 3 * MIB),
        name="local_carry",
    )(rows, crossed, decayed)
    carries, later_rows = lax.optimization_barrier((carries, rows))
    carries = lax.all_to_all(carries, "tm", 0, 0, tiled=True)

    part_spec = pl.BlockSpec((WHITEN_CHUNKS, 16, OWN), lambda i: (i, 0, 0))
    tall_spec = pl.BlockSpec((WHITEN_STEP, cadences), lambda i: (i, 0))
    coeffs, local = pl.pallas_call(
        local_kernel,
        grid=(stars // WHITEN_STEP,),
        in_specs=[tall_spec, part_spec, vmem(), vmem(), vmem()],
        out_specs=[pl.BlockSpec((16, WHITEN_STEP), lambda i: (0, i)), tall_spec],
        out_shape=[
            jax.ShapeDtypeStruct((16, stars), F32),
            jax.ShapeDtypeStruct((stars, cadences), F32),
        ],
        compiler_params=params(16),
        cost_estimate=cost(2 * stars * cadences * 1500, 10 * MIB),
        name="local",
    )(marked, later_rows, stack, high, low)
    carries, local = lax.optimization_barrier((carries, local))

    states = pl.pallas_call(
        state_kernel,
        in_specs=[vmem()],
        out_specs=vmem(),
        out_shape=jax.ShapeDtypeStruct((blocks, 16, OWN), F32),
        compiler_params=params(16),
        cost_estimate=cost(1 << 20, MIB),
        name="state",
    )(carries)
    states = lax.all_to_all(states, "tm", 0, 0, tiled=True)

    whitened = pl.pallas_call(
        finish_kernel,
        grid=(stars // WHITEN_STEP,),
        in_specs=[tall_spec, part_spec, vmem(), vmem()],
        out_specs=tall_spec,
        out_shape=jax.ShapeDtypeStruct((stars, cadences), F32),
        compiler_params=params(16),
        cost_estimate=cost(2 * stars * cadences * 100, 9 * MIB),
        name="finish",
    )(local, states, entry, inv_diag[None, :])
    return coeffs.T, whitened


def solution(mesh):
    devices = mesh.devices
    split = Mesh(devices.reshape(devices.shape[0] // 2, 2, devices.shape[1]), ("y", "c", "tm"))
    star = ("y", "c")
    in_specs = (
        P(star, "tm"),
        P(star, "tm"),
        P(star, "tm"),
        P(None, "tm"),
        P(star, None),
        P(),
        P(None, "tm"),
        P(None, "tm"),
        P(None, "tm"),
        P("tm"),
    )
    out_specs = (P(star, None), P(star, "tm"))
    return jax.shard_map(
        per_device, mesh=split, in_specs=in_specs, out_specs=out_specs, check_vma=False
    )
```

time: 761 us -> 120 us (0.16)
  local copies, waits for them, and re-layouts: 462 us -> 20.1 us
  waiting for transfers between devices: 100 us -> 17.1 us
  other arithmetic: 80.8 us -> 1.39 us
  matrix products: 53.5 us -> 0 us
  Pallas kernels: 0 us -> 36 us
  starting transfers between devices: 0.12 us -> 18.3 us
  between operations: 16.6 us -> 0.85 us
  blocking collectives: 40.6 us -> 25.5 us
    gather x1 -> x0, local copies, waits for them, and re-layouts: 437 us -> none  [neighbour_mean(): return jnp.mean(jnp.take(coeff_table, listed, axis=1), axis=2)]
    psum x1 -> x0, waiting for transfers between devices: 88.8 us -> none  [per_device(): gram_sums, right_sums = lax.psum((gram_part, right_part), 'tm')]
    dot_general x8 -> x0, matrix products: 53.5 us -> none  [the longest x1 16.3 us: per_device(): jnp.einsum('jt,jtu,ju->tu', load_u, kernel_terms, feed_w, precision=HIGHEST)]
    unnamed x1 -> x0, blocking collectives: 40.6 us -> none
    div x30 -> x1, other arithmetic: 40.4 us -> 0.01 us  [per_device(): lax.broadcasted_iota(jnp.int32, listed.shape, 1) // NEIGH]
    pallas_call x0 -> x10, Pallas kernels: none -> 36 us  [the longest x1 10.3 us: per_device(): pl.pallas_call(gram_kernel, grid=(steps,), in_specs=[wide_spec, wide_spec...]
    all_to_all x0 -> x2, blocking collectives: none -> 25.5 us  [the longest x1 14.9 us: per_device(): states = lax.all_to_all(states, 'tm', 0, 0, tiled=True)]
    reduce_sum x1 -> x0, other arithmetic: 25 us -> none  [neighbour_mean(): return jnp.mean(jnp.take(coeff_table, listed, axis=1), axis=2)]
  transfers between devices with their start and end apart: 3 -> 3, of which waited for: 2 -> 2; matrix products, arithmetic and copies ran while one was open for 5% -> 2% of each run, Pallas kernels for 0% -> 16%
where the time goes in v1:
time: 120 us; the launch traced here: 119 us
  Pallas kernels  36 us (30%)
  blocking collectives  25.5 us (21%)
  local copies, waits for them, and re-layouts  20.1 us (17%)
  starting transfers between devices  18.3 us (15%)
  waiting for transfers between devices  17.1 us (14%)
  other arithmetic  1.39 us (1%)
    unnamed x54, local copies, waits for them, and re-layouts  19.1 us
    all_to_all x1, blocking collectives, per_device(): states = lax.all_to_all(states, 'tm', 0, 0, tiled=True)  14.9 us
    all_to_all x1, blocking collectives, per_device(): rows = lax.all_to_all(rows, 'tm', 0, 0, tiled=True)  10.7 us
    pallas_call x1, Pallas kernels, per_device(): pl.pallas_call(gram_kernel, grid=(steps,), in_specs=[wide_spec, wide_spec...  10.3 us
    all_to_all x1, waiting for transfers between devices, per_device(): parts = lax.all_to_all(parts, 'tm', 0, 0, tiled=True)  9.47 us
    pallas_call x1, Pallas kernels, per_device(): pl.pallas_call(cross_kernel, grid=(steps,), in_specs=[wide_spec, table_sp...  8.17 us
    all_to_all x1, starting transfers between devices, per_device(): parts = lax.all_to_all(parts, 'tm', 0, 0, tiled=True)  8.09 us
    all_to_all x1, waiting for transfers between devices, per_device(): fitted = lax.all_to_all(fitted, everyone, 0, 0, tiled=True)  7.65 us
  transfers between devices with their start and end apart: 3, of which 2 were waited for; matrix products, arithmetic and copies ran while one was open for 2% of the time, Pallas kernels for 16%

profile of v1, /device:TPU:0, one launch (start us, length us, event | category | flops | bytes accessed | tf_op | source)
XLA Modules:
  0.0 119.2 jit_solution(9273531326405414306)
XLA Ops:
  0.6 10.3 %gram.1 = (f32[16,152,128]{2,1,0:T(8,128)}, f32[2048,512]{1,0:T(8,128)}) custom-call(f32[2048,512]{1,0:T(8,128)} %flux_ref.1, s32[2048,512]{1,0:T(8,128)} %valid_ref.1, s32[2048,512]{1,0:T(8,128)} %quality_ref.1, f32[16,512]{1,0:T(8,128)} %basis_ref.4), custom_call_target="tpu_custom_call" | custom-call | flops 1258291200 | bytes 18874368 | tf_op jit(solution)/shard_map/gram/pallas_call | solution.py:364
  10.9 8.1 %all-to-all-start = ((f32[16,152,128]{2,1,0:T(8,128)}), f32[16,152,128]{2,1,0:T(8,128)S(1)}, u32[]{:S(2)}, u32[]{:S(2)}) async-start(f32[16,152,128]{2,1,0:T(8,128)} %get-tuple-element.36), calls=%async_computation | async-start | bytes 2490368 | tf_op jit(solution)/shard_map/all_to_all | solution.py:396
  20.8 8.2 %cross.1 = (f32[16,272,128]{2,1,0:T(8,128)}, f32[16,128]{1,0:T(8,128)}) custom-call(f32[2048,512]{1,0:T(8,128)} %get-tuple-element.35.marked_ref, f32[16,512]{1,0:T(8,128)} %basis_ref.4, f32[16,512]{1,0:T(8,128)} %decay_ref.2, f32[16,512]{1,0:T(8,128)} %feed_ref.3), custom_call_target="tpu_custom_call" | custom-call | flops 1677721600 | bytes 8388608 | tf_op jit(solution)/shard_map/cross/pallas_call | solution.py:379
  29.6 9.5 %all-to-all-done.parts_ref = f32[16,152,128]{2,1,0:T(8,128)S(1)} async-done(((f32[16,152,128]{2,1,0:T(8,128)}), f32[16,152,128]{2,1,0:T(8,128)S(1)}, u32[]{:S(2)}, u32[]{:S(2)}) %all-to-all-start) | async-done | bytes 1245216 | tf_op jit(solution)/shard_map/all_to_all | solution.py:396
  39.1 1.4 %solve.1 = (f32[128,16,128]{2,1,0:T(8,128)}, f32[16,16,128]{2,1,0:T(8,128)S(1)}, f32[16,16,128]{2,1,0:T(8,128)S(1)}, f32[16,128]{1,0:T(8,128)S(1)}, f32[16,128]{1,0:T(8,128)S(1)}) custom-call(f32[16,152,128]{2,1,0:T(8,128)S(1)} %all-to-all-done.parts_ref, f32[16,128]{1,0:T(8,128)S(1)} %broadcast_in_dim.4.prec_ref), custom_call_target="tpu_custom_call" | custom-call | flops 1048576 | bytes 2097152 | tf_op jit(solution)/shard_map/solve/pallas_call | solution.py:403
  41.7 6.6 %all-to-all-start.1 = ((f32[128,16,128]{2,1,0:T(8,128)}), f32[128,16,128]{2,1,0:T(8,128)S(1)}, u32[]{:S(2)}, u32[]{:S(2)}) async-start(f32[128,16,128]{2,1,0:T(8,128)} %get-tuple-element.41), calls=%async_computation.1 | async-start | bytes 2097152 | tf_op jit(solution)/shard_map/all_to_all | solution.py:417
  49.6 0.8 copy-done.20
  52.0 5.7 %count.1.counts_ref = bf16[128,128,128]{2,1,0:T(8,128)(2,1)S(1)} custom-call(s32[16,512]{1,0:T(8,128)S(1)} %copy-done.9, s32[16,512]{1,0:T(8,128)S(1)} %copy-done.8), custom_call_target="tpu_custom_call" | custom-call | flops 4294967296 | bytes 4194304 | tf_op jit(solution)/shard_map/count/pallas_call | solution.py:418
  57.7 2.0 %copy-done.2 = bf16[128,128,128]{2,1,0:T(8,128)(2,1)} copy-done((bf16[128,128,128]{2,1,0:T(8,128)(2,1)}, bf16[128,128,128]{2,1,0:T(8,128)(2,1)S(1)}, u32[]{:S(2)}) %copy-start.2) | copy-done | bytes 4194328
  59.7 7.6 %all-to-all-done.1.fitted_ref = f32[128,16,128]{2,1,0:T(8,128)S(1)} async-done(((f32[128,16,128]{2,1,0:T(8,128)}), f32[128,16,128]{2,1,0:T(8,128)S(1)}, u32[]{:S(2)}, u32[]{:S(2)}) %all-to-all-start.1) | async-done | bytes 1048608 | tf_op jit(solution)/shard_map/all_to_all | solution.py:417
  67.4 2.2 %copy-done.3 = bf16[128,128,128]{2,1,0:T(8,128)(2,1)S(1)} copy-done((bf16[128,128,128]{2,1,0:T(8,128)(2,1)S(1)}, bf16[128,128,128]{2,1,0:T(8,128)(2,1)}, u32[]{:S(2)}) %copy-start.3) | copy-done | bytes 4194328
  70.9 1.4 %map.1 = f32[16,16,128]{2,1,0:T(8,128)S(1)} custom-call(f32[128,16,128]{2,1,0:T(8,128)S(1)} %all-to-all-done.1.fitted_ref, bf16[128,128,128]{2,1,0:T(8,128)(2,1)S(1)} %copy-done.3, f32[16,128]{1,0:T(8,128)S(1)} %broadcast_in_dim.4.prec_ref, f32[16,16,128]{2,1,0:T(8,128)S(1)} %get-tuple-element.52.factor_ref, f32[16,16,128]{2,1,0:T(8,128)S(1)} %get-tuple-element.53.upper_ref, ...), custom_call_target="tpu_custom_call" | custom-call | flops 268435456 | bytes 6291456 | tf_op jit(solution)/shard_map/map/pallas_call | solution.py:445
  72.4 10.7 %all_to_all.25.rows_ref = f32[16,16,128]{2,1,0:T(8,128)S(1)} all-to-all(f32[16,16,128]{2,1,0:T(8,128)S(1)} %map.1), channel_id=1, replica_groups=mesh['y'=4,'c'=2,'tm'=16] {'tm'}, dimensions={0} | all-to-all | bytes 262144 | tf_op jit(solution)/shard_map/all_to_all | solution.py:454
  83.0 0.9 local_carry.1
  83.9 3.6 %all-to-all-start.3 = ((f32[16,32,128]{2,1,0:T(8,128)}), f32[16,32,128]{2,1,0:T(8,128)S(1)}, u32[]{:S(2)}, u32[]{:S(2)}) async-start(f32[16,32,128]{2,1,0:T(8,128)} %local_carry.1), calls=%async_computation.3 | async-start | bytes 524288 | tf_op jit(solution)/shard_map/all_to_all | solution.py:466
  87.5 2.2 %copy-done.16 = f32[2048,512]{1,0:T(8,128)S(1)} copy-done((f32[2048,512]{1,0:T(8,128)S(1)}, f32[2048,512]{1,0:T(8,128)}, u32[]{:S(2)}) %copy-start.16) | copy-done | bytes 4194328
  89.7 1.0 copy-done.21
  90.7 1.0 copy-done.23
  91.7 0.9 copy-done.25
  92.6 4.5 %local.1 = (f32[16,2048]{1,0:T(8,128)}, f32[2048,512]{1,0:T(8,128)S(1)}) custom-call(f32[2048,512]{1,0:T(8,128)S(1)} %copy-done.16, f32[16,16,128]{2,1,0:T(8,128)S(1)} %all_to_all.25.rows_ref, bf16[96,512]{1,0:T(8,128)(2,1)S(1)} %copy-done.25, bf16[512,512]{1,0:T(8,128)(2,1)S(1)} %copy-done.21, bf16[512,512]{1,0:T(8,128)(2,1)S(1)} %copy-done.23), custom_call_target="tpu_custom_call" | custom-call | flops 3145728000 | bytes 10485760 | tf_op jit(solution)/shard_map/local/pallas_call | solution.py:470
  97.2 2.0 %copy-done = f32[2048,512]{1,0:T(8,128)} copy-done((f32[2048,512]{1,0:T(8,128)}, f32[2048,512]{1,0:T(8,128)S(1)}, u32[]{:S(2)}) %copy-start) | copy-done | bytes 4194328
  99.3 14.9 %all_to_all.26.states_ref = f32[16,16,128]{2,1,0:T(8,128)S(1)} all-to-all(f32[16,16,128]{2,1,0:T(8,128)S(1)} %state.1), channel_id=1, replica_groups=mesh['y'=4,'c'=2,'tm'=16] {'tm'}, dimensions={0} | all-to-all | bytes 262144 | tf_op jit(solution)/shard_map/all_to_all | solution.py:494
  114.1 2.2 %copy-done.1 = f32[2048,512]{1,0:T(8,128)S(1)} copy-done((f32[2048,512]{1,0:T(8,128)S(1)}, f32[2048,512]{1,0:T(8,128)}, u32[]{:S(2)}) %copy-start.1) | copy-done | bytes 4194328
  116.3 2.9 %finish.1 = f32[2048,512]{1,0:T(8,128)} custom-call(f32[2048,512]{1,0:T(8,128)S(1)} %copy-done.1, f32[16,16,128]{2,1,0:T(8,128)S(1)} %all_to_all.26.states_ref, bf16[96,512]{1,0:T(8,128)(2,1)S(1)} %copy-done.6, f32[1,512]{1,0:T(1,128)S(1)} %bitcast.2), custom_call_target="tpu_custom_call" | custom-call | flops 209715200 | bytes 9437184 | tf_op jit(solution)/shard_map/finish/pallas_call | solution.py:496
  (57 shorter events, 7.8 us)
Async XLA Ops:
  10.9 28.2 %copy-start.26 = (f32[16]{0:T(128)S(1)}, f32[16]{0:T(128)}, u32[]{:S(2)}) copy-start(f32[16]{0:T(128)} %param.15) | copy-start | bytes 196
  10.9 28.1 %all-to-all-start = ((f32[16,152,128]{2,1,0:T(8,128)}), f32[16,152,128]{2,1,0:T(8,128)S(1)}, u32[]{:S(2)}, u32[]{:S(2)}) async-start(f32[16,152,128]{2,1,0:T(8,128)} %get-tuple-element.36), calls=%async_computation | async-start | bytes 2490368 | tf_op jit(solution)/shard_map/all_to_all | solution.py:396
  20.8 27.5 %copy-start.7 = (f32[16,512]{1,0:T(8,128)S(1)}, f32[16,512]{1,0:T(8,128)}, u32[]{:S(2)}) copy-start(f32[16,512]{1,0:T(8,128)} %basis_ref.4) | copy-start | bytes 98308
  20.8 27.5 %copy-start.17 = (f32[16,512]{1,0:T(8,128)S(1)}, f32[16,512]{1,0:T(8,128)}, u32[]{:S(2)}) copy-start(f32[16,512]{1,0:T(8,128)} %decay_ref.2) | copy-start | bytes 98308
  20.8 27.5 %copy-start.18 = (f32[16,512]{1,0:T(8,128)S(1)}, f32[16,512]{1,0:T(8,128)}, u32[]{:S(2)}) copy-start(f32[16,512]{1,0:T(8,128)} %load_ref.1) | copy-start | bytes 98308
  20.8 27.5 %copy-start.19 = (f32[16,512]{1,0:T(8,128)S(1)}, f32[16,512]{1,0:T(8,128)}, u32[]{:S(2)}) copy-start(f32[16,512]{1,0:T(8,128)} %feed_ref.3) | copy-start | bytes 98308
  41.7 25.6 %all-to-all-start.1 = ((f32[128,16,128]{2,1,0:T(8,128)}), f32[128,16,128]{2,1,0:T(8,128)S(1)}, u32[]{:S(2)}, u32[]{:S(2)}) async-start(f32[128,16,128]{2,1,0:T(8,128)} %get-tuple-element.41), calls=%async_computation.1 | async-start | bytes 2097152 | tf_op jit(solution)/shard_map/all_to_all | solution.py:417
  48.3 3.6 %copy-start.8 = (s32[16,512]{1,0:T(8,128)S(1)}, s32[16,512]{1,0:T(8,128)}, u32[]{:S(2)}) copy-start(s32[16,512]{1,0:T(8,128)} %and.19.low_ref) | copy-start | bytes 98308
  48.4 3.6 %copy-start.9 = (s32[16,512]{1,0:T(8,128)S(1)}, s32[16,512]{1,0:T(8,128)}, u32[]{:S(2)}) copy-start(s32[16,512]{1,0:T(8,128)} %select_add_fusion.code_ref) | copy-start | bytes 98308
  49.6 0.8 copy-start.20
  50.5 0.8 copy-start.22
  52.0 31.0 %copy-start.4 = (f32[16,272,128]{2,1,0:T(8,128)S(1)}, f32[16,272,128]{2,1,0:T(8,128)}, u32[]{:S(2)}) copy-start(f32[16,272,128]{2,1,0:T(8,128)} %get-tuple-element.56.crossed_ref) | copy-start | bytes 6684676
  57.7 2.0 %copy-start.2 = (bf16[128,128,128]{2,1,0:T(8,128)(2,1)}, bf16[128,128,128]{2,1,0:T(8,128)(2,1)S(1)}, u32[]{:S(2)}) copy-start(bf16[128,128,128]{2,1,0:T(8,128)(2,1)S(1)} %count.1.counts_ref) | copy-start | bytes 12582916
  59.7 23.3 %copy-start.10 = (f32[16,128]{1,0:T(8,128)S(1)}, f32[16,128]{1,0:T(8,128)}, u32[]{:S(2)}) copy-start(f32[16,128]{1,0:T(8,128)} %get-tuple-element.57.decayed_ref) | copy-start | bytes 24580
  67.4 2.2 %copy-start.3 = (bf16[128,128,128]{2,1,0:T(8,128)(2,1)S(1)}, bf16[128,128,128]{2,1,0:T(8,128)(2,1)}, u32[]{:S(2)}) copy-start(bf16[128,128,128]{2,1,0:T(8,128)(2,1)} %copy-done.2) | copy-start | bytes 12582916
  83.9 15.3 %all-to-all-start.3 = ((f32[16,32,128]{2,1,0:T(8,128)}), f32[16,32,128]{2,1,0:T(8,128)S(1)}, u32[]{:S(2)}, u32[]{:S(2)}) async-start(f32[16,32,128]{2,1,0:T(8,128)} %local_carry.1), calls=%async_computation.3 | async-start | bytes 524288 | tf_op jit(solution)/shard_map/all_to_all | solution.py:466
  87.5 2.2 %copy-start.16 = (f32[2048,512]{1,0:T(8,128)S(1)}, f32[2048,512]{1,0:T(8,128)}, u32[]{:S(2)}) copy-start(f32[2048,512]{1,0:T(8,128)} %get-tuple-element.35.marked_ref) | copy-start | bytes 12582916
  89.7 1.0 copy-start.21
  90.7 1.0 copy-start.23
  91.7 0.9 copy-start.25
  92.6 21.5 %copy-start.6 = (bf16[96,512]{1,0:T(8,128)(2,1)S(1)}, bf16[96,512]{1,0:T(8,128)(2,1)}, u32[]{:S(2)}) copy-start(bf16[96,512]{1,0:T(8,128)(2,1)} %copy-done.5) | copy-start | bytes 294916
  92.6 21.5 %copy-start.15 = (f32[512]{0:T(512)S(1)}, f32[512]{0:T(512)}, u32[]{:S(2)}) copy-start(f32[512]{0:T(512)} %param.19) | copy-start | bytes 6148
  97.2 2.0 %copy-start = (f32[2048,512]{1,0:T(8,128)}, f32[2048,512]{1,0:T(8,128)S(1)}, u32[]{:S(2)}) copy-start(f32[2048,512]{1,0:T(8,128)S(1)} %get-tuple-element.65.local_ref) | copy-start | bytes 12582916
  114.1 2.2 %copy-start.1 = (f32[2048,512]{1,0:T(8,128)S(1)}, f32[2048,512]{1,0:T(8,128)}, u32[]{:S(2)}) copy-start(f32[2048,512]{1,0:T(8,128)} %copy-done) | copy-start | bytes 12582916
  (6 other events, 3.9 us)

commit v2 on v1

--- a/solution.py
+++ b/solution.py
@@ -13,11 +13,14 @@
 PAIRS = 136
 OWN = 128
 CUT = 128
-STEP = 256
+STEP = 512
+AHEAD = 2
+CROSS_STEP = 512
+CROSS_CHUNKS = CROSS_STEP // OWN
 CHUNKS = STEP // OWN
 GRAM_ROWS = PAIRS + 16
 CROSS_ROWS = 16 + BASIS_VECTORS * NOISE_TERMS
-WHITEN_STEP = 512
+WHITEN_STEP = 1024
 WHITEN_CHUNKS = WHITEN_STEP // OWN
 
 F32 = jnp.float32
@@ -75,43 +78,59 @@
     return sums[0][0:16] + (mid + total)
 
 
-def gram_kernel(flux_ref, valid_ref, quality_ref, basis_ref, out_ref, marked_ref, table_ref):
+def gram_kernel(
+    flux_hbm, valid_hbm, quality_hbm, basis_ref, out_ref, flux_ref, valid_ref, quality_ref, table_ref, arrived
+):
     wide = DIAGONALS * BASIS_VECTORS
     rights = 3 * wide
-
-    @pl.when(pl.program_id(0) == 0)
-    def _():
-        basis = basis_ref[...]
-        scaled = basis * (1.0 / 12.0)
-        products = []
-        for diagonal in range(DIAGONALS):
-            turned = basis
-            if diagonal:
-                turned = jnp.concatenate([basis[diagonal:], basis[:diagonal]], axis=0)
-            products.append(scaled * turned)
-        for place, piece in enumerate(split3(jnp.concatenate(products, axis=0))):
-            table_ref[place * wide : (place + 1) * wide, :] = piece
-        for place, piece in enumerate(split3(scaled)):
-            table_ref[rights + place * 16 : rights + place * 16 + 16, :] = piece
-
-    flux = flux_ref[...]
-    quality = quality_ref[...]
-    usable = valid_ref[...] != 0
-    marked_ref[...] = jnp.where(usable, flux, jnp.nan)
-    twelfths = jnp.where(
-        quality == 0, 12.0, jnp.where(quality == 1, 6.0, jnp.where(quality == 2, 4.0, 3.0))
-    )
-    weight = jnp.where(usable, twelfths, 0.0)
-    grams = dot_nt(table_ref[0:rights, :], weight.astype(BF16))
-    gram = grams[0:PAIRS] + (grams[wide : wide + PAIRS] + grams[2 * wide : 2 * wide + PAIRS])
-    right = narrow_dots(table_ref, rights, weight * flux, 3)
-    for chunk in range(CHUNKS):
-        lanes = slice(chunk * OWN, (chunk + 1) * OWN)
-        out_ref[chunk, 0:PAIRS, :] = gram[:, lanes]
-        out_ref[chunk, PAIRS:GRAM_ROWS, :] = right[:, lanes]
-
-
-def cross_kernel(marked_ref, basis_ref, decay_ref, feed_ref, out_ref, decayed_ref, table_ref):
+    steps = flux_ref.shape[0] // STEP
+    pairs = ((flux_hbm, flux_ref), (valid_hbm, valid_ref), (quality_hbm, quality_ref))
+
+    def arrival(which, step):
+        source, target = pairs[which]
+        stars = pl.ds(step * STEP, STEP)
+        return pltpu.make_async_copy(source.at[stars], target.at[stars], arrived.at[which, step])
+
+    for step in range(AHEAD):
+        for which in range(3):
+            arrival(which, step).start()
+
+    basis = basis_ref[...]
+    scaled = basis * (1.0 / 12.0)
+    products = []
+    for diagonal in range(DIAGONALS):
+        turned = basis
+        if diagonal:
+            turned = jnp.concatenate([basis[diagonal:], basis[:diagonal]], axis=0)
+        products.append(scaled * turned)
+    for place, piece in enumerate(split3(jnp.concatenate(products, axis=0))):
+        table_ref[place * wide : (place + 1) * wide, :] = piece
+    for place, piece in enumerate(split3(scaled)):
+        table_ref[rights + place * 16 : rights + place * 16 + 16, :] = piece
+
+    for step in range(steps):
+        for which in range(3):
+            arrival(which, step).wait()
+            if step + AHEAD < steps:
+                arrival(which, step + AHEAD).start()
+        stars = slice(step * STEP, (step + 1) * STEP)
+        quality = quality_ref[stars, :]
+        twelfths = jnp.where(
+            quality == 0, 12.0, jnp.where(quality == 1, 6.0, jnp.where(quality == 2, 4.0, 3.0))
+        )
+        weight = jnp.where(valid_ref[stars, :] != 0, twelfths, 0.0)
+        grams = dot_nt(table_ref[0:rights, :], weight.astype(BF16))
+        gram = grams[0:PAIRS] + (grams[wide : wide + PAIRS] + grams[2 * wide : 2 * wide + PAIRS])
+        right = narrow_dots(table_ref, rights, weight * flux_ref[stars, :], 3)
+        for chunk in range(CHUNKS):
+            lanes = slice(chunk * OWN, (chunk + 1) * OWN)
+            out_ref[step * CHUNKS + chunk, 0:PAIRS, :] = gram[:, lanes]
+            out_ref[step * CHUNKS + chunk, PAIRS:GRAM_ROWS, :] = right[:, lanes]
+
+
+def cross_kernel(
+    flux_ref, valid_ref, basis_ref, decay_ref, feed_ref, out_ref, decayed_ref, marked_ref, table_ref
+):
     cross = BASIS_VECTORS * NOISE_TERMS
     feeds = 2 * cross
 
@@ -133,12 +152,13 @@
         for place, piece in enumerate(split3(feed)):
             table_ref[feeds + place * 16 : feeds + place * 16 + 16, :] = piece
 
-    marked = marked_ref[...]
-    usable = marked == marked
+    usable = valid_ref[...] != 0
+    flux = flux_ref[...]
+    marked_ref[...] = jnp.where(usable, flux, jnp.nan)
     sums = dot_nt(table_ref[0:feeds, :], jnp.where(usable, 1.0, 0.0).astype(BF16))
     crossed = sums[0:cross] + sums[cross : 2 * cross]
-    plain = narrow_dots(table_ref, feeds, jnp.where(usable, marked, 0.0), 2)
-    for chunk in range(CHUNKS):
+    plain = narrow_dots(table_ref, feeds, jnp.where(usable, flux, 0.0), 2)
+    for chunk in range(CROSS_CHUNKS):
         lanes = slice(chunk * OWN, (chunk + 1) * OWN)
         out_ref[chunk, 0:16, :] = plain[:, lanes]
         out_ref[chunk, 16:CROSS_ROWS, :] = crossed[:, lanes]
@@ -247,13 +267,13 @@
     return solved
 
 
-def solve_kernel(parts_ref, prec_ref, fitted_ref, factor_ref, upper_ref, pivot_ref, right_ref, sums_ref, matrix_ref):
+def solve_kernel(parts_ref, prec_ref, fitted_ref, kept_ref, sums_ref, matrix_ref):
     total = parts_ref[0]
     for part in range(1, parts_ref.shape[0]):
         total = total + parts_ref[part]
     sums_ref[...] = total
     right = total[PAIRS : PAIRS + 16]
-    right_ref[...] = right
+    kept_ref[33] = right
     order = BASIS_VECTORS
     for j in range(order):
         for i in range(order):
@@ -270,25 +290,25 @@
     weighted = [jnp.where(rows == j, plain[j] + prec, plain[j]) for j in range(order)]
     factors, pivots, ignored, uppers = eliminate(weighted, None)
     for k in range(order):
-        factor_ref[k] = factors[k]
-        upper_ref[k] = uppers[k]
-        pivot_ref[k : k + 1, :] = pivots[k]
-
-
-def map_kernel(
-    fitted_ref, counts_ref, prec_ref, factor_ref, upper_ref, pivot_ref, right_ref, out_ref
-):
+        kept_ref[k] = factors[k]
+        kept_ref[16 + k] = uppers[k]
+        kept_ref[32, k : k + 1, :] = pivots[k]
+
+
+def map_kernel(near_ref, far_ref, counts_ref, prec_ref, kept_ref, out_ref):
+    half = near_ref.shape[0]
     prior = jnp.zeros((48, OWN), F32)
-    for place in range(0, fitted_ref.shape[0], 2):
-        wide = jnp.concatenate([fitted_ref[place], fitted_ref[place + 1]], axis=1)
-        listed = jnp.concatenate([counts_ref[place], counts_ref[place + 1]], axis=1)
+    for spot in range(0, 2 * half, 2):
+        table_ref, place = (near_ref, spot) if spot < half else (far_ref, spot - half)
+        wide = jnp.concatenate([table_ref[place], table_ref[place + 1]], axis=1)
+        listed = jnp.concatenate([counts_ref[spot], counts_ref[spot + 1]], axis=1)
         prior = prior + dot_nt(jnp.concatenate(split3(wide), axis=0), listed)
     prior_mean = (prior[0:16] + (prior[16:32] + prior[32:48])) * (1.0 / NEIGH)
-    vector = right_ref[...] + prec_ref[...] * prior_mean
+    vector = kept_ref[33] + prec_ref[...] * prior_mean
     for k in range(BASIS_VECTORS):
-        vector = vector - factor_ref[k] * vector[k : k + 1, :]
-    uppers = [upper_ref[k] for k in range(BASIS_VECTORS)]
-    pivots = [pivot_ref[k : k + 1, :] for k in range(BASIS_VECTORS)]
+        vector = vector - kept_ref[k] * vector[k : k + 1, :]
+    uppers = [kept_ref[16 + k] for k in range(BASIS_VECTORS)]
+    pivots = [kept_ref[32, k : k + 1, :] for k in range(BASIS_VECTORS)]
     coeffs = back_substitute(vector, uppers, pivots)
     for peer in range(out_ref.shape[0]):
         out_ref[peer] = coeffs
@@ -312,12 +332,17 @@
         state = state * carry_ref[block, 16:32, :] + carry_ref[block, 0:16, :]
 
 
-def local_kernel(marked_ref, rows_ref, stack_ref, high_ref, low_ref, coeffs_ref, out_ref):
+def whiten_kernel(
+    marked_ref, rows_ref, states_ref, stack_ref, entry_ref, high_ref, low_ref, scale_ref, coeffs_ref, out_ref
+):
     coeffs = jnp.concatenate([rows_ref[chunk] for chunk in range(WHITEN_CHUNKS)], axis=1)
+    states = jnp.concatenate([states_ref[chunk] for chunk in range(WHITEN_CHUNKS)], axis=1)
     coeffs_ref[...] = coeffs
     trend = dot_tn(left_stack(coeffs), stack_ref[...])
-    marked = marked_ref[...]
+    first = pl.multiple_of(pl.program_id(0) * WHITEN_STEP, WHITEN_STEP)
+    marked = marked_ref[pl.ds(first, WHITEN_STEP), :]
     residual = jnp.where(marked == marked, marked - trend, 0.0)
+    incoming = dot_tn(left_stack(states), entry_ref[...])
     high = residual.astype(BF16)
     low = (residual - high.astype(F32)).astype(BF16)
     count = residual.shape[1]
@@ -326,13 +351,7 @@
         upto = slice(0, first + 256)
         local = dot_nn(low[:, upto], high_ref[upto, lanes]) + dot_nn(high[:, upto], low_ref[upto, lanes])
         local = local + dot_nn(high[:, upto], high_ref[upto, lanes])
-        out_ref[:, lanes] = residual[:, lanes] - local
-
-
-def finish_kernel(local_ref, states_ref, entry_ref, scale_ref, out_ref):
-    states = jnp.concatenate([states_ref[chunk] for chunk in range(WHITEN_CHUNKS)], axis=1)
-    incoming = dot_tn(left_stack(states), entry_ref[...])
-    out_ref[...] = (local_ref[...] - incoming) * scale_ref[...]
+        out_ref[:, lanes] = (residual[:, lanes] - local - incoming[:, lanes]) * scale_ref[:, lanes]
 
 
 def vmem():
@@ -352,69 +371,73 @@
 ):
     stars, cadences = flux.shape
     blocks = stars // OWN
-    steps = stars // STEP
     place = lax.axis_index("tm")
     prec = jnp.broadcast_to(prior_prec[:, None], (BASIS_VECTORS, OWN))
 
     listed = lax.dynamic_slice_in_dim(neighbours, place * OWN, OWN, 0).reshape(blocks, -1)
-    code = (listed >> 7) * 8 + lax.broadcasted_iota(jnp.int32, listed.shape, 1) // NEIGH
-
-    wide_spec = pl.BlockSpec((STEP, cadences), lambda i: (i, 0))
-    table_spec = pl.BlockSpec((16, cadences), lambda i: (0, 0))
-    parts, marked = pl.pallas_call(
+    low_bits = listed & 127
+    owner = listed >> 7
+    spot = (owner & 15) + 16 * (owner >> 5) + 64 * (((owner >> 4) & 1) ^ lax.axis_index("c"))
+    code = spot * 8 + lax.broadcasted_iota(jnp.int32, listed.shape, 1) // NEIGH
+
+    in_hbm = pl.BlockSpec(memory_space=pl.ANY)
+    parts = pl.pallas_call(
         gram_kernel,
-        grid=(steps,),
-        in_specs=[wide_spec, wide_spec, wide_spec, table_spec],
-        out_specs=[pl.BlockSpec((CHUNKS, GRAM_ROWS, OWN), lambda i: (i, 0, 0)), wide_spec],
-        out_shape=[
-            jax.ShapeDtypeStruct((blocks, GRAM_ROWS, OWN), F32),
-            jax.ShapeDtypeStruct((stars, cadences), F32),
+        in_specs=[in_hbm] * 3 + [vmem()],
+        out_specs=vmem(),
+        out_shape=jax.ShapeDtypeStruct((blocks, GRAM_ROWS, OWN), F32),
+        scratch_shapes=[
+            pltpu.VMEM((stars, cadences), F32),
+            pltpu.VMEM((stars, cadences), jnp.int32),
+            pltpu.VMEM((stars, cadences), jnp.int32),
+            pltpu.VMEM((480, cadences), BF16),
+            pltpu.SemaphoreType.DMA((3, stars // STEP)),
         ],
-        scratch_shapes=[pltpu.VMEM((480, cadences), BF16)],
-        compiler_params=params(56),
-        cost_estimate=cost(2 * stars * cadences * 600, 18 * MIB),
+        compiler_params=params(58),
+        cost_estimate=cost(2 * stars * cadences * 600, 14 * MIB),
         name="gram",
     )(flux, valid, quality, basis)
 
-    crossed, decayed = pl.pallas_call(
+    parts, later_basis, later_decay = lax.optimization_barrier((parts, basis, decay))
+    cross_spec = pl.BlockSpec((CROSS_STEP, cadences), lambda i: (i, 0))
+    table_spec = pl.BlockSpec((16, cadences), lambda i: (0, 0))
+    crossed, decayed, marked = pl.pallas_call(
         cross_kernel,
-        grid=(steps,),
-        in_specs=[wide_spec, table_spec, table_spec, table_spec],
+        grid=(stars // CROSS_STEP,),
+        in_specs=[cross_spec, cross_spec, table_spec, table_spec, table_spec],
         out_specs=[
-            pl.BlockSpec((CHUNKS, CROSS_ROWS, OWN), lambda i: (i, 0, 0)),
+            pl.BlockSpec((CROSS_CHUNKS, CROSS_ROWS, OWN), lambda i: (i, 0, 0)),
             pl.BlockSpec((NOISE_TERMS, OWN), lambda i: (0, 0)),
+            cross_spec,
         ],
         out_shape=[
             jax.ShapeDtypeStruct((blocks, CROSS_ROWS, OWN), F32),
             jax.ShapeDtypeStruct((NOISE_TERMS, OWN), F32),
+            jax.ShapeDtypeStruct((stars, cadences), F32),
         ],
         scratch_shapes=[pltpu.VMEM((560, cadences), BF16)],
-        compiler_params=params(56),
-        cost_estimate=cost(2 * stars * cadences * 800, 8 * MIB),
+        compiler_params=params(58),
+        cost_estimate=cost(2 * stars * cadences * 800, 16 * MIB),
         name="cross",
-    )(marked, basis, decay, feed_w)
+    )(flux, valid, later_basis, later_decay, feed_w)
     parts = lax.all_to_all(parts, "tm", 0, 0, tiled=True)
-    parts, crossed, decayed = lax.optimization_barrier((parts, crossed, decayed))
-
-    square = jax.ShapeDtypeStruct((16, 16, OWN), F32)
-    flat = jax.ShapeDtypeStruct((16, OWN), F32)
-    everyone = ("y", "c", "tm")
-    copies = jax.ShapeDtypeStruct((lax.axis_size(everyone), 16, OWN), F32)
-    fitted, factor, upper, pivot, right = pl.pallas_call(
+    parts, crossed, decayed, marked = lax.optimization_barrier((parts, crossed, decayed, marked))
+
+    nearby = ("y", "tm")
+    copies = jax.ShapeDtypeStruct((lax.axis_size(nearby), 16, OWN), F32)
+    fitted, kept = pl.pallas_call(
         solve_kernel,
         in_specs=[vmem()] * 2,
-        out_specs=[vmem()] * 5,
-        out_shape=[copies, square, square, flat, flat],
+        out_specs=[vmem()] * 2,
+        out_shape=[copies, jax.ShapeDtypeStruct((34, 16, OWN), F32)],
         scratch_shapes=[pltpu.VMEM((GRAM_ROWS, OWN), F32), pltpu.VMEM((256, OWN), F32)],
         compiler_params=params(16),
         cost_estimate=cost(1 << 20, 2 * MIB),
         name="solve",
     )(parts, prec)
 
-    fitted, later_code, later_low, later_decay, later_basis = lax.optimization_barrier(
-        (fitted, code, listed & 127, decay, basis)
-    )
-    fitted = lax.all_to_all(fitted, everyone, 0, 0, tiled=True)
+    fitted, later_code, later_low = lax.optimization_barrier((fitted, code, low_bits))
+    near = lax.all_to_all(fitted, nearby, 0, 0, tiled=True)
     counts = pl.pallas_call(
         count_kernel,
         in_specs=[vmem(), vmem()],
@@ -424,6 +447,42 @@
         cost_estimate=cost(4 << 30, 4 * MIB),
         name="count",
     )(later_code, later_low)
+    near, counts = lax.optimization_barrier((near, counts))
+    far = lax.ppermute(near, "c", [(0, 1), (1, 0)])
+
+    rows = pl.pallas_call(
+        map_kernel,
+        in_specs=[vmem()] * 5,
+        out_specs=vmem(),
+        out_shape=jax.ShapeDtypeStruct((blocks, 16, OWN), F32),
+        compiler_params=params(16),
+        cost_estimate=cost(1 << 28, 6 * MIB),
+        name="map",
+    )(near, far, counts, prec, kept)
+    rows = lax.all_to_all(rows, "tm", 0, 0, tiled=True)
+
+    carries = pl.pallas_call(
+        carry_kernel,
+        in_specs=[vmem()] * 3,
+        out_specs=vmem(),
+        out_shape=jax.ShapeDtypeStruct((blocks, 32, OWN), F32),
+        compiler_params=params(16),
+        cost_estimate=cost(1 << 24, 3 * MIB),
+        name="local_carry",
+    )(rows, crossed, decayed)
+    carries = lax.all_to_all(carries, "tm", 0, 0, tiled=True)
+    states = pl.pallas_call(
+        state_kernel,
+        in_specs=[vmem()],
+        out_specs=vmem(),
+        out_shape=jax.ShapeDtypeStruct((blocks, 16, OWN), F32),
+        compiler_params=params(16),
+        cost_estimate=cost(1 << 20, MIB),
+        name="state",
+    )(carries)
+    states = lax.all_to_all(states, "tm", 0, 0, tiled=True)
+
+    states, last_decay, last_basis = lax.optimization_barrier((states, decay, basis))
     high, low, entry, stack = pl.pallas_call(
         noise_kernel,
         in_specs=[vmem()] * 4,
@@ -437,72 +496,24 @@
         compiler_params=params(16),
         cost_estimate=cost(2 << 30, 2 * MIB),
         name="noise",
-    )(later_decay, load_u, feed_w, later_basis)
-    fitted, counts, high, low, entry, stack = lax.optimization_barrier(
-        (fitted, counts, high, low, entry, stack)
-    )
-
-    rows = pl.pallas_call(
-        map_kernel,
-        in_specs=[vmem()] * 7,
-        out_specs=vmem(),
-        out_shape=jax.ShapeDtypeStruct((blocks, 16, OWN), F32),
-        compiler_params=params(16),
-        cost_estimate=cost(1 << 28, 6 * MIB),
-        name="map",
-    )(fitted, counts, prec, factor, upper, pivot, right)
-    rows = lax.all_to_all(rows, "tm", 0, 0, tiled=True)
-
-    carries = pl.pallas_call(
-        carry_kernel,
-        in_specs=[vmem()] * 3,
-        out_specs=vmem(),
-        out_shape=jax.ShapeDtypeStruct((blocks, 32, OWN), F32),
-        compiler_params=params(16),
-        cost_estimate=cost(1 << 24, 3 * MIB),
-        name="local_carry",
-    )(rows, crossed, decayed)
-    carries, later_rows = lax.optimization_barrier((carries, rows))
-    carries = lax.all_to_all(carries, "tm", 0, 0, tiled=True)
-
+    )(last_decay, load_u, feed_w, last_basis)
     part_spec = pl.BlockSpec((WHITEN_CHUNKS, 16, OWN), lambda i: (i, 0, 0))
-    tall_spec = pl.BlockSpec((WHITEN_STEP, cadences), lambda i: (i, 0))
-    coeffs, local = pl.pallas_call(
-        local_kernel,
+    coeffs, whitened = pl.pallas_call(
+        whiten_kernel,
         grid=(stars // WHITEN_STEP,),
-        in_specs=[tall_spec, part_spec, vmem(), vmem(), vmem()],
-        out_specs=[pl.BlockSpec((16, WHITEN_STEP), lambda i: (0, i)), tall_spec],
+        in_specs=[vmem(), part_spec, part_spec] + [vmem()] * 5,
+        out_specs=[
+            pl.BlockSpec((16, WHITEN_STEP), lambda i: (0, i)),
+            pl.BlockSpec((WHITEN_STEP, cadences), lambda i: (i, 0)),
+        ],
         out_shape=[
             jax.ShapeDtypeStruct((16, stars), F32),
             jax.ShapeDtypeStruct((stars, cadences), F32),
         ],
-        compiler_params=params(16),
-        cost_estimate=cost(2 * stars * cadences * 1500, 10 * MIB),
-        name="local",
-    )(marked, later_rows, stack, high, low)
-    carries, local = lax.optimization_barrier((carries, local))
-
-    states = pl.pallas_call(
-        state_kernel,
-        in_specs=[vmem()],
-        out_specs=vmem(),
-        out_shape=jax.ShapeDtypeStruct((blocks, 16, OWN), F32),
-        compiler_params=params(16),
-        cost_estimate=cost(1 << 20, MIB),
-        name="state",
-    )(carries)
-    states = lax.all_to_all(states, "tm", 0, 0, tiled=True)
-
-    whitened = pl.pallas_call(
-        finish_kernel,
-        grid=(stars // WHITEN_STEP,),
-        in_specs=[tall_spec, part_spec, vmem(), vmem()],
-        out_specs=tall_spec,
-        out_shape=jax.ShapeDtypeStruct((stars, cadences), F32),
-        compiler_params=params(16),
-        cost_estimate=cost(2 * stars * cadences * 100, 9 * MIB),
-        name="finish",
-    )(local, states, entry, inv_diag[None, :])
+        compiler_params=params(32),
+        cost_estimate=cost(2 * stars * cadences * 1700, 14 * MIB),
+        name="whiten",
+    )(marked, rows, states, stack, entry, high, low, inv_diag[None, :])
     return coeffs.T, whitened
 
 

time: 120 us -> 103 us (0.86)
  local copies, waits for them, and re-layouts: 20.1 us -> 4.58 us
  blocking collectives: 25.5 us -> 34.3 us
  Pallas kernels: 36 us -> 30.2 us
  starting transfers between devices: 18.3 us -> 14.9 us
    unnamed x54 -> x22, local copies, waits for them, and re-layouts: 19.1 us -> 4.17 us
    all_to_all x0 -> x1, blocking collectives: none -> 11.9 us  [per_device(): carries = lax.all_to_all(carries, 'tm', 0, 0, tiled=True)]
    pallas_call x5 -> x4, Pallas kernels: 27.3 us -> 22.3 us  [the longest x1 7.82 us: per_device(): pl.pallas_call(gram_kernel, in_specs=[in_hbm] * 3 + [vmem()], out_specs=v...]
    all_to_all x2 -> x1, waiting for transfers between devices: 7.65 us -> 4.15 us  [per_device(): near = lax.all_to_all(fitted, nearby, 0, 0, tiled=True)]
    all_to_all x1, blocking collectives: 14.9 us -> 11.6 us  [per_device(): states = lax.all_to_all(states, 'tm', 0, 0, tiled=True)]
    all_to_all x2 -> x1, starting transfers between devices: 10.2 us -> 6.93 us  [per_device(): near = lax.all_to_all(fitted, nearby, 0, 0, tiled=True)]
    ppermute x0 -> x1, waiting for transfers between devices: none -> 1.91 us  [per_device(): far = lax.ppermute(near, 'c', [(0, 1), (1, 0)])]
    all_to_all x1, waiting for transfers between devices: 9.47 us -> 11.1 us  [per_device(): parts = lax.all_to_all(parts, 'tm', 0, 0, tiled=True)]
  transfers between devices with their start and end apart: 3 -> 3, of which waited for: 2 -> 3; matrix products, arithmetic and copies ran while one was open for 2% -> 1% of each run, Pallas kernels for 16% -> 13%
where the time goes in v2:
time: 103 us
  blocking collectives  34.3 us (33%)
  Pallas kernels  30.2 us (29%)
  waiting for transfers between devices  17.2 us (17%)
  starting transfers between devices  14.9 us (14%)
  local copies, waits for them, and re-layouts  4.58 us (4%)
    all_to_all x1, blocking collectives, per_device(): carries = lax.all_to_all(carries, 'tm', 0, 0, tiled=True)  11.9 us
    all_to_all x1, blocking collectives, per_device(): states = lax.all_to_all(states, 'tm', 0, 0, tiled=True)  11.6 us
    all_to_all x1, waiting for transfers between devices, per_device(): parts = lax.all_to_all(parts, 'tm', 0, 0, tiled=True)  11.1 us
    all_to_all x1, blocking collectives, per_device(): rows = lax.all_to_all(rows, 'tm', 0, 0, tiled=True)  10.8 us
    all_to_all x1, starting transfers between devices, per_device(): parts = lax.all_to_all(parts, 'tm', 0, 0, tiled=True)  7.98 us
    pallas_call x1, Pallas kernels, per_device(): pl.pallas_call(gram_kernel, in_specs=[in_hbm] * 3 + [vmem()], out_specs=v...  7.82 us
    pallas_call x1, Pallas kernels, per_device(): pl.pallas_call(cross_kernel, grid=(stars // CROSS_STEP,), in_specs=[cross...  7.75 us
    all_to_all x1, starting transfers between devices, per_device(): near = lax.all_to_all(fitted, nearby, 0, 0, tiled=True)  6.93 us
  transfers between devices with their start and end apart: 3, of which 3 were waited for; matrix products, arithmetic and copies ran while one was open for 1% of the time, Pallas kernels for 13%

profile of v2, /device:TPU:0, one launch (start us, length us, event | category | flops | bytes accessed | tf_op | source)
XLA Modules:
  0.0 102.7 jit_solution(6590802961141641404)
XLA Ops:
  0.6 7.8 %gram.1 = f32[16,152,128]{2,1,0:T(8,128)} custom-call(f32[2048,512]{1,0:T(8,128)} %flux_ref.1, s32[2048,512]{1,0:T(8,128)} %valid_ref.1, s32[2048,512]{1,0:T(8,128)} %quality_hbm.1, f32[16,512]{1,0:T(8,128)} %basis_ref.3), custom_call_target="tpu_custom_call" | custom-call | flops 1258291200 | bytes 14680064 | tf_op jit(solution)/shard_map/gram/pallas_call | solution.py:384
  8.5 8.0 %all-to-all-start = ((f32[16,152,128]{2,1,0:T(8,128)}), f32[16,152,128]{2,1,0:T(8,128)S(1)}, u32[]{:S(2)}, u32[]{:S(2)}) async-start(f32[16,152,128]{2,1,0:T(8,128)} %gram.1), calls=%async_computation | async-start | bytes 2490368 | tf_op jit(solution)/shard_map/all_to_all | solution.py:423
  16.4 0.8 dynamic-slice_and_fusion
  17.2 0.1 copy.15
  17.3 0.1 and.38.low_ref
  17.4 0.1 copy.14
  17.5 0.1 reshape.27
  17.6 7.8 %cross.1 = (f32[16,272,128]{2,1,0:T(8,128)}, f32[16,128]{1,0:T(8,128)}, f32[2048,512]{1,0:T(8,128)}) custom-call(f32[2048,512]{1,0:T(8,128)} %flux_ref.1, s32[2048,512]{1,0:T(8,128)} %valid_ref.1, f32[16,512]{1,0:T(8,128)} %basis_ref.3, f32[16,512]{1,0:T(8,128)} %decay_ref.1, f32[16,512]{1,0:T(8,128)} %feed_ref.3), custom_call_target="tpu_custom_call" | custom-call | flops 1677721600 | bytes 16777216 | tf_op jit(solution)/shard_map/cross/pallas_call | solution.py:404
  25.4 11.1 %all-to-all-done.parts_ref = f32[16,152,128]{2,1,0:T(8,128)S(1)} async-done(((f32[16,152,128]{2,1,0:T(8,128)}), f32[16,152,128]{2,1,0:T(8,128)S(1)}, u32[]{:S(2)}, u32[]{:S(2)}) %all-to-all-start) | async-done | bytes 1245216 | tf_op jit(solution)/shard_map/all_to_all | solution.py:423
  36.5 0.1 broadcast_in_dim.4.prec_ref
  36.6 1.2 %solve.1 = (f32[64,16,128]{2,1,0:T(8,128)}, f32[34,16,128]{2,1,0:T(8,128)S(1)}) custom-call(f32[16,152,128]{2,1,0:T(8,128)S(1)} %all-to-all-done.parts_ref, f32[16,128]{1,0:T(8,128)S(1)} %broadcast_in_dim.4.prec_ref), custom_call_target="tpu_custom_call" | custom-call | flops 1048576 | bytes 2097152 | tf_op jit(solution)/shard_map/solve/pallas_call | solution.py:428
  37.8 6.9 %all-to-all-start.1 = ((f32[64,16,128]{2,1,0:T(8,128)}), f32[64,16,128]{2,1,0:T(8,128)S(1)}, u32[]{:S(2)}, u32[]{:S(2)}) async-start(f32[64,16,128]{2,1,0:T(8,128)} %get-tuple-element.37), calls=%async_computation.1 | async-start | bytes 1048576 | tf_op jit(solution)/shard_map/all_to_all | solution.py:440
  44.7 5.8 %count.1.counts_ref = bf16[128,128,128]{2,1,0:T(8,128)(2,1)S(1)} custom-call(s32[16,512]{1,0:T(8,128)S(1)} %select_add_fusion.code_ref, s32[16,512]{1,0:T(8,128)S(1)} %and.38.low_ref), custom_call_target="tpu_custom_call" | custom-call | flops 4294967296 | bytes 4194304 | tf_op jit(solution)/shard_map/count/pallas_call | solution.py:441
  50.5 1.9 %copy-done = bf16[128,128,128]{2,1,0:T(8,128)(2,1)} copy-done((bf16[128,128,128]{2,1,0:T(8,128)(2,1)}, bf16[128,128,128]{2,1,0:T(8,128)(2,1)S(1)}, u32[]{:S(2)}) %copy-start) | copy-done | bytes 4194328
  52.4 4.2 %all-to-all-done.1.near_ref = f32[64,16,128]{2,1,0:T(8,128)S(1)} async-done(((f32[64,16,128]{2,1,0:T(8,128)}), f32[64,16,128]{2,1,0:T(8,128)S(1)}, u32[]{:S(2)}, u32[]{:S(2)}) %all-to-all-start.1) | async-done | bytes 524320 | tf_op jit(solution)/shard_map/all_to_all | solution.py:440
  56.6 1.9 %collective-permute-done.far_ref = f32[64,16,128]{2,1,0:T(8,128)S(1)} collective-permute-done((f32[64,16,128]{2,1,0:T(8,128)S(1)}, f32[64,16,128]{2,1,0:T(8,128)S(1)}, u32[]{:S(2)}, u32[]{:S(2)}) %collective-permute-start) | collective-permute-done | bytes 524320 | tf_op jit(solution)/shard_map/ppermute | solution.py:451
  58.5 2.2 %copy-done.1 = bf16[128,128,128]{2,1,0:T(8,128)(2,1)S(1)} copy-done((bf16[128,128,128]{2,1,0:T(8,128)(2,1)S(1)}, bf16[128,128,128]{2,1,0:T(8,128)(2,1)}, u32[]{:S(2)}) %copy-start.1) | copy-done | bytes 4194328
  60.7 1.4 %map.1 = f32[16,16,128]{2,1,0:T(8,128)S(1)} custom-call(f32[64,16,128]{2,1,0:T(8,128)S(1)} %all-to-all-done.1.near_ref, f32[64,16,128]{2,1,0:T(8,128)S(1)} %collective-permute-done.far_ref, bf16[128,128,128]{2,1,0:T(8,128)(2,1)S(1)} %copy-done.1, f32[16,128]{1,0:T(8,128)S(1)} %broadcast_in_dim.4.prec_ref, f32[34,16,128]{2,1,0:T(8,128)S(1)} %get-tuple-element.42.kept_ref), custom_call_target="tpu_custom_call" | custom-call | flops 268435456 | bytes 6291456 | tf_op jit(solution)/shard_map/map/pallas_call | solution.py:453
  62.1 10.8 %all_to_all.25.rows_ref = f32[16,16,128]{2,1,0:T(8,128)S(1)} all-to-all(f32[16,16,128]{2,1,0:T(8,128)S(1)} %map.1), channel_id=1, replica_groups=mesh['y'=4,'c'=2,'tm'=16] {'tm'}, dimensions={0} | all-to-all | bytes 262144 | tf_op jit(solution)/shard_map/all_to_all | solution.py:462
  72.9 0.2 local_carry.1
  73.2 11.9 %all_to_all.26.carry_ref = f32[16,32,128]{2,1,0:T(8,128)S(1)} all-to-all(f32[16,32,128]{2,1,0:T(8,128)S(1)} %local_carry.1), channel_id=1, replica_groups=mesh['y'=4,'c'=2,'tm'=16] {'tm'}, dimensions={0} | all-to-all | bytes 524288 | tf_op jit(solution)/shard_map/all_to_all | solution.py:473
  85.1 11.6 %all_to_all.27.states_ref = f32[16,16,128]{2,1,0:T(8,128)S(1)} all-to-all(f32[16,16,128]{2,1,0:T(8,128)S(1)} %state.1), channel_id=1, replica_groups=mesh['y'=4,'c'=2,'tm'=16] {'tm'}, dimensions={0} | all-to-all | bytes 262144 | tf_op jit(solution)/shard_map/all_to_all | solution.py:483
  96.7 0.6 noise.1
  97.3 5.4 %whiten.1 = (f32[16,2048]{1,0:T(8,128)}, f32[2048,512]{1,0:T(8,128)}) custom-call(f32[2048,512]{1,0:T(8,128)S(1)} %copy-done.7, f32[16,16,128]{2,1,0:T(8,128)S(1)} %all_to_all.25.rows_ref, f32[16,16,128]{2,1,0:T(8,128)S(1)} %all_to_all.27.states_ref, bf16[96,512]{1,0:T(8,128)(2,1)S(1)} %get-tuple-element.48.stack_ref, ...), custom_call_target="tpu_custom_call" | custom-call | flops 3565158400 | bytes 14680064 | tf_op jit(solution)/shard_map/whiten/pallas_call | solution.py:501
  (25 shorter events, 0.1 us)
Async XLA Ops:
  8.5 28.0 %all-to-all-start = ((f32[16,152,128]{2,1,0:T(8,128)}), f32[16,152,128]{2,1,0:T(8,128)S(1)}, u32[]{:S(2)}, u32[]{:S(2)}) async-start(f32[16,152,128]{2,1,0:T(8,128)} %gram.1), calls=%async_computation | async-start | bytes 2490368 | tf_op jit(solution)/shard_map/all_to_all | solution.py:423
  17.6 18.9 %copy-start.10 = (f32[16]{0:T(128)S(1)}, f32[16]{0:T(128)}, u32[]{:S(2)}) copy-start(f32[16]{0:T(128)} %param.15) | copy-start | bytes 196
  37.8 18.8 %all-to-all-start.1 = ((f32[64,16,128]{2,1,0:T(8,128)}), f32[64,16,128]{2,1,0:T(8,128)S(1)}, u32[]{:S(2)}, u32[]{:S(2)}) async-start(f32[64,16,128]{2,1,0:T(8,128)} %get-tuple-element.37), calls=%async_computation.1 | async-start | bytes 1048576 | tf_op jit(solution)/shard_map/all_to_all | solution.py:440
  44.7 28.2 %copy-start.2 = (f32[16,272,128]{2,1,0:T(8,128)S(1)}, f32[16,272,128]{2,1,0:T(8,128)}, u32[]{:S(2)}) copy-start(f32[16,272,128]{2,1,0:T(8,128)} %get-tuple-element.43.crossed_ref) | copy-start | bytes 6684676
  44.7 28.2 %copy-start.6 = (f32[16,128]{1,0:T(8,128)S(1)}, f32[16,128]{1,0:T(8,128)}, u32[]{:S(2)}) copy-start(f32[16,128]{1,0:T(8,128)} %get-tuple-element.44.decayed_ref) | copy-start | bytes 24580
  50.5 1.9 %copy-start = (bf16[128,128,128]{2,1,0:T(8,128)(2,1)}, bf16[128,128,128]{2,1,0:T(8,128)(2,1)S(1)}, u32[]{:S(2)}) copy-start(bf16[128,128,128]{2,1,0:T(8,128)(2,1)S(1)} %count.1.counts_ref) | copy-start | bytes 12582916
  56.6 1.9 %collective-permute-start = (f32[64,16,128]{2,1,0:T(8,128)S(1)}, f32[64,16,128]{2,1,0:T(8,128)S(1)}, u32[]{:S(2)}, u32[]{:S(2)}) collective-permute-start(f32[64,16,128]{2,1,0:T(8,128)S(1)} %all-to-all-done.1.near_ref), channel_id=1, source_target_pairs={{0,16},{16,0},{1,17},{17,1},{2,18},{18,2},{3,19},{19,3},{4,20},{20... | collective-permute-start | bytes 1572872 | tf_op jit(solution)/shard_map/ppermute | solution.py:451
  58.5 2.2 %copy-start.1 = (bf16[128,128,128]{2,1,0:T(8,128)(2,1)S(1)}, bf16[128,128,128]{2,1,0:T(8,128)(2,1)}, u32[]{:S(2)}) copy-start(bf16[128,128,128]{2,1,0:T(8,128)(2,1)} %copy-done) | copy-start | bytes 12582916
  60.7 36.0 %copy-start.3 = (f32[16,512]{1,0:T(8,128)S(1)}, f32[16,512]{1,0:T(8,128)}, u32[]{:S(2)}) copy-start(f32[16,512]{1,0:T(8,128)} %basis_ref.3) | copy-start | bytes 98308
  60.7 36.0 %copy-start.4 = (f32[16,512]{1,0:T(8,128)S(1)}, f32[16,512]{1,0:T(8,128)}, u32[]{:S(2)}) copy-start(f32[16,512]{1,0:T(8,128)} %decay_ref.1) | copy-start | bytes 98308
  60.7 36.0 %copy-start.5 = (f32[16,512]{1,0:T(8,128)S(1)}, f32[16,512]{1,0:T(8,128)}, u32[]{:S(2)}) copy-start(f32[16,512]{1,0:T(8,128)} %feed_ref.3) | copy-start | bytes 98308
  60.7 36.0 %copy-start.8 = (f32[16,512]{1,0:T(8,128)S(1)}, f32[16,512]{1,0:T(8,128)}, u32[]{:S(2)}) copy-start(f32[16,512]{1,0:T(8,128)} %load_ref.1) | copy-start | bytes 98308
  85.1 12.3 %copy-start.7 = (f32[2048,512]{1,0:T(8,128)S(1)}, f32[2048,512]{1,0:T(8,128)}, u32[]{:S(2)}) copy-start(f32[2048,512]{1,0:T(8,128)} %get-tuple-element.34.marked_ref) | copy-start | bytes 12582916
  85.1 12.3 %copy-start.9 = (f32[512]{0:T(512)S(1)}, f32[512]{0:T(512)}, u32[]{:S(2)}) copy-start(f32[512]{0:T(512)} %param.19) | copy-start | bytes 6148

commit v3 on v2

--- a/solution.py
+++ b/solution.py
@@ -129,7 +129,7 @@
 
 
 def cross_kernel(
-    flux_ref, valid_ref, basis_ref, decay_ref, feed_ref, out_ref, decayed_ref, marked_ref, table_ref
+    flux_ref, valid_ref, basis_ref, decay_ref, feed_ref, out_ref, decayed_ref, table_ref
 ):
     cross = BASIS_VECTORS * NOISE_TERMS
     feeds = 2 * cross
@@ -154,7 +154,6 @@
 
     usable = valid_ref[...] != 0
     flux = flux_ref[...]
-    marked_ref[...] = jnp.where(usable, flux, jnp.nan)
     sums = dot_nt(table_ref[0:feeds, :], jnp.where(usable, 1.0, 0.0).astype(BF16))
     crossed = sums[0:cross] + sums[cross : 2 * cross]
     plain = narrow_dots(table_ref, feeds, jnp.where(usable, flux, 0.0), 2)
@@ -164,21 +163,24 @@
         out_ref[chunk, 16:CROSS_ROWS, :] = crossed[:, lanes]
 
 
-def count_kernel(code_ref, low_ref, out_ref):
+def count_kernel(code_ref, low_ref, near_ref, far_ref):
     entries = 8 * NEIGH
-    row_code = lax.broadcasted_iota(jnp.int32, (128 * 8, entries), 0)
-    low_code = lax.broadcasted_iota(jnp.int32, (128, entries), 0)
+    half, lows_all = near_ref.shape[0], near_ref.shape[2]
+    row_code = lax.broadcasted_iota(jnp.int32, (2 * half * 8, entries), 0)
+    low_code = lax.broadcasted_iota(jnp.int32, (lows_all, entries), 0)
 
     def one_half(group):
         code = code_ref[pl.ds(group, 1), :]
         low = low_ref[pl.ds(group, 1), :]
         highs = jnp.where(row_code == code, 1.0, 0.0).astype(BF16)
         lows = jnp.where(low_code == low, 1.0, 0.0).astype(BF16)
-        return dot_nt(highs, lows).reshape(128, 8, 128)
+        return dot_nt(highs, lows).reshape(2 * half, 8, lows_all)
 
     def one(step, ignored):
-        both = jnp.concatenate([one_half(2 * step), one_half(2 * step + 1)], axis=1)
-        out_ref[:, pl.ds(pl.multiple_of(step * 16, 16), 16), :] = both.astype(BF16)
+        both = jnp.concatenate([one_half(2 * step), one_half(2 * step + 1)], axis=1).astype(BF16)
+        span = pl.ds(pl.multiple_of(step * 16, 16), 16)
+        near_ref[:, span, :] = both[:half]
+        far_ref[:, span, :] = both[half:]
         return ignored
 
     lax.fori_loop(0, OWN // 16, one, 0)
@@ -295,14 +297,20 @@
         kept_ref[32, k : k + 1, :] = pivots[k]
 
 
-def map_kernel(near_ref, far_ref, counts_ref, prec_ref, kept_ref, out_ref):
-    half = near_ref.shape[0]
-    prior = jnp.zeros((48, OWN), F32)
-    for spot in range(0, 2 * half, 2):
-        table_ref, place = (near_ref, spot) if spot < half else (far_ref, spot - half)
+def listed_sums(table_ref, counts_ref):
+    sums = jnp.zeros((48, OWN), F32)
+    for place in range(0, table_ref.shape[0], 2):
         wide = jnp.concatenate([table_ref[place], table_ref[place + 1]], axis=1)
-        listed = jnp.concatenate([counts_ref[spot], counts_ref[spot + 1]], axis=1)
-        prior = prior + dot_nt(jnp.concatenate(split3(wide), axis=0), listed)
+        sums = sums + dot_nt(jnp.concatenate(split3(wide), axis=0), counts_ref[place // 2])
+    return sums
+
+
+def near_kernel(near_ref, counts_ref, out_ref):
+    out_ref[...] = listed_sums(near_ref, counts_ref)
+
+
+def map_kernel(begun_ref, far_ref, counts_ref, prec_ref, kept_ref, out_ref):
+    prior = begun_ref[...] + listed_sums(far_ref, counts_ref)
     prior_mean = (prior[0:16] + (prior[16:32] + prior[32:48])) * (1.0 / NEIGH)
     vector = kept_ref[33] + prec_ref[...] * prior_mean
     for k in range(BASIS_VECTORS):
@@ -333,15 +341,15 @@
 
 
 def whiten_kernel(
-    marked_ref, rows_ref, states_ref, stack_ref, entry_ref, high_ref, low_ref, scale_ref, coeffs_ref, out_ref
+    flux_ref, valid_ref, rows_ref, states_ref, stack_ref, entry_ref, high_ref, low_ref, scale_ref, coeffs_ref, out_ref
 ):
     coeffs = jnp.concatenate([rows_ref[chunk] for chunk in range(WHITEN_CHUNKS)], axis=1)
     states = jnp.concatenate([states_ref[chunk] for chunk in range(WHITEN_CHUNKS)], axis=1)
     coeffs_ref[...] = coeffs
     trend = dot_tn(left_stack(coeffs), stack_ref[...])
     first = pl.multiple_of(pl.program_id(0) * WHITEN_STEP, WHITEN_STEP)
-    marked = marked_ref[pl.ds(first, WHITEN_STEP), :]
-    residual = jnp.where(marked == marked, marked - trend, 0.0)
+    stars = pl.ds(first, WHITEN_STEP)
+    residual = jnp.where(valid_ref[stars, :] != 0, flux_ref[stars, :] - trend, 0.0)
     incoming = dot_tn(left_stack(states), entry_ref[...])
     high = residual.astype(BF16)
     low = (residual - high.astype(F32)).astype(BF16)
@@ -373,12 +381,6 @@
     blocks = stars // OWN
     place = lax.axis_index("tm")
     prec = jnp.broadcast_to(prior_prec[:, None], (BASIS_VECTORS, OWN))
-
-    listed = lax.dynamic_slice_in_dim(neighbours, place * OWN, OWN, 0).reshape(blocks, -1)
-    low_bits = listed & 127
-    owner = listed >> 7
-    spot = (owner & 15) + 16 * (owner >> 5) + 64 * (((owner >> 4) & 1) ^ lax.axis_index("c"))
-    code = spot * 8 + lax.broadcasted_iota(jnp.int32, listed.shape, 1) // NEIGH
 
     in_hbm = pl.BlockSpec(memory_space=pl.ANY)
     parts = pl.pallas_call(
@@ -398,22 +400,28 @@
         name="gram",
     )(flux, valid, quality, basis)
 
-    parts, later_basis, later_decay = lax.optimization_barrier((parts, basis, decay))
+    parts, later_basis, later_decay, neighbours = lax.optimization_barrier(
+        (parts, basis, decay, neighbours)
+    )
+    listed = lax.dynamic_slice_in_dim(neighbours, place * OWN, OWN, 0).reshape(blocks, -1)
+    owner = listed >> 7
+    spot = (owner & 15) + 16 * (owner >> 5) + 64 * (((owner >> 4) & 1) ^ lax.axis_index("c"))
+    low_bits = (listed & 127) + 128 * (spot & 1)
+    code = (spot >> 1) * 8 + lax.broadcasted_iota(jnp.int32, listed.shape, 1) // NEIGH
+
     cross_spec = pl.BlockSpec((CROSS_STEP, cadences), lambda i: (i, 0))
     table_spec = pl.BlockSpec((16, cadences), lambda i: (0, 0))
-    crossed, decayed, marked = pl.pallas_call(
+    crossed, decayed = pl.pallas_call(
         cross_kernel,
         grid=(stars // CROSS_STEP,),
         in_specs=[cross_spec, cross_spec, table_spec, table_spec, table_spec],
         out_specs=[
             pl.BlockSpec((CROSS_CHUNKS, CROSS_ROWS, OWN), lambda i: (i, 0, 0)),
             pl.BlockSpec((NOISE_TERMS, OWN), lambda i: (0, 0)),
-            cross_spec,
         ],
         out_shape=[
             jax.ShapeDtypeStruct((blocks, CROSS_ROWS, OWN), F32),
             jax.ShapeDtypeStruct((NOISE_TERMS, OWN), F32),
-            jax.ShapeDtypeStruct((stars, cadences), F32),
         ],
         scratch_shapes=[pltpu.VMEM((560, cadences), BF16)],
         compiler_params=params(58),
@@ -421,7 +429,18 @@
         name="cross",
     )(flux, valid, later_basis, later_decay, feed_w)
     parts = lax.all_to_all(parts, "tm", 0, 0, tiled=True)
-    parts, crossed, decayed, marked = lax.optimization_barrier((parts, crossed, decayed, marked))
+    near_counts, far_counts = pl.pallas_call(
+        count_kernel,
+        in_specs=[vmem(), vmem()],
+        out_specs=[vmem()] * 2,
+        out_shape=[jax.ShapeDtypeStruct((32, OWN, 256), BF16)] * 2,
+        compiler_params=params(16),
+        cost_estimate=cost(4 << 30, 4 * MIB),
+        name="count",
+    )(code, low_bits)
+    parts, crossed, decayed, near_counts, far_counts = lax.optimization_barrier(
+        (parts, crossed, decayed, near_counts, far_counts)
+    )
 
     nearby = ("y", "tm")
     copies = jax.ShapeDtypeStruct((lax.axis_size(nearby), 16, OWN), F32)
@@ -436,53 +455,19 @@
         name="solve",
     )(parts, prec)
 
-    fitted, later_code, later_low = lax.optimization_barrier((fitted, code, low_bits))
     near = lax.all_to_all(fitted, nearby, 0, 0, tiled=True)
-    counts = pl.pallas_call(
-        count_kernel,
-        in_specs=[vmem(), vmem()],
+    near, last_decay, last_basis = lax.optimization_barrier((near, decay, basis))
+    far = lax.ppermute(near, "c", [(0, 1), (1, 0)])
+    begun = pl.pallas_call(
+        near_kernel,
+        in_specs=[vmem()] * 2,
         out_specs=vmem(),
-        out_shape=jax.ShapeDtypeStruct((128, OWN, 128), BF16),
-        compiler_params=params(16),
-        cost_estimate=cost(4 << 30, 4 * MIB),
-        name="count",
-    )(later_code, later_low)
-    near, counts = lax.optimization_barrier((near, counts))
-    far = lax.ppermute(near, "c", [(0, 1), (1, 0)])
-
-    rows = pl.pallas_call(
-        map_kernel,
-        in_specs=[vmem()] * 5,
-        out_specs=vmem(),
-        out_shape=jax.ShapeDtypeStruct((blocks, 16, OWN), F32),
-        compiler_params=params(16),
-        cost_estimate=cost(1 << 28, 6 * MIB),
-        name="map",
-    )(near, far, counts, prec, kept)
-    rows = lax.all_to_all(rows, "tm", 0, 0, tiled=True)
-
-    carries = pl.pallas_call(
-        carry_kernel,
-        in_specs=[vmem()] * 3,
-        out_specs=vmem(),
-        out_shape=jax.ShapeDtypeStruct((blocks, 32, OWN), F32),
-        compiler_params=params(16),
-        cost_estimate=cost(1 << 24, 3 * MIB),
-        name="local_carry",
-    )(rows, crossed, decayed)
-    carries = lax.all_to_all(carries, "tm", 0, 0, tiled=True)
-    states = pl.pallas_call(
-        state_kernel,
-        in_specs=[vmem()],
-        out_specs=vmem(),
-        out_shape=jax.ShapeDtypeStruct((blocks, 16, OWN), F32),
-        compiler_params=params(16),
-        cost_estimate=cost(1 << 20, MIB),
-        name="state",
-    )(carries)
-    states = lax.all_to_all(states, "tm", 0, 0, tiled=True)
-
-    states, last_decay, last_basis = lax.optimization_barrier((states, decay, basis))
+        out_shape=jax.ShapeDtypeStruct((48, OWN), F32),
+        compiler_params=params(16),
+        cost_estimate=cost(1 << 28, 3 * MIB),
+        name="near",
+    )(near, near_counts)
+
     high, low, entry, stack = pl.pallas_call(
         noise_kernel,
         in_specs=[vmem()] * 4,
@@ -497,11 +482,46 @@
         cost_estimate=cost(2 << 30, 2 * MIB),
         name="noise",
     )(last_decay, load_u, feed_w, last_basis)
+    far, begun, high, low, entry, stack = lax.optimization_barrier(
+        (far, begun, high, low, entry, stack)
+    )
+    rows = pl.pallas_call(
+        map_kernel,
+        in_specs=[vmem()] * 5,
+        out_specs=vmem(),
+        out_shape=jax.ShapeDtypeStruct((blocks, 16, OWN), F32),
+        compiler_params=params(16),
+        cost_estimate=cost(1 << 28, 6 * MIB),
+        name="map",
+    )(begun, far, far_counts, prec, kept)
+    rows = lax.all_to_all(rows, "tm", 0, 0, tiled=True)
+
+    carries = pl.pallas_call(
+        carry_kernel,
+        in_specs=[vmem()] * 3,
+        out_specs=vmem(),
+        out_shape=jax.ShapeDtypeStruct((blocks, 32, OWN), F32),
+        compiler_params=params(16),
+        cost_estimate=cost(1 << 24, 3 * MIB),
+        name="local_carry",
+    )(rows, crossed, decayed)
+    carries = lax.all_to_all(carries, "tm", 0, 0, tiled=True)
+    states = pl.pallas_call(
+        state_kernel,
+        in_specs=[vmem()],
+        out_specs=vmem(),
+        out_shape=jax.ShapeDtypeStruct((blocks, 16, OWN), F32),
+        compiler_params=params(16),
+        cost_estimate=cost(1 << 20, MIB),
+        name="state",
+    )(carries)
+    states = lax.all_to_all(states, "tm", 0, 0, tiled=True)
+
     part_spec = pl.BlockSpec((WHITEN_CHUNKS, 16, OWN), lambda i: (i, 0, 0))
     coeffs, whitened = pl.pallas_call(
         whiten_kernel,
         grid=(stars // WHITEN_STEP,),
-        in_specs=[vmem(), part_spec, part_spec] + [vmem()] * 5,
+        in_specs=[vmem(), vmem(), part_spec, part_spec] + [vmem()] * 5,
         out_specs=[
             pl.BlockSpec((16, WHITEN_STEP), lambda i: (0, i)),
             pl.BlockSpec((WHITEN_STEP, cadences), lambda i: (i, 0)),
@@ -513,7 +533,7 @@
         compiler_params=params(32),
         cost_estimate=cost(2 * stars * cadences * 1700, 14 * MIB),
         name="whiten",
-    )(marked, rows, states, stack, entry, high, low, inv_diag[None, :])
+    )(flux, valid, rows, states, stack, entry, high, low, inv_diag[None, :])
     return coeffs.T, whitened
 
 

time: 103 us -> 99.3 us (0.964)
  blocking collectives: 34.3 us -> 52.9 us
  waiting for transfers between devices: 17.2 us -> 7.14 us
  starting transfers between devices: 14.9 us -> 7.98 us
  Pallas kernels: 30.2 us -> 26.8 us
  local copies, waits for them, and re-layouts: 4.58 us -> 2.32 us
    all_to_all x0 -> x1, blocking collectives: none -> 18.6 us  [per_device(): near = lax.all_to_all(fitted, nearby, 0, 0, tiled=True)]
    all_to_all x1 -> x0, starting transfers between devices: 6.93 us -> none  [per_device(): near = lax.all_to_all(fitted, nearby, 0, 0, tiled=True)]
    all_to_all x1, waiting for transfers between devices: 11.1 us -> 6.76 us  [per_device(): parts = lax.all_to_all(parts, 'tm', 0, 0, tiled=True)]
    all_to_all x1 -> x0, waiting for transfers between devices: 4.15 us -> none  [per_device(): near = lax.all_to_all(fitted, nearby, 0, 0, tiled=True)]
    unnamed x22 -> x24, local copies, waits for them, and re-layouts: 4.17 us -> 1.91 us
    ppermute x1, waiting for transfers between devices: 1.91 us -> 0.38 us  [per_device(): far = lax.ppermute(near, 'c', [(0, 1), (1, 0)])]
    pallas_call x1 -> x2, Pallas kernels: 5.75 us -> 4.7 us  [the longest x1 3.91 us: per_device(): pl.pallas_call(count_kernel, in_specs=[vmem(), vmem()], out_specs=[vmem()...]
  transfers between devices with their start and end apart: 3 -> 2, of which waited for: 3 -> 2; matrix products, arithmetic and copies ran while one was open for 1% -> 1% of each run, Pallas kernels for 13% -> 12%
where the time goes in v3:
time: 99.3 us; the launch traced here: 98.8 us
  blocking collectives  52.9 us (53%)
  Pallas kernels  26.8 us (27%)
  starting transfers between devices  7.98 us (8%)
  waiting for transfers between devices  7.14 us (7%)
  local copies, waits for them, and re-layouts  2.32 us (2%)
    all_to_all x1, blocking collectives, per_device(): near = lax.all_to_all(fitted, nearby, 0, 0, tiled=True)  18.6 us
    all_to_all x1, blocking collectives, per_device(): carries = lax.all_to_all(carries, 'tm', 0, 0, tiled=True)  11.8 us
    all_to_all x1, blocking collectives, per_device(): states = lax.all_to_all(states, 'tm', 0, 0, tiled=True)  11.3 us
    all_to_all x1, blocking collectives, per_device(): rows = lax.all_to_all(rows, 'tm', 0, 0, tiled=True)  11.2 us
    all_to_all x1, starting transfers between devices, per_device(): parts = lax.all_to_all(parts, 'tm', 0, 0, tiled=True)  7.98 us
    pallas_call x1, Pallas kernels, per_device(): pl.pallas_call(gram_kernel, in_specs=[in_hbm] * 3 + [vmem()], out_specs=v...  7.8 us
    pallas_call x1, Pallas kernels, per_device(): pl.pallas_call(cross_kernel, grid=(stars // CROSS_STEP,), in_specs=[cross...  6.84 us
    all_to_all x1, waiting for transfers between devices, per_device(): parts = lax.all_to_all(parts, 'tm', 0, 0, tiled=True)  6.76 us
  transfers between devices with their start and end apart: 2, of which 2 were waited for; matrix products, arithmetic and copies ran while one was open for 1% of the time, Pallas kernels for 12%

profile of v3, /device:TPU:0, one launch (start us, length us, event | category | flops | bytes accessed | tf_op | source)
XLA Modules:
  0.0 98.8 jit_solution(3097037043536596646)
XLA Ops:
  0.6 7.8 %gram.1 = f32[16,152,128]{2,1,0:T(8,128)} custom-call(f32[2048,512]{1,0:T(8,128)} %flux_ref.3, s32[2048,512]{1,0:T(8,128)} %valid_ref.3, s32[2048,512]{1,0:T(8,128)} %quality_hbm.1, f32[16,512]{1,0:T(8,128)} %basis_ref.3), custom_call_target="tpu_custom_call" | custom-call | flops 1258291200 | bytes 14680064 | tf_op jit(solution)/shard_map/gram/pallas_call | solution.py:386
  8.4 8.0 %all-to-all-start = ((f32[16,152,128]{2,1,0:T(8,128)}), f32[16,152,128]{2,1,0:T(8,128)S(1)}, u32[]{:S(2)}, u32[]{:S(2)}) async-start(f32[16,152,128]{2,1,0:T(8,128)} %gram.1), calls=%async_computation | async-start | bytes 2490368 | tf_op jit(solution)/shard_map/all_to_all | solution.py:431
  16.4 0.8 multiply_add_fusion
  17.2 0.1 copy.15
  17.3 0.1 reshape.34.low_ref
  17.4 0.1 copy.14
  17.5 0.1 reshape.31
  17.6 6.8 %cross.1 = (f32[16,272,128]{2,1,0:T(8,128)}, f32[16,128]{1,0:T(8,128)}) custom-call(f32[2048,512]{1,0:T(8,128)} %flux_ref.3, s32[2048,512]{1,0:T(8,128)} %valid_ref.3, f32[16,512]{1,0:T(8,128)} %basis_ref.3, f32[16,512]{1,0:T(8,128)} %decay_ref.1, f32[16,512]{1,0:T(8,128)} %feed_ref.3), custom_call_target="tpu_custom_call" | custom-call | flops 1677721600 | bytes 16777216 | tf_op jit(solution)/shard_map/cross/pallas_call | solution.py:414
  24.5 3.9 %count.1 = (bf16[32,128,256]{2,1,0:T(8,128)(2,1)S(1)}, bf16[32,128,256]{2,1,0:T(8,128)(2,1)S(1)}) custom-call(s32[16,512]{1,0:T(8,128)S(1)} %select_add_fusion.code_ref, s32[16,512]{1,0:T(8,128)S(1)} %reshape.34.low_ref), custom_call_target="tpu_custom_call" | custom-call | flops 4294967296 | bytes 4194304 | tf_op jit(solution)/shard_map/count/pallas_call | solution.py:432
  28.4 1.3 %copy-done.3 = bf16[32,128,256]{2,1,0:T(8,128)(2,1)} copy-done((bf16[32,128,256]{2,1,0:T(8,128)(2,1)}, bf16[32,128,256]{2,1,0:T(8,128)(2,1)S(1)}, u32[]{:S(2)}) %copy-start.3) | copy-done | bytes 2097176
  29.7 6.8 %all-to-all-done.parts_ref = f32[16,152,128]{2,1,0:T(8,128)S(1)} async-done(((f32[16,152,128]{2,1,0:T(8,128)}), f32[16,152,128]{2,1,0:T(8,128)S(1)}, u32[]{:S(2)}, u32[]{:S(2)}) %all-to-all-start) | async-done | bytes 1245216 | tf_op jit(solution)/shard_map/all_to_all | solution.py:431
  36.5 0.1 broadcast_in_dim.4.prec_ref
  36.6 0.4 solve.1
  37.0 18.6 %all_to_all.25.near_ref = f32[64,16,128]{2,1,0:T(8,128)S(1)} all-to-all(f32[64,16,128]{2,1,0:T(8,128)S(1)} %get-tuple-element.41), channel_id=1, replica_groups=mesh['y'=4,'c'=2,'tm'=16] {'y','tm'}, dimensions={0} | all-to-all | bytes 1048576 | tf_op jit(solution)/shard_map/all_to_all | solution.py:458
  55.6 0.8 near.1.begun_ref
  56.5 0.6 noise.1
  57.1 0.4 collective-permute-done.far_ref
  57.5 0.5 copy-done.4
  58.0 0.9 map.1
  58.9 11.2 %all_to_all.26.rows_ref = f32[16,16,128]{2,1,0:T(8,128)S(1)} all-to-all(f32[16,16,128]{2,1,0:T(8,128)S(1)} %map.1), channel_id=1, replica_groups=mesh['y'=4,'c'=2,'tm'=16] {'tm'}, dimensions={0} | all-to-all | bytes 262144 | tf_op jit(solution)/shard_map/all_to_all | solution.py:497
  70.1 0.2 local_carry.1
  70.3 11.8 %all_to_all.27.carry_ref = f32[16,32,128]{2,1,0:T(8,128)S(1)} all-to-all(f32[16,32,128]{2,1,0:T(8,128)S(1)} %local_carry.1), channel_id=1, replica_groups=mesh['y'=4,'c'=2,'tm'=16] {'tm'}, dimensions={0} | all-to-all | bytes 524288 | tf_op jit(solution)/shard_map/all_to_all | solution.py:508
  82.1 11.3 %all_to_all.28.states_ref = f32[16,16,128]{2,1,0:T(8,128)S(1)} all-to-all(f32[16,16,128]{2,1,0:T(8,128)S(1)} %state.1), channel_id=1, replica_groups=mesh['y'=4,'c'=2,'tm'=16] {'tm'}, dimensions={0} | all-to-all | bytes 262144 | tf_op jit(solution)/shard_map/all_to_all | solution.py:518
  93.4 5.4 %whiten.1 = (f32[16,2048]{1,0:T(8,128)}, f32[2048,512]{1,0:T(8,128)}) custom-call(f32[2048,512]{1,0:T(8,128)S(1)} %copy-done, s32[2048,512]{1,0:T(8,128)S(1)} %copy-done.1, f32[16,16,128]{2,1,0:T(8,128)S(1)} %all_to_all.26.rows_ref, f32[16,16,128]{2,1,0:T(8,128)S(1)} %all_to_all.28.states_ref, bf16[96,512]{1,0:T(8,128)(2,1)S(1)} %get-tuple-element.56.stack_ref, ...), custom_call_target="tpu_custom_call" | custom-call | flops 3565158400 | bytes 14680064 | tf_op jit(solution)/shard_map/whiten/pallas_call | solution.py:521
  (27 shorter events, 0.1 us)
Async XLA Ops:
  8.4 28.0 %all-to-all-start = ((f32[16,152,128]{2,1,0:T(8,128)}), f32[16,152,128]{2,1,0:T(8,128)S(1)}, u32[]{:S(2)}, u32[]{:S(2)}) async-start(f32[16,152,128]{2,1,0:T(8,128)} %gram.1), calls=%async_computation | async-start | bytes 2490368 | tf_op jit(solution)/shard_map/all_to_all | solution.py:431
  24.4 12.0 %copy-start.11 = (f32[16]{0:T(128)S(1)}, f32[16]{0:T(128)}, u32[]{:S(2)}) copy-start(f32[16]{0:T(128)} %param.15) | copy-start | bytes 196
  28.4 1.3 %copy-start.3 = (bf16[32,128,256]{2,1,0:T(8,128)(2,1)}, bf16[32,128,256]{2,1,0:T(8,128)(2,1)S(1)}, u32[]{:S(2)}) copy-start(bf16[32,128,256]{2,1,0:T(8,128)(2,1)S(1)} %get-tuple-element.52.counts_ref) | copy-start | bytes 6291460
  36.5 19.8 %copy-start.5 = (f32[16,512]{1,0:T(8,128)S(1)}, f32[16,512]{1,0:T(8,128)}, u32[]{:S(2)}) copy-start(f32[16,512]{1,0:T(8,128)} %basis_ref.3) | copy-start | bytes 98308
  36.5 19.9 %copy-start.6 = (f32[16,512]{1,0:T(8,128)S(1)}, f32[16,512]{1,0:T(8,128)}, u32[]{:S(2)}) copy-start(f32[16,512]{1,0:T(8,128)} %decay_ref.1) | copy-start | bytes 98308
  36.5 19.9 %copy-start.7 = (f32[16,512]{1,0:T(8,128)S(1)}, f32[16,512]{1,0:T(8,128)}, u32[]{:S(2)}) copy-start(f32[16,512]{1,0:T(8,128)} %feed_ref.3) | copy-start | bytes 98308
  36.6 19.9 %copy-start.9 = (f32[16,512]{1,0:T(8,128)S(1)}, f32[16,512]{1,0:T(8,128)}, u32[]{:S(2)}) copy-start(f32[16,512]{1,0:T(8,128)} %load_ref.1) | copy-start | bytes 98308
  55.6 1.9 %collective-permute-start = (f32[64,16,128]{2,1,0:T(8,128)S(1)}, f32[64,16,128]{2,1,0:T(8,128)S(1)}, u32[]{:S(2)}, u32[]{:S(2)}) collective-permute-start(f32[64,16,128]{2,1,0:T(8,128)S(1)} %all_to_all.25.near_ref), channel_id=1, source_target_pairs={{0,16},{16,0},{1,17},{17,1},{2,18},{18,2},{3,19},{19,3},{4,20},{20... | collective-permute-start | bytes 1572872 | tf_op jit(solution)/shard_map/ppermute | solution.py:460
  56.4 1.6 %copy-start.4 = (bf16[32,128,256]{2,1,0:T(8,128)(2,1)S(1)}, bf16[32,128,256]{2,1,0:T(8,128)(2,1)}, u32[]{:S(2)}) copy-start(bf16[32,128,256]{2,1,0:T(8,128)(2,1)} %copy-done.3) | copy-start | bytes 6291460
  56.4 37.0 %copy-start.1 = (s32[2048,512]{1,0:T(8,128)S(1)}, s32[2048,512]{1,0:T(8,128)}, u32[]{:S(2)}) copy-start(s32[2048,512]{1,0:T(8,128)} %valid_ref.3) | copy-start | bytes 12582916
  57.1 13.0 %copy-start.2 = (f32[16,272,128]{2,1,0:T(8,128)S(1)}, f32[16,272,128]{2,1,0:T(8,128)}, u32[]{:S(2)}) copy-start(f32[16,272,128]{2,1,0:T(8,128)} %get-tuple-element.54.crossed_ref) | copy-start | bytes 6684676
  57.1 13.0 %copy-start.8 = (f32[16,128]{1,0:T(8,128)S(1)}, f32[16,128]{1,0:T(8,128)}, u32[]{:S(2)}) copy-start(f32[16,128]{1,0:T(8,128)} %get-tuple-element.55.decayed_ref) | copy-start | bytes 24580
  58.0 35.4 %copy-start = (f32[2048,512]{1,0:T(8,128)S(1)}, f32[2048,512]{1,0:T(8,128)}, u32[]{:S(2)}) copy-start(f32[2048,512]{1,0:T(8,128)} %flux_ref.3) | copy-start | bytes 12582916
  58.9 34.5 %copy-start.10 = (f32[512]{0:T(512)S(1)}, f32[512]{0:T(512)}, u32[]{:S(2)}) copy-start(f32[512]{0:T(512)} %param.19) | copy-start | bytes 6148

commit v4 on v3

--- a/solution.py
+++ b/solution.py
@@ -323,21 +323,53 @@
 
 
 def carry_kernel(rows_ref, crossed_ref, decayed_ref, out_ref):
-    for owner in range(rows_ref.shape[0]):
+    owners = rows_ref.shape[0]
+    for owner in range(owners):
         coeffs = rows_ref[owner]
         carry = crossed_ref[owner, 0:16, :]
         for k in range(BASIS_VECTORS):
             first = 16 + 16 * k
             carry = carry - coeffs[k : k + 1, :] * crossed_ref[owner, first : first + 16, :]
-        out_ref[owner, 0:16, :] = carry
-        out_ref[owner, 16:32, :] = decayed_ref[...]
-
-
-def state_kernel(carry_ref, out_ref):
+        for peer in range(out_ref.shape[0]):
+            out_ref[peer, owner] = carry
+    for peer in range(out_ref.shape[0]):
+        out_ref[peer, owners] = decayed_ref[...]
+
+
+def entering(parts_ref, owner, place):
+    last = parts_ref.shape[1] - 1
     state = jnp.zeros((NOISE_TERMS, OWN), F32)
-    for block in range(carry_ref.shape[0]):
-        out_ref[block] = state
-        state = state * carry_ref[block, 16:32, :] + carry_ref[block, 0:16, :]
+    found = state
+    for block in range(parts_ref.shape[0]):
+        found = jnp.where(place == block, state, found)
+        state = state * parts_ref[block, last] + parts_ref[block, owner]
+    return found, state
+
+
+def level_kernel(parts_ref, inner_ref, out_ref):
+    place = lax.axis_index("z")
+    owners = inner_ref.shape[0] - 1
+    for owner in range(owners):
+        found, state = entering(parts_ref, owner, place)
+        inner_ref[owner] = found
+        for peer in range(out_ref.shape[0]):
+            out_ref[peer, owner] = state
+    product = jnp.ones((NOISE_TERMS, OWN), F32)
+    before = product
+    for block in range(parts_ref.shape[0]):
+        before = jnp.where(place == block, product, before)
+        product = product * parts_ref[block, owners]
+    inner_ref[owners] = before
+    for peer in range(out_ref.shape[0]):
+        out_ref[peer, owners] = product
+
+
+def state_kernel(parts_ref, inner_ref, out_ref):
+    place = lax.axis_index("x")
+    owners = out_ref.shape[0]
+    for owner in range(owners):
+        found, ignored = entering(parts_ref, owner, place)
+        out_ref[owner] = inner_ref[owner] + inner_ref[owners] * found
 
 
 def whiten_kernel(
@@ -379,7 +411,8 @@
 ):
     stars, cadences = flux.shape
     blocks = stars // OWN
-    place = lax.axis_index("tm")
+    cadence_axes = ("x", "z")
+    place = lax.axis_index(cadence_axes)
     prec = jnp.broadcast_to(prior_prec[:, None], (BASIS_VECTORS, OWN))
 
     in_hbm = pl.BlockSpec(memory_space=pl.ANY)
@@ -428,7 +461,7 @@
         cost_estimate=cost(2 * stars * cadences * 800, 16 * MIB),
         name="cross",
     )(flux, valid, later_basis, later_decay, feed_w)
-    parts = lax.all_to_all(parts, "tm", 0, 0, tiled=True)
+    parts = lax.all_to_all(parts, cadence_axes, 0, 0, tiled=True)
     near_counts, far_counts = pl.pallas_call(
         count_kernel,
         in_specs=[vmem(), vmem()],
@@ -442,7 +475,7 @@
         (parts, crossed, decayed, near_counts, far_counts)
     )
 
-    nearby = ("y", "tm")
+    nearby = ("y", "x", "z")
     copies = jax.ShapeDtypeStruct((lax.axis_size(nearby), 16, OWN), F32)
     fitted, kept = pl.pallas_call(
         solve_kernel,
@@ -494,28 +527,41 @@
         cost_estimate=cost(1 << 28, 6 * MIB),
         name="map",
     )(begun, far, far_counts, prec, kept)
-    rows = lax.all_to_all(rows, "tm", 0, 0, tiled=True)
-
+    rows = lax.all_to_all(rows, cadence_axes, 0, 0, tiled=True)
+
+    along_z, along_x = lax.axis_size("z"), lax.axis_size("x")
     carries = pl.pallas_call(
         carry_kernel,
         in_specs=[vmem()] * 3,
         out_specs=vmem(),
-        out_shape=jax.ShapeDtypeStruct((blocks, 32, OWN), F32),
+        out_shape=jax.ShapeDtypeStruct((along_z, blocks + 1, 16, OWN), F32),
         compiler_params=params(16),
         cost_estimate=cost(1 << 24, 3 * MIB),
         name="local_carry",
     )(rows, crossed, decayed)
-    carries = lax.all_to_all(carries, "tm", 0, 0, tiled=True)
+    carries = lax.all_to_all(carries, "z", 0, 0, tiled=True)
+    inner, carries = pl.pallas_call(
+        level_kernel,
+        in_specs=[vmem()],
+        out_specs=[vmem()] * 2,
+        out_shape=[
+            jax.ShapeDtypeStruct((blocks + 1, 16, OWN), F32),
+            jax.ShapeDtypeStruct((along_x, blocks + 1, 16, OWN), F32),
+        ],
+        compiler_params=params(16),
+        cost_estimate=cost(1 << 20, MIB),
+        name="level",
+    )(carries)
+    carries = lax.all_to_all(carries, "x", 0, 0, tiled=True)
     states = pl.pallas_call(
         state_kernel,
-        in_specs=[vmem()],
+        in_specs=[vmem()] * 2,
         out_specs=vmem(),
         out_shape=jax.ShapeDtypeStruct((blocks, 16, OWN), F32),
         compiler_params=params(16),
         cost_estimate=cost(1 << 20, MIB),
         name="state",
-    )(carries)
-    states = lax.all_to_all(states, "tm", 0, 0, tiled=True)
+    )(carries, inner)
 
     part_spec = pl.BlockSpec((WHITEN_CHUNKS, 16, OWN), lambda i: (i, 0, 0))
     coeffs, whitened = pl.pallas_call(
@@ -539,21 +585,22 @@
 
 def solution(mesh):
     devices = mesh.devices
-    split = Mesh(devices.reshape(devices.shape[0] // 2, 2, devices.shape[1]), ("y", "c", "tm"))
+    split = Mesh(devices.reshape(devices.shape[0] // 2, 2, 4, devices.shape[1] // 4), ("y", "c", "x", "z"))
+    tm = ("x", "z")
     star = ("y", "c")
     in_specs = (
-        P(star, "tm"),
-        P(star, "tm"),
-        P(star, "tm"),
-        P(None, "tm"),
+        P(star, tm),
+        P(star, tm),
+        P(star, tm),
+        P(None, tm),
         P(star, None),
         P(),
-        P(None, "tm"),
-        P(None, "tm"),
-        P(None, "tm"),
-        P("tm"),
+        P(None, tm),
+        P(None, tm),
+        P(None, tm),
+        P(tm),
     )
-    out_specs = (P(star, None), P(star, "tm"))
+    out_specs = (P(star, None), P(star, tm))
     return jax.shard_map(
         per_device, mesh=split, in_specs=in_specs, out_specs=out_specs, check_vma=False
     )

time: 99.3 us -> 98.9 us (level)
  no operation moved by 1% of the time
where the time goes in v4:
time: 98.9 us; the launch traced here: 98.4 us
  blocking collectives  52.4 us (53%)
  Pallas kernels  26.9 us (27%)
  starting transfers between devices  7.98 us (8%)
  waiting for transfers between devices  7.14 us (7%)
  local copies, waits for them, and re-layouts  2.31 us (2%)
    all_to_all x1, blocking collectives, per_device(): near = lax.all_to_all(fitted, nearby, 0, 0, tiled=True)  18.6 us
    all_to_all x1, blocking collectives, per_device(): carries = lax.all_to_all(carries, 'z', 0, 0, tiled=True)  12 us
    all_to_all x1, blocking collectives, per_device(): rows = lax.all_to_all(rows, cadence_axes, 0, 0, tiled=True)  11.1 us
    all_to_all x1, blocking collectives, per_device(): carries = lax.all_to_all(carries, 'x', 0, 0, tiled=True)  10.8 us
    all_to_all x1, starting transfers between devices, per_device(): parts = lax.all_to_all(parts, cadence_axes, 0, 0, tiled=True)  7.98 us
    pallas_call x1, Pallas kernels, per_device(): pl.pallas_call(gram_kernel, in_specs=[in_hbm] * 3 + [vmem()], out_specs=v...  7.81 us
    pallas_call x1, Pallas kernels, per_device(): pl.pallas_call(cross_kernel, grid=(stars // CROSS_STEP,), in_specs=[cross...  6.86 us
    all_to_all x1, waiting for transfers between devices, per_device(): parts = lax.all_to_all(parts, cadence_axes, 0, 0, tiled=True)  6.75 us
  transfers between devices with their start and end apart: 2, of which 2 were waited for; matrix products, arithmetic and copies ran while one was open for 1% of the time, Pallas kernels for 12%

profile of v4, /device:TPU:0, one launch (start us, length us, event | category | flops | bytes accessed | tf_op | source)
XLA Modules:
  0.0 98.4 jit_solution(13750092698668753634)
XLA Ops:
  0.6 7.8 %gram.1 = f32[16,152,128]{2,1,0:T(8,128)} custom-call(f32[2048,512]{1,0:T(8,128)} %flux_ref.3, s32[2048,512]{1,0:T(8,128)} %valid_ref.3, s32[2048,512]{1,0:T(8,128)} %quality_hbm.1, f32[16,512]{1,0:T(8,128)} %basis_ref.3), custom_call_target="tpu_custom_call" | custom-call | flops 1258291200 | bytes 14680064 | tf_op jit(solution)/shard_map/gram/pallas_call | solution.py:419
  8.5 8.0 %all-to-all-start = ((f32[16,152,128]{2,1,0:T(8,128)}), f32[16,152,128]{2,1,0:T(8,128)S(1)}, u32[]{:S(2)}, u32[]{:S(2)}) async-start(f32[16,152,128]{2,1,0:T(8,128)} %gram.1), calls=%async_computation | async-start | bytes 2490368 | tf_op jit(solution)/shard_map/all_to_all | solution.py:464
  16.4 0.8 multiply_add_fusion
  17.2 0.1 copy.15
  17.3 0.1 reshape.34.low_ref
  17.4 0.1 copy.14
  17.5 0.1 reshape.31
  17.6 6.9 %cross.1 = (f32[16,272,128]{2,1,0:T(8,128)}, f32[16,128]{1,0:T(8,128)}) custom-call(f32[2048,512]{1,0:T(8,128)} %flux_ref.3, s32[2048,512]{1,0:T(8,128)} %valid_ref.3, f32[16,512]{1,0:T(8,128)} %basis_ref.3, f32[16,512]{1,0:T(8,128)} %decay_ref.1, f32[16,512]{1,0:T(8,128)} %feed_ref.3), custom_call_target="tpu_custom_call" | custom-call | flops 1677721600 | bytes 16777216 | tf_op jit(solution)/shard_map/cross/pallas_call | solution.py:447
  24.5 3.9 %count.1 = (bf16[32,128,256]{2,1,0:T(8,128)(2,1)S(1)}, bf16[32,128,256]{2,1,0:T(8,128)(2,1)S(1)}) custom-call(s32[16,512]{1,0:T(8,128)S(1)} %select_add_fusion.code_ref, s32[16,512]{1,0:T(8,128)S(1)} %reshape.34.low_ref), custom_call_target="tpu_custom_call" | custom-call | flops 4294967296 | bytes 4194304 | tf_op jit(solution)/shard_map/count/pallas_call | solution.py:465
  28.4 1.3 %copy-done.3 = bf16[32,128,256]{2,1,0:T(8,128)(2,1)} copy-done((bf16[32,128,256]{2,1,0:T(8,128)(2,1)}, bf16[32,128,256]{2,1,0:T(8,128)(2,1)S(1)}, u32[]{:S(2)}) %copy-start.3) | copy-done | bytes 2097176
  29.7 6.7 %all-to-all-done.parts_ref = f32[16,152,128]{2,1,0:T(8,128)S(1)} async-done(((f32[16,152,128]{2,1,0:T(8,128)}), f32[16,152,128]{2,1,0:T(8,128)S(1)}, u32[]{:S(2)}, u32[]{:S(2)}) %all-to-all-start) | async-done | bytes 1245216 | tf_op jit(solution)/shard_map/all_to_all | solution.py:464
  36.5 0.1 broadcast_in_dim.4.prec_ref
  36.6 0.4 solve.1
  37.0 18.6 %all_to_all.25.near_ref = f32[64,16,128]{2,1,0:T(8,128)S(1)} all-to-all(f32[64,16,128]{2,1,0:T(8,128)S(1)} %get-tuple-element.43), channel_id=1, replica_groups=mesh['y'=4,'c'=2,'x'=4,'z'=4] {'y','x','z'}, dimensions={0} | all-to-all | bytes 1048576 | tf_op jit(solution)/shard_map/all_to_all | solution.py:491
  55.6 0.8 near.1.begun_ref
  56.5 0.6 noise.1
  57.1 0.4 collective-permute-done.far_ref
  57.5 0.5 copy-done.4
  58.0 0.9 map.1
  58.9 11.1 %all_to_all.26.rows_ref = f32[16,16,128]{2,1,0:T(8,128)S(1)} all-to-all(f32[16,16,128]{2,1,0:T(8,128)S(1)} %map.1), channel_id=1, replica_groups=mesh['y'=4,'c'=2,'x'=4,'z'=4] {'x','z'}, dimensions={0} | all-to-all | bytes 262144 | tf_op jit(solution)/shard_map/all_to_all | solution.py:530
  70.0 0.2 local_carry.1
  70.2 12.0 %all_to_all.27.parts_ref = f32[4,17,16,128]{3,2,1,0:T(8,128)S(1)} all-to-all(f32[4,17,16,128]{3,2,1,0:T(8,128)S(1)} %local_carry.1), channel_id=1, replica_groups=mesh['y'=4,'c'=2,'x'=4,'z'=4] {'z'}, dimensions={0} | all-to-all | bytes 1114112 | tf_op jit(solution)/shard_map/all_to_all | solution.py:542
  82.2 10.8 %all_to_all.28.parts_ref = f32[4,17,16,128]{3,2,1,0:T(8,128)S(1)} all-to-all(f32[4,17,16,128]{3,2,1,0:T(8,128)S(1)} %get-tuple-element.58), channel_id=1, replica_groups=mesh['y'=4,'c'=2,'x'=4,'z'=4] {'x'}, dimensions={0} | all-to-all | bytes 1114112 | tf_op jit(solution)/shard_map/all_to_all | solution.py:555
  93.1 5.4 %whiten.1 = (f32[16,2048]{1,0:T(8,128)}, f32[2048,512]{1,0:T(8,128)}) custom-call(f32[2048,512]{1,0:T(8,128)S(1)} %copy-done, s32[2048,512]{1,0:T(8,128)S(1)} %copy-done.1, f32[16,16,128]{2,1,0:T(8,128)S(1)} %all_to_all.26.rows_ref, f32[16,16,128]{2,1,0:T(8,128)S(1)} %state.1.states_ref, bf16[96,512]{1,0:T(8,128)(2,1)S(1)} %get-tuple-element.60.stack_ref, ...), custom_call_target="tpu_custom_call" | custom-call | flops 3565158400 | bytes 14680064 | tf_op jit(solution)/shard_map/whiten/pallas_call | solution.py:567
  (28 shorter events, 0.2 us)
Async XLA Ops:
  8.5 28.0 %all-to-all-start = ((f32[16,152,128]{2,1,0:T(8,128)}), f32[16,152,128]{2,1,0:T(8,128)S(1)}, u32[]{:S(2)}, u32[]{:S(2)}) async-start(f32[16,152,128]{2,1,0:T(8,128)} %gram.1), calls=%async_computation | async-start | bytes 2490368 | tf_op jit(solution)/shard_map/all_to_all | solution.py:464
  24.5 12.0 %copy-start.11 = (f32[16]{0:T(128)S(1)}, f32[16]{0:T(128)}, u32[]{:S(2)}) copy-start(f32[16]{0:T(128)} %param.15) | copy-start | bytes 196
  28.4 1.3 %copy-start.3 = (bf16[32,128,256]{2,1,0:T(8,128)(2,1)}, bf16[32,128,256]{2,1,0:T(8,128)(2,1)S(1)}, u32[]{:S(2)}) copy-start(bf16[32,128,256]{2,1,0:T(8,128)(2,1)S(1)} %get-tuple-element.54.counts_ref) | copy-start | bytes 6291460
  36.6 19.8 %copy-start.5 = (f32[16,512]{1,0:T(8,128)S(1)}, f32[16,512]{1,0:T(8,128)}, u32[]{:S(2)}) copy-start(f32[16,512]{1,0:T(8,128)} %basis_ref.3) | copy-start | bytes 98308
  36.6 19.9 %copy-start.6 = (f32[16,512]{1,0:T(8,128)S(1)}, f32[16,512]{1,0:T(8,128)}, u32[]{:S(2)}) copy-start(f32[16,512]{1,0:T(8,128)} %decay_ref.1) | copy-start | bytes 98308
  36.6 19.9 %copy-start.7 = (f32[16,512]{1,0:T(8,128)S(1)}, f32[16,512]{1,0:T(8,128)}, u32[]{:S(2)}) copy-start(f32[16,512]{1,0:T(8,128)} %feed_ref.3) | copy-start | bytes 98308
  36.6 19.9 %copy-start.9 = (f32[16,512]{1,0:T(8,128)S(1)}, f32[16,512]{1,0:T(8,128)}, u32[]{:S(2)}) copy-start(f32[16,512]{1,0:T(8,128)} %load_ref.1) | copy-start | bytes 98308
  55.6 1.9 %collective-permute-start = (f32[64,16,128]{2,1,0:T(8,128)S(1)}, f32[64,16,128]{2,1,0:T(8,128)S(1)}, u32[]{:S(2)}, u32[]{:S(2)}) collective-permute-start(f32[64,16,128]{2,1,0:T(8,128)S(1)} %all_to_all.25.near_ref), channel_id=1, source_target_pairs={{0,16},{16,0},{1,17},{17,1},{2,18},{18,2},{3,19},{19,3},{4,20},{20... | collective-permute-start | bytes 1572872 | tf_op jit(solution)/shard_map/ppermute | solution.py:493
  56.4 1.6 %copy-start.4 = (bf16[32,128,256]{2,1,0:T(8,128)(2,1)S(1)}, bf16[32,128,256]{2,1,0:T(8,128)(2,1)}, u32[]{:S(2)}) copy-start(bf16[32,128,256]{2,1,0:T(8,128)(2,1)} %copy-done.3) | copy-start | bytes 6291460
  56.4 13.5 %copy-start.2 = (f32[16,272,128]{2,1,0:T(8,128)S(1)}, f32[16,272,128]{2,1,0:T(8,128)}, u32[]{:S(2)}) copy-start(f32[16,272,128]{2,1,0:T(8,128)} %get-tuple-element.56.crossed_ref) | copy-start | bytes 6684676
  57.1 12.9 %copy-start.8 = (f32[16,128]{1,0:T(8,128)S(1)}, f32[16,128]{1,0:T(8,128)}, u32[]{:S(2)}) copy-start(f32[16,128]{1,0:T(8,128)} %get-tuple-element.57.decayed_ref) | copy-start | bytes 24580
  58.0 35.0 %copy-start.1 = (s32[2048,512]{1,0:T(8,128)S(1)}, s32[2048,512]{1,0:T(8,128)}, u32[]{:S(2)}) copy-start(s32[2048,512]{1,0:T(8,128)} %valid_ref.3) | copy-start | bytes 12582916
  70.0 23.0 %copy-start = (f32[2048,512]{1,0:T(8,128)S(1)}, f32[2048,512]{1,0:T(8,128)}, u32[]{:S(2)}) copy-start(f32[2048,512]{1,0:T(8,128)} %flux_ref.3) | copy-start | bytes 12582916
  70.2 22.9 %copy-start.10 = (f32[512]{0:T(512)S(1)}, f32[512]{0:T(512)}, u32[]{:S(2)}) copy-start(f32[512]{0:T(512)} %param.19) | copy-start | bytes 6148

commit v5 on v4

--- a/solution.py
+++ b/solution.py
@@ -330,46 +330,46 @@
         for k in range(BASIS_VECTORS):
             first = 16 + 16 * k
             carry = carry - coeffs[k : k + 1, :] * crossed_ref[owner, first : first + 16, :]
-        for peer in range(out_ref.shape[0]):
-            out_ref[peer, owner] = carry
-    for peer in range(out_ref.shape[0]):
-        out_ref[peer, owners] = decayed_ref[...]
-
-
-def entering(parts_ref, owner, place):
-    last = parts_ref.shape[1] - 1
-    state = jnp.zeros((NOISE_TERMS, OWN), F32)
-    found = state
-    for block in range(parts_ref.shape[0]):
-        found = jnp.where(place == block, state, found)
-        state = state * parts_ref[block, last] + parts_ref[block, owner]
-    return found, state
-
-
-def level_kernel(parts_ref, inner_ref, out_ref):
+        out_ref[owner] = carry
+    out_ref[owners] = decayed_ref[...]
+
+
+def level_kernel(own_ref, first_ref, second_ref, third_ref, inner_ref, out_ref):
     place = lax.axis_index("z")
-    owners = inner_ref.shape[0] - 1
+    refs = (own_ref, first_ref, second_ref, third_ref)
+    around = len(refs)
+    owners = own_ref.shape[0] - 1
+
+    def of_block(block, row):
+        value = refs[0][row]
+        for back in range(1, around):
+            value = jnp.where(lax.rem(place + around - back, around) == block, refs[back][row], value)
+        return value
+
+    decays = [of_block(block, owners) for block in range(around)]
     for owner in range(owners):
-        found, state = entering(parts_ref, owner, place)
+        state = jnp.zeros((NOISE_TERMS, OWN), F32)
+        found = state
+        for block in range(around):
+            found = jnp.where(place == block, state, found)
+            state = state * decays[block] + of_block(block, owner)
         inner_ref[owner] = found
-        for peer in range(out_ref.shape[0]):
-            out_ref[peer, owner] = state
+        out_ref[owner] = state
     product = jnp.ones((NOISE_TERMS, OWN), F32)
     before = product
-    for block in range(parts_ref.shape[0]):
+    for block in range(around):
         before = jnp.where(place == block, product, before)
-        product = product * parts_ref[block, owners]
+        product = product * decays[block]
     inner_ref[owners] = before
-    for peer in range(out_ref.shape[0]):
-        out_ref[peer, owners] = product
-
-
-def state_kernel(parts_ref, inner_ref, out_ref):
-    place = lax.axis_index("x")
+    out_ref[owners] = product
+
+
+def state_kernel(first_ref, second_ref, third_ref, inner_ref, out_ref):
     owners = out_ref.shape[0]
     for owner in range(owners):
-        found, ignored = entering(parts_ref, owner, place)
-        out_ref[owner] = inner_ref[owner] + inner_ref[owners] * found
+        state = second_ref[owner] + second_ref[owners] * third_ref[owner]
+        state = first_ref[owner] + first_ref[owners] * state
+        out_ref[owner] = inner_ref[owner] + inner_ref[owners] * state
 
 
 def whiten_kernel(
@@ -529,39 +529,43 @@
     )(begun, far, far_counts, prec, kept)
     rows = lax.all_to_all(rows, cadence_axes, 0, 0, tiled=True)
 
-    along_z, along_x = lax.axis_size("z"), lax.axis_size("x")
+    block_shape = jax.ShapeDtypeStruct((blocks + 1, 16, OWN), F32)
     carries = pl.pallas_call(
         carry_kernel,
         in_specs=[vmem()] * 3,
         out_specs=vmem(),
-        out_shape=jax.ShapeDtypeStruct((along_z, blocks + 1, 16, OWN), F32),
+        out_shape=block_shape,
         compiler_params=params(16),
         cost_estimate=cost(1 << 24, 3 * MIB),
         name="local_carry",
     )(rows, crossed, decayed)
-    carries = lax.all_to_all(carries, "z", 0, 0, tiled=True)
-    inner, carries = pl.pallas_call(
+    along_z, along_x = lax.axis_size("z"), lax.axis_size("x")
+    rings = [
+        lax.ppermute(carries, "z", [(i, (i + back) % along_z) for i in range(along_z)])
+        for back in range(1, along_z)
+    ]
+    inner, lines = pl.pallas_call(
         level_kernel,
-        in_specs=[vmem()],
+        in_specs=[vmem()] * 4,
         out_specs=[vmem()] * 2,
-        out_shape=[
-            jax.ShapeDtypeStruct((blocks + 1, 16, OWN), F32),
-            jax.ShapeDtypeStruct((along_x, blocks + 1, 16, OWN), F32),
-        ],
+        out_shape=[block_shape] * 2,
         compiler_params=params(16),
         cost_estimate=cost(1 << 20, MIB),
         name="level",
-    )(carries)
-    carries = lax.all_to_all(carries, "x", 0, 0, tiled=True)
+    )(carries, *rings)
+    earlier = [
+        lax.ppermute(lines, "x", [(i, i + back) for i in range(along_x - back)])
+        for back in range(1, along_x)
+    ]
     states = pl.pallas_call(
         state_kernel,
-        in_specs=[vmem()] * 2,
+        in_specs=[vmem()] * 4,
         out_specs=vmem(),
         out_shape=jax.ShapeDtypeStruct((blocks, 16, OWN), F32),
         compiler_params=params(16),
         cost_estimate=cost(1 << 20, MIB),
         name="state",
-    )(carries, inner)
+    )(*earlier, inner)
 
     part_spec = pl.BlockSpec((WHITEN_CHUNKS, 16, OWN), lambda i: (i, 0, 0))
     coeffs, whitened = pl.pallas_call(

time: 98.9 us -> 97.2 us (0.983)
  blocking collectives: 52.4 us -> 29.8 us
  waiting for transfers between devices: 7.14 us -> 17.1 us
  starting transfers between devices: 7.98 us -> 17.9 us
    all_to_all x2 -> x0, blocking collectives: 22.7 us -> none  [the longest x1 12 us: per_device(): carries = lax.all_to_all(carries, 'z', 0, 0, tiled=True)]
    ppermute x0 -> x6, starting transfers between devices: none -> 9.94 us  [the longest x3 7.07 us: per_device(): lax.ppermute(lines, 'x', [(i, i + back) for i in range(along_x - back)])]
    ppermute x0 -> x6, waiting for transfers between devices: none -> 9.94 us  [the longest x3 7.18 us: per_device(): lax.ppermute(carries, 'z', [(i, (i + back) % along_z) for i in range(alon...]
  transfers between devices with their start and end apart: 2 -> 8, of which waited for: 2 -> 7; matrix products, arithmetic and copies ran while one was open for 1% -> 1% of each run, Pallas kernels for 12% -> 13%
where the time goes in v5:
time: 97.2 us; the launch traced here: 95.8 us
  blocking collectives  29.8 us (31%)
  Pallas kernels  27 us (28%)
  starting transfers between devices  17.9 us (18%)
  waiting for transfers between devices  17.1 us (18%)
  local copies, waits for them, and re-layouts  2.33 us (2%)
    all_to_all x1, blocking collectives, per_device(): near = lax.all_to_all(fitted, nearby, 0, 0, tiled=True)  18.6 us
    all_to_all x1, blocking collectives, per_device(): rows = lax.all_to_all(rows, cadence_axes, 0, 0, tiled=True)  11.2 us
    all_to_all x1, starting transfers between devices, per_device(): parts = lax.all_to_all(parts, cadence_axes, 0, 0, tiled=True)  7.98 us
    pallas_call x1, Pallas kernels, per_device(): pl.pallas_call(gram_kernel, in_specs=[in_hbm] * 3 + [vmem()], out_specs=v...  7.8 us
    ppermute x3, waiting for transfers between devices, per_device(): lax.ppermute(carries, 'z', [(i, (i + back) % along_z) for i in range(alon...  7.18 us
    ppermute x3, starting transfers between devices, per_device(): lax.ppermute(lines, 'x', [(i, i + back) for i in range(along_x - back)])  7.07 us
    pallas_call x1, Pallas kernels, per_device(): pl.pallas_call(cross_kernel, grid=(stars // CROSS_STEP,), in_specs=[cross...  6.84 us
    all_to_all x1, waiting for transfers between devices, per_device(): parts = lax.all_to_all(parts, cadence_axes, 0, 0, tiled=True)  6.75 us
  transfers between devices with their start and end apart: 8, of which 7 were waited for; matrix products, arithmetic and copies ran while one was open for 1% of the time, Pallas kernels for 13%

profile of v5, /device:TPU:0, one launch (start us, length us, event | category | flops | bytes accessed | tf_op | source)
XLA Modules:
  0.0 95.8 jit_solution(10715763814414312577)
XLA Ops:
  0.6 7.8 %gram.1 = f32[16,152,128]{2,1,0:T(8,128)} custom-call(f32[2048,512]{1,0:T(8,128)} %flux_ref.3, s32[2048,512]{1,0:T(8,128)} %valid_ref.3, s32[2048,512]{1,0:T(8,128)} %quality_hbm.1, f32[16,512]{1,0:T(8,128)} %basis_ref.3), custom_call_target="tpu_custom_call" | custom-call | flops 1258291200 | bytes 14680064 | tf_op jit(solution)/shard_map/gram/pallas_call | solution.py:419
  8.4 8.0 %all-to-all-start = ((f32[16,152,128]{2,1,0:T(8,128)}), f32[16,152,128]{2,1,0:T(8,128)S(1)}, u32[]{:S(2)}, u32[]{:S(2)}) async-start(f32[16,152,128]{2,1,0:T(8,128)} %gram.1), calls=%async_computation | async-start | bytes 2490368 | tf_op jit(solution)/shard_map/all_to_all | solution.py:464
  16.4 0.8 multiply_add_fusion
  17.6 6.8 %cross.1 = (f32[16,272,128]{2,1,0:T(8,128)}, f32[16,128]{1,0:T(8,128)}) custom-call(f32[2048,512]{1,0:T(8,128)} %flux_ref.3, s32[2048,512]{1,0:T(8,128)} %valid_ref.3, f32[16,512]{1,0:T(8,128)} %basis_ref.3, f32[16,512]{1,0:T(8,128)} %decay_ref.1, f32[16,512]{1,0:T(8,128)} %feed_ref.3), custom_call_target="tpu_custom_call" | custom-call | flops 1677721600 | bytes 16777216 | tf_op jit(solution)/shard_map/cross/pallas_call | solution.py:447
  24.5 3.9 %count.1 = (bf16[32,128,256]{2,1,0:T(8,128)(2,1)S(1)}, bf16[32,128,256]{2,1,0:T(8,128)(2,1)S(1)}) custom-call(s32[16,512]{1,0:T(8,128)S(1)} %select_add_fusion.code_ref, s32[16,512]{1,0:T(8,128)S(1)} %reshape.34.low_ref), custom_call_target="tpu_custom_call" | custom-call | flops 4294967296 | bytes 4194304 | tf_op jit(solution)/shard_map/count/pallas_call | solution.py:465
  28.4 1.3 %copy-done.3 = bf16[32,128,256]{2,1,0:T(8,128)(2,1)} copy-done((bf16[32,128,256]{2,1,0:T(8,128)(2,1)}, bf16[32,128,256]{2,1,0:T(8,128)(2,1)S(1)}, u32[]{:S(2)}) %copy-start.3) | copy-done | bytes 2097176
  29.7 6.7 %all-to-all-done.parts_ref = f32[16,152,128]{2,1,0:T(8,128)S(1)} async-done(((f32[16,152,128]{2,1,0:T(8,128)}), f32[16,152,128]{2,1,0:T(8,128)S(1)}, u32[]{:S(2)}, u32[]{:S(2)}) %all-to-all-start) | async-done | bytes 1245216 | tf_op jit(solution)/shard_map/all_to_all | solution.py:464
  37.0 18.6 %all_to_all.15.near_ref = f32[64,16,128]{2,1,0:T(8,128)S(1)} all-to-all(f32[64,16,128]{2,1,0:T(8,128)S(1)} %get-tuple-element.43), channel_id=1, replica_groups=mesh['y'=4,'c'=2,'x'=4,'z'=4] {'y','x','z'}, dimensions={0} | all-to-all | bytes 1048576 | tf_op jit(solution)/shard_map/all_to_all | solution.py:491
  55.6 0.8 near.1.begun_ref
  56.5 0.6 noise.1
  57.5 0.5 copy-done.4
  58.0 0.9 map.1
  58.9 11.2 %all_to_all.16.rows_ref = f32[16,16,128]{2,1,0:T(8,128)S(1)} all-to-all(f32[16,16,128]{2,1,0:T(8,128)S(1)} %map.1), channel_id=1, replica_groups=mesh['y'=4,'c'=2,'x'=4,'z'=4] {'x','z'}, dimensions={0} | all-to-all | bytes 262144 | tf_op jit(solution)/shard_map/all_to_all | solution.py:530
  70.3 1.2 %collective-permute-start.3 = (f32[17,16,128]{2,1,0:T(8,128)S(1)}, f32[17,16,128]{2,1,0:T(8,128)S(1)}, u32[]{:S(2)}, u32[]{:S(2)}) collective-permute-start(f32[17,16,128]{2,1,0:T(8,128)S(1)} %local_carry.1.own_ref), channel_id=1, source_target_pairs={{0,3},{1,0},{2,1},{3,2},{4,7},{5,4},{6,5},{7,6},{8,11},{9,8},{10,9... | collective-permute-start | bytes 417800 | tf_op jit(solution)/shard_map/ppermute | solution.py:544
  71.5 1.5 %collective-permute-start.2 = (f32[17,16,128]{2,1,0:T(8,128)S(1)}, f32[17,16,128]{2,1,0:T(8,128)S(1)}, u32[]{:S(2)}, u32[]{:S(2)}) collective-permute-start(f32[17,16,128]{2,1,0:T(8,128)S(1)} %local_carry.1.own_ref), channel_id=1, source_target_pairs={{0,2},{1,3},{2,0},{3,1},{4,6},{5,7},{6,4},{7,5},{8,10},{9,11},{10,... | collective-permute-start | bytes 417800 | tf_op jit(solution)/shard_map/ppermute | solution.py:544
  73.2 3.2 %collective-permute-done.3.third_ref = f32[17,16,128]{2,1,0:T(8,128)S(1)} collective-permute-done((f32[17,16,128]{2,1,0:T(8,128)S(1)}, f32[17,16,128]{2,1,0:T(8,128)S(1)}, u32[]{:S(2)}, u32[]{:S(2)}) %collective-permute-start.3) | collective-permute-done | bytes 139296 | tf_op jit(solution)/shard_map/ppermute | solution.py:544
  76.4 2.5 %collective-permute-done.2.second_ref = f32[17,16,128]{2,1,0:T(8,128)S(1)} collective-permute-done((f32[17,16,128]{2,1,0:T(8,128)S(1)}, f32[17,16,128]{2,1,0:T(8,128)S(1)}, u32[]{:S(2)}, u32[]{:S(2)}) %collective-permute-start.2) | collective-permute-done | bytes 139296 | tf_op jit(solution)/shard_map/ppermute | solution.py:544
  78.9 1.4 %collective-permute-done.1.first_ref = f32[17,16,128]{2,1,0:T(8,128)S(1)} collective-permute-done((f32[17,16,128]{2,1,0:T(8,128)S(1)}, f32[17,16,128]{2,1,0:T(8,128)S(1)}, u32[]{:S(2)}, u32[]{:S(2)}) %collective-permute-start.1) | collective-permute-done | bytes 139296 | tf_op jit(solution)/shard_map/ppermute | solution.py:544
  80.5 3.0 %collective-permute-start.6 = (f32[17,16,128]{2,1,0:T(8,128)S(1)}, f32[17,16,128]{2,1,0:T(8,128)S(1)}, u32[]{:S(2)}, u32[]{:S(2)}) collective-permute-start(f32[17,16,128]{2,1,0:T(8,128)S(1)} %get-tuple-element.58), channel_id=1, source_target_pairs={{0,12},{1,13},{2,14},{3,15},{16,28},{17,29},{18,30},{19,31},{32,44... | collective-permute-start | bytes 417800 | tf_op jit(solution)/shard_map/ppermute | solution.py:557
  83.5 1.3 %collective-permute-start.5 = (f32[17,16,128]{2,1,0:T(8,128)S(1)}, f32[17,16,128]{2,1,0:T(8,128)S(1)}, u32[]{:S(2)}, u32[]{:S(2)}) collective-permute-start(f32[17,16,128]{2,1,0:T(8,128)S(1)} %get-tuple-element.58), channel_id=1, source_target_pairs={{0,8},{4,12},{1,9},{5,13},{2,10},{6,14},{3,11},{7,15},{16,24},{20,... | collective-permute-start | bytes 417800 | tf_op jit(solution)/shard_map/ppermute | solution.py:557
  84.8 2.8 %collective-permute-start.4 = (f32[17,16,128]{2,1,0:T(8,128)S(1)}, f32[17,16,128]{2,1,0:T(8,128)S(1)}, u32[]{:S(2)}, u32[]{:S(2)}) collective-permute-start(f32[17,16,128]{2,1,0:T(8,128)S(1)} %get-tuple-element.58), channel_id=1, source_target_pairs={{0,4},{4,8},{8,12},{1,5},{5,9},{9,13},{2,6},{6,10},{10,14},{3,7},{... | collective-permute-start | bytes 417800 | tf_op jit(solution)/shard_map/ppermute | solution.py:557
  87.6 1.0 %collective-permute-done.6.third_ref = f32[17,16,128]{2,1,0:T(8,128)S(1)} collective-permute-done((f32[17,16,128]{2,1,0:T(8,128)S(1)}, f32[17,16,128]{2,1,0:T(8,128)S(1)}, u32[]{:S(2)}, u32[]{:S(2)}) %collective-permute-start.6) | collective-permute-done | bytes 139296 | tf_op jit(solution)/shard_map/ppermute | solution.py:557
  88.6 1.8 %collective-permute-done.4.first_ref = f32[17,16,128]{2,1,0:T(8,128)S(1)} collective-permute-done((f32[17,16,128]{2,1,0:T(8,128)S(1)}, f32[17,16,128]{2,1,0:T(8,128)S(1)}, u32[]{:S(2)}, u32[]{:S(2)}) %collective-permute-start.4) | collective-permute-done | bytes 139296 | tf_op jit(solution)/shard_map/ppermute | solution.py:557
  90.4 5.4 %whiten.1 = (f32[16,2048]{1,0:T(8,128)}, f32[2048,512]{1,0:T(8,128)}) custom-call(f32[2048,512]{1,0:T(8,128)S(1)} %copy-done, s32[2048,512]{1,0:T(8,128)S(1)} %copy-done.1, f32[16,16,128]{2,1,0:T(8,128)S(1)} %all_to_all.16.rows_ref, f32[16,16,128]{2,1,0:T(8,128)S(1)} %state.1.states_ref, bf16[96,512]{1,0:T(8,128)(2,1)S(1)} %get-tuple-element.60.stack_ref, ...), custom_call_target="tpu_custom_call" | custom-call | flops 3565158400 | bytes 14680064 | tf_op jit(solution)/shard_map/whiten/pallas_call | solution.py:571
  (38 shorter events, 1.8 us)
Async XLA Ops:
  8.4 28.0 %all-to-all-start = ((f32[16,152,128]{2,1,0:T(8,128)}), f32[16,152,128]{2,1,0:T(8,128)S(1)}, u32[]{:S(2)}, u32[]{:S(2)}) async-start(f32[16,152,128]{2,1,0:T(8,128)} %gram.1), calls=%async_computation | async-start | bytes 2490368 | tf_op jit(solution)/shard_map/all_to_all | solution.py:464
  24.5 12.0 %copy-start.11 = (f32[16]{0:T(128)S(1)}, f32[16]{0:T(128)}, u32[]{:S(2)}) copy-start(f32[16]{0:T(128)} %param.15) | copy-start | bytes 196
  28.4 1.3 %copy-start.3 = (bf16[32,128,256]{2,1,0:T(8,128)(2,1)}, bf16[32,128,256]{2,1,0:T(8,128)(2,1)S(1)}, u32[]{:S(2)}) copy-start(bf16[32,128,256]{2,1,0:T(8,128)(2,1)S(1)} %get-tuple-element.54.counts_ref) | copy-start | bytes 6291460
  36.5 19.8 %copy-start.5 = (f32[16,512]{1,0:T(8,128)S(1)}, f32[16,512]{1,0:T(8,128)}, u32[]{:S(2)}) copy-start(f32[16,512]{1,0:T(8,128)} %basis_ref.3) | copy-start | bytes 98308
  36.5 19.9 %copy-start.6 = (f32[16,512]{1,0:T(8,128)S(1)}, f32[16,512]{1,0:T(8,128)}, u32[]{:S(2)}) copy-start(f32[16,512]{1,0:T(8,128)} %decay_ref.1) | copy-start | bytes 98308
  36.5 19.9 %copy-start.7 = (f32[16,512]{1,0:T(8,128)S(1)}, f32[16,512]{1,0:T(8,128)}, u32[]{:S(2)}) copy-start(f32[16,512]{1,0:T(8,128)} %feed_ref.3) | copy-start | bytes 98308
  36.6 19.9 %copy-start.9 = (f32[16,512]{1,0:T(8,128)S(1)}, f32[16,512]{1,0:T(8,128)}, u32[]{:S(2)}) copy-start(f32[16,512]{1,0:T(8,128)} %load_ref.1) | copy-start | bytes 98308
  55.6 1.9 %collective-permute-start = (f32[64,16,128]{2,1,0:T(8,128)S(1)}, f32[64,16,128]{2,1,0:T(8,128)S(1)}, u32[]{:S(2)}, u32[]{:S(2)}) collective-permute-start(f32[64,16,128]{2,1,0:T(8,128)S(1)} %all_to_all.15.near_ref), channel_id=1, source_target_pairs={{0,16},{16,0},{1,17},{17,1},{2,18},{18,2},{3,19},{19,3},{4,20},{20... | collective-permute-start | bytes 1572872 | tf_op jit(solution)/shard_map/ppermute | solution.py:493
  56.4 1.6 %copy-start.4 = (bf16[32,128,256]{2,1,0:T(8,128)(2,1)S(1)}, bf16[32,128,256]{2,1,0:T(8,128)(2,1)}, u32[]{:S(2)}) copy-start(bf16[32,128,256]{2,1,0:T(8,128)(2,1)} %copy-done.3) | copy-start | bytes 6291460
  56.4 34.0 %copy-start.1 = (s32[2048,512]{1,0:T(8,128)S(1)}, s32[2048,512]{1,0:T(8,128)}, u32[]{:S(2)}) copy-start(s32[2048,512]{1,0:T(8,128)} %valid_ref.3) | copy-start | bytes 12582916
  57.1 13.0 %copy-start.2 = (f32[16,272,128]{2,1,0:T(8,128)S(1)}, f32[16,272,128]{2,1,0:T(8,128)}, u32[]{:S(2)}) copy-start(f32[16,272,128]{2,1,0:T(8,128)} %get-tuple-element.56.crossed_ref) | copy-start | bytes 6684676
  57.1 13.0 %copy-start.8 = (f32[16,128]{1,0:T(8,128)S(1)}, f32[16,128]{1,0:T(8,128)}, u32[]{:S(2)}) copy-start(f32[16,128]{1,0:T(8,128)} %get-tuple-element.57.decayed_ref) | copy-start | bytes 24580
  58.0 32.4 %copy-start = (f32[2048,512]{1,0:T(8,128)S(1)}, f32[2048,512]{1,0:T(8,128)}, u32[]{:S(2)}) copy-start(f32[2048,512]{1,0:T(8,128)} %flux_ref.3) | copy-start | bytes 12582916
  58.9 31.5 %copy-start.10 = (f32[512]{0:T(512)S(1)}, f32[512]{0:T(512)}, u32[]{:S(2)}) copy-start(f32[512]{0:T(512)} %param.19) | copy-start | bytes 6148
  70.3 6.1 %collective-permute-start.3 = (f32[17,16,128]{2,1,0:T(8,128)S(1)}, f32[17,16,128]{2,1,0:T(8,128)S(1)}, u32[]{:S(2)}, u32[]{:S(2)}) collective-permute-start(f32[17,16,128]{2,1,0:T(8,128)S(1)} %local_carry.1.own_ref), channel_id=1, source_target_pairs={{0,3},{1,0},{2,1},{3,2},{4,7},{5,4},{6,5},{7,6},{8,11},{9,8},{10,9... | collective-permute-start | bytes 417800 | tf_op jit(solution)/shard_map/ppermute | solution.py:544
  71.5 7.4 %collective-permute-start.2 = (f32[17,16,128]{2,1,0:T(8,128)S(1)}, f32[17,16,128]{2,1,0:T(8,128)S(1)}, u32[]{:S(2)}, u32[]{:S(2)}) collective-permute-start(f32[17,16,128]{2,1,0:T(8,128)S(1)} %local_carry.1.own_ref), channel_id=1, source_target_pairs={{0,2},{1,3},{2,0},{3,1},{4,6},{5,7},{6,4},{7,5},{8,10},{9,11},{10,... | collective-permute-start | bytes 417800 | tf_op jit(solution)/shard_map/ppermute | solution.py:544
  73.0 7.4 %collective-permute-start.1 = (f32[17,16,128]{2,1,0:T(8,128)S(1)}, f32[17,16,128]{2,1,0:T(8,128)S(1)}, u32[]{:S(2)}, u32[]{:S(2)}) collective-permute-start(f32[17,16,128]{2,1,0:T(8,128)S(1)} %local_carry.1.own_ref), channel_id=1, source_target_pairs={{0,1},{1,2},{2,3},{3,0},{4,5},{5,6},{6,7},{7,4},{8,9},{9,10},{10,1... | collective-permute-start | bytes 417800 | tf_op jit(solution)/shard_map/ppermute | solution.py:544
  80.5 8.1 %collective-permute-start.6 = (f32[17,16,128]{2,1,0:T(8,128)S(1)}, f32[17,16,128]{2,1,0:T(8,128)S(1)}, u32[]{:S(2)}, u32[]{:S(2)}) collective-permute-start(f32[17,16,128]{2,1,0:T(8,128)S(1)} %get-tuple-element.58), channel_id=1, source_target_pairs={{0,12},{1,13},{2,14},{3,15},{16,28},{17,29},{18,30},{19,31},{32,44... | collective-permute-start | bytes 417800 | tf_op jit(solution)/shard_map/ppermute | solution.py:557
  83.5 5.1 %collective-permute-start.5 = (f32[17,16,128]{2,1,0:T(8,128)S(1)}, f32[17,16,128]{2,1,0:T(8,128)S(1)}, u32[]{:S(2)}, u32[]{:S(2)}) collective-permute-start(f32[17,16,128]{2,1,0:T(8,128)S(1)} %get-tuple-element.58), channel_id=1, source_target_pairs={{0,8},{4,12},{1,9},{5,13},{2,10},{6,14},{3,11},{7,15},{16,24},{20,... | collective-permute-start | bytes 417800 | tf_op jit(solution)/shard_map/ppermute | solution.py:557
  84.8 5.5 %collective-permute-start.4 = (f32[17,16,128]{2,1,0:T(8,128)S(1)}, f32[17,16,128]{2,1,0:T(8,128)S(1)}, u32[]{:S(2)}, u32[]{:S(2)}) collective-permute-start(f32[17,16,128]{2,1,0:T(8,128)S(1)} %get-tuple-element.58), channel_id=1, source_target_pairs={{0,4},{4,8},{8,12},{1,5},{5,9},{9,13},{2,6},{6,10},{10,14},{3,7},{... | collective-permute-start | bytes 417800 | tf_op jit(solution)/shard_map/ppermute | solution.py:557

commit v6 on v5

--- a/solution.py
+++ b/solution.py
@@ -20,7 +20,9 @@
 CHUNKS = STEP // OWN
 GRAM_ROWS = PAIRS + 16
 CROSS_ROWS = 16 + BASIS_VECTORS * NOISE_TERMS
-WHITEN_STEP = 1024
+WHITEN_STEP = 512
+FINISH_STEP = 512
+FINISH_CHUNKS = FINISH_STEP // OWN
 WHITEN_CHUNKS = WHITEN_STEP // OWN
 
 F32 = jnp.float32
@@ -372,17 +374,13 @@
         out_ref[owner] = inner_ref[owner] + inner_ref[owners] * state
 
 
-def whiten_kernel(
-    flux_ref, valid_ref, rows_ref, states_ref, stack_ref, entry_ref, high_ref, low_ref, scale_ref, coeffs_ref, out_ref
-):
+def local_kernel(flux_ref, valid_ref, rows_ref, stack_ref, high_ref, low_ref, coeffs_ref, out_ref):
     coeffs = jnp.concatenate([rows_ref[chunk] for chunk in range(WHITEN_CHUNKS)], axis=1)
-    states = jnp.concatenate([states_ref[chunk] for chunk in range(WHITEN_CHUNKS)], axis=1)
     coeffs_ref[...] = coeffs
     trend = dot_tn(left_stack(coeffs), stack_ref[...])
     first = pl.multiple_of(pl.program_id(0) * WHITEN_STEP, WHITEN_STEP)
-    stars = pl.ds(first, WHITEN_STEP)
-    residual = jnp.where(valid_ref[stars, :] != 0, flux_ref[stars, :] - trend, 0.0)
-    incoming = dot_tn(left_stack(states), entry_ref[...])
+    span = pl.ds(first, WHITEN_STEP)
+    residual = jnp.where(valid_ref[span, :] != 0, flux_ref[span, :] - trend, 0.0)
     high = residual.astype(BF16)
     low = (residual - high.astype(F32)).astype(BF16)
     count = residual.shape[1]
@@ -391,7 +389,14 @@
         upto = slice(0, first + 256)
         local = dot_nn(low[:, upto], high_ref[upto, lanes]) + dot_nn(high[:, upto], low_ref[upto, lanes])
         local = local + dot_nn(high[:, upto], high_ref[upto, lanes])
-        out_ref[:, lanes] = (residual[:, lanes] - local - incoming[:, lanes]) * scale_ref[:, lanes]
+        out_ref[:, lanes] = residual[:, lanes] - local
+
+
+def finish_kernel(local_ref, states_ref, entry_ref, scale_ref, out_ref):
+    states = jnp.concatenate([states_ref[chunk] for chunk in range(FINISH_CHUNKS)], axis=1)
+    incoming = dot_tn(left_stack(states), entry_ref[...])
+    first = pl.multiple_of(pl.program_id(0) * FINISH_STEP, FINISH_STEP)
+    out_ref[...] = (local_ref[pl.ds(first, FINISH_STEP), :] - incoming) * scale_ref[...]
 
 
 def vmem():
@@ -553,6 +558,21 @@
         cost_estimate=cost(1 << 20, MIB),
         name="level",
     )(carries, *rings)
+    part_spec = pl.BlockSpec((WHITEN_CHUNKS, 16, OWN), lambda i: (i, 0, 0))
+    tall_spec = pl.BlockSpec((WHITEN_STEP, cadences), lambda i: (i, 0))
+    coeffs, local = pl.pallas_call(
+        local_kernel,
+        grid=(stars // WHITEN_STEP,),
+        in_specs=[vmem(), vmem(), part_spec] + [vmem()] * 3,
+        out_specs=[pl.BlockSpec((16, WHITEN_STEP), lambda i: (0, i)), tall_spec],
+        out_shape=[
+            jax.ShapeDtypeStruct((16, stars), F32),
+            jax.ShapeDtypeStruct((stars, cadences), F32),
+        ],
+        compiler_params=params(24),
+        cost_estimate=cost(2 * stars * cadences * 1500, 14 * MIB),
+        name="local",
+    )(flux, valid, rows, stack, high, low)
     earlier = [
         lax.ppermute(lines, "x", [(i, i + back) for i in range(along_x - back)])
         for back in range(1, along_x)
@@ -567,23 +587,21 @@
         name="state",
     )(*earlier, inner)
 
-    part_spec = pl.BlockSpec((WHITEN_CHUNKS, 16, OWN), lambda i: (i, 0, 0))
-    coeffs, whitened = pl.pallas_call(
-        whiten_kernel,
-        grid=(stars // WHITEN_STEP,),
-        in_specs=[vmem(), vmem(), part_spec, part_spec] + [vmem()] * 5,
-        out_specs=[
-            pl.BlockSpec((16, WHITEN_STEP), lambda i: (0, i)),
-            pl.BlockSpec((WHITEN_STEP, cadences), lambda i: (i, 0)),
+    whitened = pl.pallas_call(
+        finish_kernel,
+        grid=(stars // FINISH_STEP,),
+        in_specs=[
+            vmem(),
+            pl.BlockSpec((FINISH_CHUNKS, 16, OWN), lambda i: (i, 0, 0)),
+            vmem(),
+            vmem(),
         ],
-        out_shape=[
-            jax.ShapeDtypeStruct((16, stars), F32),
-            jax.ShapeDtypeStruct((stars, cadences), F32),
-        ],
-        compiler_params=params(32),
-        cost_estimate=cost(2 * stars * cadences * 1700, 14 * MIB),
-        name="whiten",
-    )(flux, valid, rows, states, stack, entry, high, low, inv_diag[None, :])
+        out_specs=pl.BlockSpec((FINISH_STEP, cadences), lambda i: (i, 0)),
+        out_shape=jax.ShapeDtypeStruct((stars, cadences), F32),
+        compiler_params=params(16),
+        cost_estimate=cost(2 * stars * cadences * 100, 9 * MIB),
+        name="finish",
+    )(local, states, entry, inv_diag[None, :])
     return coeffs.T, whitened
 
 

time: 97.2 us -> 94.8 us (0.975)
  waiting for transfers between devices: 17.1 us -> 14 us
  Pallas kernels: 27 us -> 29.1 us
    ppermute x3, waiting for transfers between devices: 2.76 us -> 0.01 us  [per_device(): lax.ppermute(lines, 'x', [(i, i + back) for i in range(along_x - back)])]
    pallas_call x1 -> x2, Pallas kernels: 5.38 us -> 7.55 us  [the longest x1 4.58 us: per_device(): pl.pallas_call(local_kernel, grid=(stars // WHITEN_STEP,), in_specs=[vmem...]
  transfers between devices with their start and end apart: 8 -> 8, of which waited for: 7 -> 5; matrix products, arithmetic and copies ran while one was open for 1% -> 1% of each run, Pallas kernels for 13% -> 18%
where the time goes in v6:
time: 94.8 us; the launch traced here: 94.3 us
  blocking collectives  29.7 us (31%)
  Pallas kernels  29.1 us (31%)
  starting transfers between devices  18 us (19%)
  waiting for transfers between devices  14 us (15%)
  local copies, waits for them, and re-layouts  1.81 us (2%)
    all_to_all x1, blocking collectives, per_device(): near = lax.all_to_all(fitted, nearby, 0, 0, tiled=True)  18.6 us
    all_to_all x1, blocking collectives, per_device(): rows = lax.all_to_all(rows, cadence_axes, 0, 0, tiled=True)  11.1 us
    all_to_all x1, starting transfers between devices, per_device(): parts = lax.all_to_all(parts, cadence_axes, 0, 0, tiled=True)  7.98 us
    pallas_call x1, Pallas kernels, per_device(): pl.pallas_call(gram_kernel, in_specs=[in_hbm] * 3 + [vmem()], out_specs=v...  7.8 us
    ppermute x3, starting transfers between devices, per_device(): lax.ppermute(lines, 'x', [(i, i + back) for i in range(along_x - back)])  7.01 us
    ppermute x3, waiting for transfers between devices, per_device(): lax.ppermute(carries, 'z', [(i, (i + back) % along_z) for i in range(alon...  6.86 us
    pallas_call x1, Pallas kernels, per_device(): pl.pallas_call(cross_kernel, grid=(stars // CROSS_STEP,), in_specs=[cross...  6.84 us
    all_to_all x1, waiting for transfers between devices, per_device(): parts = lax.all_to_all(parts, cadence_axes, 0, 0, tiled=True)  6.73 us
  transfers between devices with their start and end apart: 8, of which 5 were waited for; matrix products, arithmetic and copies ran while one was open for 1% of the time, Pallas kernels for 18%

profile of v6, /device:TPU:0, one launch (start us, length us, event | category | flops | bytes accessed | tf_op | source)
XLA Modules:
  0.0 94.3 jit_solution(5780486225024199936)
XLA Ops:
  0.6 7.8 %gram.1 = f32[16,152,128]{2,1,0:T(8,128)} custom-call(f32[2048,512]{1,0:T(8,128)} %flux_ref.3, s32[2048,512]{1,0:T(8,128)} %valid_ref.3, s32[2048,512]{1,0:T(8,128)} %quality_hbm.1, f32[16,512]{1,0:T(8,128)} %basis_ref.3), custom_call_target="tpu_custom_call" | custom-call | flops 1258291200 | bytes 14680064 | tf_op jit(solution)/shard_map/gram/pallas_call | solution.py:424
  8.4 8.0 %all-to-all-start = ((f32[16,152,128]{2,1,0:T(8,128)}), f32[16,152,128]{2,1,0:T(8,128)S(1)}, u32[]{:S(2)}, u32[]{:S(2)}) async-start(f32[16,152,128]{2,1,0:T(8,128)} %gram.1), calls=%async_computation | async-start | bytes 2490368 | tf_op jit(solution)/shard_map/all_to_all | solution.py:469
  16.4 0.8 multiply_add_fusion
  17.6 6.8 %cross.1 = (f32[16,272,128]{2,1,0:T(8,128)}, f32[16,128]{1,0:T(8,128)}) custom-call(f32[2048,512]{1,0:T(8,128)} %flux_ref.3, s32[2048,512]{1,0:T(8,128)} %valid_ref.3, f32[16,512]{1,0:T(8,128)} %basis_ref.3, f32[16,512]{1,0:T(8,128)} %decay_ref.1, f32[16,512]{1,0:T(8,128)} %feed_ref.3), custom_call_target="tpu_custom_call" | custom-call | flops 1677721600 | bytes 16777216 | tf_op jit(solution)/shard_map/cross/pallas_call | solution.py:452
  24.5 3.9 %count.1 = (bf16[32,128,256]{2,1,0:T(8,128)(2,1)S(1)}, bf16[32,128,256]{2,1,0:T(8,128)(2,1)S(1)}) custom-call(s32[16,512]{1,0:T(8,128)S(1)} %select_add_fusion.code_ref, s32[16,512]{1,0:T(8,128)S(1)} %reshape.34.low_ref), custom_call_target="tpu_custom_call" | custom-call | flops 4294967296 | bytes 4194304 | tf_op jit(solution)/shard_map/count/pallas_call | solution.py:470
  28.4 1.3 %copy-done.3 = bf16[32,128,256]{2,1,0:T(8,128)(2,1)} copy-done((bf16[32,128,256]{2,1,0:T(8,128)(2,1)}, bf16[32,128,256]{2,1,0:T(8,128)(2,1)S(1)}, u32[]{:S(2)}) %copy-start.3) | copy-done | bytes 2097176
  29.7 6.7 %all-to-all-done.parts_ref = f32[16,152,128]{2,1,0:T(8,128)S(1)} async-done(((f32[16,152,128]{2,1,0:T(8,128)}), f32[16,152,128]{2,1,0:T(8,128)S(1)}, u32[]{:S(2)}, u32[]{:S(2)}) %all-to-all-start) | async-done | bytes 1245216 | tf_op jit(solution)/shard_map/all_to_all | solution.py:469
  36.5 0.4 solve.1
  37.0 18.6 %all_to_all.15.near_ref = f32[64,16,128]{2,1,0:T(8,128)S(1)} all-to-all(f32[64,16,128]{2,1,0:T(8,128)S(1)} %get-tuple-element.43), channel_id=1, replica_groups=mesh['y'=4,'c'=2,'x'=4,'z'=4] {'y','x','z'}, dimensions={0} | all-to-all | bytes 1048576 | tf_op jit(solution)/shard_map/all_to_all | solution.py:496
  55.6 0.8 near.1.begun_ref
  56.5 0.6 noise.1
  57.5 0.8 map.1
  58.3 11.1 %all_to_all.16.rows_ref = f32[16,16,128]{2,1,0:T(8,128)S(1)} all-to-all(f32[16,16,128]{2,1,0:T(8,128)S(1)} %map.1), channel_id=1, replica_groups=mesh['y'=4,'c'=2,'x'=4,'z'=4] {'x','z'}, dimensions={0} | all-to-all | bytes 262144 | tf_op jit(solution)/shard_map/all_to_all | solution.py:535
  69.6 1.3 %collective-permute-start.3 = (f32[17,16,128]{2,1,0:T(8,128)S(1)}, f32[17,16,128]{2,1,0:T(8,128)S(1)}, u32[]{:S(2)}, u32[]{:S(2)}) collective-permute-start(f32[17,16,128]{2,1,0:T(8,128)S(1)} %local_carry.1.own_ref), channel_id=1, source_target_pairs={{0,3},{1,0},{2,1},{3,2},{4,7},{5,4},{6,5},{7,6},{8,11},{9,8},{10,9... | collective-permute-start | bytes 417800 | tf_op jit(solution)/shard_map/ppermute | solution.py:549
  70.9 1.3 %collective-permute-start.2 = (f32[17,16,128]{2,1,0:T(8,128)S(1)}, f32[17,16,128]{2,1,0:T(8,128)S(1)}, u32[]{:S(2)}, u32[]{:S(2)}) collective-permute-start(f32[17,16,128]{2,1,0:T(8,128)S(1)} %local_carry.1.own_ref), channel_id=1, source_target_pairs={{0,2},{1,3},{2,0},{3,1},{4,6},{5,7},{6,4},{7,5},{8,10},{9,11},{10,... | collective-permute-start | bytes 417800 | tf_op jit(solution)/shard_map/ppermute | solution.py:549
  72.2 0.4 collective-permute-start.1
  72.6 2.9 %collective-permute-done.3.third_ref = f32[17,16,128]{2,1,0:T(8,128)S(1)} collective-permute-done((f32[17,16,128]{2,1,0:T(8,128)S(1)}, f32[17,16,128]{2,1,0:T(8,128)S(1)}, u32[]{:S(2)}, u32[]{:S(2)}) %collective-permute-start.3) | collective-permute-done | bytes 139296 | tf_op jit(solution)/shard_map/ppermute | solution.py:549
  75.5 2.5 %collective-permute-done.2.second_ref = f32[17,16,128]{2,1,0:T(8,128)S(1)} collective-permute-done((f32[17,16,128]{2,1,0:T(8,128)S(1)}, f32[17,16,128]{2,1,0:T(8,128)S(1)}, u32[]{:S(2)}, u32[]{:S(2)}) %collective-permute-start.2) | collective-permute-done | bytes 139296 | tf_op jit(solution)/shard_map/ppermute | solution.py:549
  78.1 1.4 %collective-permute-done.1.first_ref = f32[17,16,128]{2,1,0:T(8,128)S(1)} collective-permute-done((f32[17,16,128]{2,1,0:T(8,128)S(1)}, f32[17,16,128]{2,1,0:T(8,128)S(1)}, u32[]{:S(2)}, u32[]{:S(2)}) %collective-permute-start.1) | collective-permute-done | bytes 139296 | tf_op jit(solution)/shard_map/ppermute | solution.py:549
  79.6 2.9 %collective-permute-start.6 = (f32[17,16,128]{2,1,0:T(8,128)S(1)}, f32[17,16,128]{2,1,0:T(8,128)S(1)}, u32[]{:S(2)}, u32[]{:S(2)}) collective-permute-start(f32[17,16,128]{2,1,0:T(8,128)S(1)} %get-tuple-element.63), channel_id=1, source_target_pairs={{0,12},{1,13},{2,14},{3,15},{16,28},{17,29},{18,30},{19,31},{32,44... | collective-permute-start | bytes 417800 | tf_op jit(solution)/shard_map/ppermute | solution.py:577
  82.6 1.3 %collective-permute-start.5 = (f32[17,16,128]{2,1,0:T(8,128)S(1)}, f32[17,16,128]{2,1,0:T(8,128)S(1)}, u32[]{:S(2)}, u32[]{:S(2)}) collective-permute-start(f32[17,16,128]{2,1,0:T(8,128)S(1)} %get-tuple-element.63), channel_id=1, source_target_pairs={{0,8},{4,12},{1,9},{5,13},{2,10},{6,14},{3,11},{7,15},{16,24},{20,... | collective-permute-start | bytes 417800 | tf_op jit(solution)/shard_map/ppermute | solution.py:577
  83.9 2.8 %collective-permute-start.4 = (f32[17,16,128]{2,1,0:T(8,128)S(1)}, f32[17,16,128]{2,1,0:T(8,128)S(1)}, u32[]{:S(2)}, u32[]{:S(2)}) collective-permute-start(f32[17,16,128]{2,1,0:T(8,128)S(1)} %get-tuple-element.63), channel_id=1, source_target_pairs={{0,4},{4,8},{8,12},{1,5},{5,9},{9,13},{2,6},{6,10},{10,14},{3,7},{... | collective-permute-start | bytes 417800 | tf_op jit(solution)/shard_map/ppermute | solution.py:577
  86.7 4.6 %local.1 = (f32[16,2048]{1,0:T(8,128)}, f32[2048,512]{1,0:T(8,128)S(1)}) custom-call(f32[2048,512]{1,0:T(8,128)S(1)} %copy-done, s32[2048,512]{1,0:T(8,128)S(1)} %copy-done.1, f32[16,16,128]{2,1,0:T(8,128)S(1)} %all_to_all.16.rows_ref, bf16[96,512]{1,0:T(8,128)(2,1)S(1)} %get-tuple-element.56.stack_ref, bf16[512,512]{1,0:T(8,128)(2,1)S(1)} %get-tuple-element.57.high_ref, ...), custom_call_target="tpu_custom_call" | custom-call | flops 3145728000 | bytes 14680064 | tf_op jit(solution)/shard_map/local/pallas_call | solution.py:563
  91.4 3.0 %finish.1 = f32[2048,512]{1,0:T(8,128)} custom-call(f32[2048,512]{1,0:T(8,128)S(1)} %get-tuple-element.60.local_ref, f32[16,16,128]{2,1,0:T(8,128)S(1)} %state.1.states_ref, bf16[96,512]{1,0:T(8,128)(2,1)S(1)} %get-tuple-element.65.entry_ref, f32[1,512]{1,0:T(1,128)S(1)} %bitcast.2), custom_call_target="tpu_custom_call" | custom-call | flops 209715200 | bytes 9437184 | tf_op jit(solution)/shard_map/finish/pallas_call | solution.py:590
  (39 shorter events, 1.2 us)
Async XLA Ops:
  8.4 28.0 %all-to-all-start = ((f32[16,152,128]{2,1,0:T(8,128)}), f32[16,152,128]{2,1,0:T(8,128)S(1)}, u32[]{:S(2)}, u32[]{:S(2)}) async-start(f32[16,152,128]{2,1,0:T(8,128)} %gram.1), calls=%async_computation | async-start | bytes 2490368 | tf_op jit(solution)/shard_map/all_to_all | solution.py:469
  24.5 12.0 %copy-start.11 = (f32[16]{0:T(128)S(1)}, f32[16]{0:T(128)}, u32[]{:S(2)}) copy-start(f32[16]{0:T(128)} %param.15) | copy-start | bytes 196
  28.4 1.3 %copy-start.3 = (bf16[32,128,256]{2,1,0:T(8,128)(2,1)}, bf16[32,128,256]{2,1,0:T(8,128)(2,1)S(1)}, u32[]{:S(2)}) copy-start(bf16[32,128,256]{2,1,0:T(8,128)(2,1)S(1)} %get-tuple-element.54.counts_ref) | copy-start | bytes 6291460
  29.7 26.7 %copy-start.5 = (f32[16,512]{1,0:T(8,128)S(1)}, f32[16,512]{1,0:T(8,128)}, u32[]{:S(2)}) copy-start(f32[16,512]{1,0:T(8,128)} %basis_ref.3) | copy-start | bytes 98308
  29.7 26.7 %copy-start.6 = (f32[16,512]{1,0:T(8,128)S(1)}, f32[16,512]{1,0:T(8,128)}, u32[]{:S(2)}) copy-start(f32[16,512]{1,0:T(8,128)} %decay_ref.1) | copy-start | bytes 98308
  29.7 26.7 %copy-start.7 = (f32[16,512]{1,0:T(8,128)S(1)}, f32[16,512]{1,0:T(8,128)}, u32[]{:S(2)}) copy-start(f32[16,512]{1,0:T(8,128)} %feed_ref.3) | copy-start | bytes 98308
  29.7 26.7 %copy-start.10 = (f32[16,512]{1,0:T(8,128)S(1)}, f32[16,512]{1,0:T(8,128)}, u32[]{:S(2)}) copy-start(f32[16,512]{1,0:T(8,128)} %load_ref.1) | copy-start | bytes 98308
  55.6 1.9 %collective-permute-start = (f32[64,16,128]{2,1,0:T(8,128)S(1)}, f32[64,16,128]{2,1,0:T(8,128)S(1)}, u32[]{:S(2)}, u32[]{:S(2)}) collective-permute-start(f32[64,16,128]{2,1,0:T(8,128)S(1)} %all_to_all.15.near_ref), channel_id=1, source_target_pairs={{0,16},{16,0},{1,17},{17,1},{2,18},{18,2},{3,19},{19,3},{4,20},{20... | collective-permute-start | bytes 1572872 | tf_op jit(solution)/shard_map/ppermute | solution.py:498
  55.6 1.9 %copy-start.4 = (bf16[32,128,256]{2,1,0:T(8,128)(2,1)S(1)}, bf16[32,128,256]{2,1,0:T(8,128)(2,1)}, u32[]{:S(2)}) copy-start(bf16[32,128,256]{2,1,0:T(8,128)(2,1)} %copy-done.3) | copy-start | bytes 6291460
  56.4 13.0 %copy-start.2 = (f32[16,272,128]{2,1,0:T(8,128)S(1)}, f32[16,272,128]{2,1,0:T(8,128)}, u32[]{:S(2)}) copy-start(f32[16,272,128]{2,1,0:T(8,128)} %get-tuple-element.61.crossed_ref) | copy-start | bytes 6684676
  56.4 13.0 %copy-start.8 = (f32[16,128]{1,0:T(8,128)S(1)}, f32[16,128]{1,0:T(8,128)}, u32[]{:S(2)}) copy-start(f32[16,128]{1,0:T(8,128)} %get-tuple-element.62.decayed_ref) | copy-start | bytes 24580
  56.4 30.2 %copy-start.1 = (s32[2048,512]{1,0:T(8,128)S(1)}, s32[2048,512]{1,0:T(8,128)}, u32[]{:S(2)}) copy-start(s32[2048,512]{1,0:T(8,128)} %valid_ref.3) | copy-start | bytes 12582916
  57.1 29.6 %copy-start = (f32[2048,512]{1,0:T(8,128)S(1)}, f32[2048,512]{1,0:T(8,128)}, u32[]{:S(2)}) copy-start(f32[2048,512]{1,0:T(8,128)} %flux_ref.3) | copy-start | bytes 12582916
  69.6 5.9 %collective-permute-start.3 = (f32[17,16,128]{2,1,0:T(8,128)S(1)}, f32[17,16,128]{2,1,0:T(8,128)S(1)}, u32[]{:S(2)}, u32[]{:S(2)}) collective-permute-start(f32[17,16,128]{2,1,0:T(8,128)S(1)} %local_carry.1.own_ref), channel_id=1, source_target_pairs={{0,3},{1,0},{2,1},{3,2},{4,7},{5,4},{6,5},{7,6},{8,11},{9,8},{10,9... | collective-permute-start | bytes 417800 | tf_op jit(solution)/shard_map/ppermute | solution.py:549
  70.9 7.1 %collective-permute-start.2 = (f32[17,16,128]{2,1,0:T(8,128)S(1)}, f32[17,16,128]{2,1,0:T(8,128)S(1)}, u32[]{:S(2)}, u32[]{:S(2)}) collective-permute-start(f32[17,16,128]{2,1,0:T(8,128)S(1)} %local_carry.1.own_ref), channel_id=1, source_target_pairs={{0,2},{1,3},{2,0},{3,1},{4,6},{5,7},{6,4},{7,5},{8,10},{9,11},{10,... | collective-permute-start | bytes 417800 | tf_op jit(solution)/shard_map/ppermute | solution.py:549
  72.2 7.3 %collective-permute-start.1 = (f32[17,16,128]{2,1,0:T(8,128)S(1)}, f32[17,16,128]{2,1,0:T(8,128)S(1)}, u32[]{:S(2)}, u32[]{:S(2)}) collective-permute-start(f32[17,16,128]{2,1,0:T(8,128)S(1)} %local_carry.1.own_ref), channel_id=1, source_target_pairs={{0,1},{1,2},{2,3},{3,0},{4,5},{5,6},{6,7},{7,4},{8,9},{9,10},{10,1... | collective-permute-start | bytes 417800 | tf_op jit(solution)/shard_map/ppermute | solution.py:549
  79.6 11.7 %copy-start.9 = (f32[512]{0:T(512)S(1)}, f32[512]{0:T(512)}, u32[]{:S(2)}) copy-start(f32[512]{0:T(512)} %param.19) | copy-start | bytes 6148
  79.6 11.6 %collective-permute-start.6 = (f32[17,16,128]{2,1,0:T(8,128)S(1)}, f32[17,16,128]{2,1,0:T(8,128)S(1)}, u32[]{:S(2)}, u32[]{:S(2)}) collective-permute-start(f32[17,16,128]{2,1,0:T(8,128)S(1)} %get-tuple-element.63), channel_id=1, source_target_pairs={{0,12},{1,13},{2,14},{3,15},{16,28},{17,29},{18,30},{19,31},{32,44... | collective-permute-start | bytes 417800 | tf_op jit(solution)/shard_map/ppermute | solution.py:577
  82.6 8.7 %collective-permute-start.5 = (f32[17,16,128]{2,1,0:T(8,128)S(1)}, f32[17,16,128]{2,1,0:T(8,128)S(1)}, u32[]{:S(2)}, u32[]{:S(2)}) collective-permute-start(f32[17,16,128]{2,1,0:T(8,128)S(1)} %get-tuple-element.63), channel_id=1, source_target_pairs={{0,8},{4,12},{1,9},{5,13},{2,10},{6,14},{3,11},{7,15},{16,24},{20,... | collective-permute-start | bytes 417800 | tf_op jit(solution)/shard_map/ppermute | solution.py:577
  83.9 7.4 %collective-permute-start.4 = (f32[17,16,128]{2,1,0:T(8,128)S(1)}, f32[17,16,128]{2,1,0:T(8,128)S(1)}, u32[]{:S(2)}, u32[]{:S(2)}) collective-permute-start(f32[17,16,128]{2,1,0:T(8,128)S(1)} %get-tuple-element.63), channel_id=1, source_target_pairs={{0,4},{4,8},{8,12},{1,5},{5,9},{9,13},{2,6},{6,10},{10,14},{3,7},{... | collective-permute-start | bytes 417800 | tf_op jit(solution)/shard_map/ppermute | solution.py:577
